TPU v7x, 32 devices: a whole 2x2x4 slice. The times are simulated.
32 devices in a mesh: batch: 2 (over core), seq: 16 (over z, y, x).
Axes of the slice: x: 2, y: 2, z: 4, core: 2. Of those that a mesh axis runs over, the one named last changes fastest.
Arguments:
- inputs: bfloat16 [4, 8192, 1024], P('batch', 'seq'), may hold values from -6 to 6
- doc_ids: int32 [4, 8192], P('batch', 'seq'), may hold values from 0 to 1, as said below
- w_query: bfloat16 [1024, 1024], replicated, may hold values from -0.1875 to 0.1875
- w_key: bfloat16 [1024, 1024], replicated, may hold values from -0.1875 to 0.1875
- w_value: bfloat16 [1024, 1024], replicated, may hold values from -0.1875 to 0.1875
- w_outgate: bfloat16 [1024, 1024], replicated, may hold values from -0.1875 to 0.1875
- w_output: bfloat16 [1024, 1024], replicated, may hold values from -0.375 to 0.375
- w_gate: bfloat16 [1024, 2816], replicated, may hold values from -0.1875 to 0.1875
- w_up: bfloat16 [1024, 2816], replicated, may hold values from -0.1875 to 0.1875
- w_down: bfloat16 [2816, 1024], replicated, may hold values from -0.109375 to 0.109375
- head_gain: float32 [1024], replicated, may hold values from 0.1 to 1.9
- cotangent: bfloat16 [4, 8192, 1024], P('batch', 'seq'), may hold values from -6 to 6
Outputs:
- block_out: bfloat16 [4, 8192, 1024], P('batch', 'seq')
- input_grad: bfloat16 [4, 8192, 1024], P('batch', 'seq')
- grad_query: float32 [1024, 1024], P(('batch', 'seq'))
- grad_key: float32 [1024, 1024], P(('batch', 'seq'))
- grad_value: float32 [1024, 1024], P(('batch', 'seq'))
- grad_outgate: float32 [1024, 1024], P(('batch', 'seq'))
- grad_output: float32 [1024, 1024], P(('batch', 'seq'))
- grad_gate: float32 [1024, 2816], P(('batch', 'seq'))
- grad_up: float32 [1024, 2816], P(('batch', 'seq'))
- grad_down: float32 [2816, 1024], P(('batch', 'seq'))
- grad_gain: float32 [1024], P(('batch', 'seq'))
Inputs may be any that keep to these rules, and one draw needn't show every extreme that they name: `doc_ids`: within each row the ids start at 0, never fall, and rise by one at the first token of each new document.
All inputs are finite; a program needn't handle non-finite values.
Results may differ from a plain program's by a relative error of at most 0.014.
Values sent between devices are 32-bit elements; how exact they have to be, the bound alone decides.
No kernel may reach another device: no remote copies, remote signals or barrier semaphores. Data moves between devices by JAX's collectives and lax.ppermute only.
A program may use at most 320 MiB of HBM per device.

v0:
```python
import jax
import jax.numpy as jnp
from jax import lax
from jax.sharding import PartitionSpec as P

HEADS = 16
HEAD_DIM = 64


epsilon = 1e-06


def prefix(part, axis, combine, identity, reverse):
    count = lax.axis_size(axis)
    place = lax.axis_index(axis)
    ahead = count - 1 - place if reverse else place
    gathered = jax.tree.map(lambda a: lax.all_gather(a, axis), part)
    state = jax.tree.map(lambda a, e: jnp.zeros_like(a) + jnp.asarray(e, a.dtype), part, identity)

    def one(turn, state):
        source = count - 1 - turn if reverse else turn
        return combine(
            state, jax.tree.map(lambda a: lax.dynamic_index_in_dim(a, source, 0, False), gathered)
        )

    return lax.fori_loop(0, ahead, one, state)


def project(activations, weight):
    return jnp.dot(activations, weight, preferred_element_type=jnp.float32)


def outer_sum(activations, grads_in):
    return lax.dot_general(
        activations, grads_in, (((0,), (0,)), ((), ())), preferred_element_type=jnp.float32
    )


def project_back(grads_in, weight):
    return lax.dot_general(
        grads_in, weight, (((1,), (1,)), ((), ())), preferred_element_type=jnp.float32
    )


def rms_scale(values):
    return lax.rsqrt(jnp.mean(values * values, axis=-1, keepdims=True) + epsilon)


def norm_back(unit_vals, scale_vals, grad_vals):
    return scale_vals * (
        grad_vals - unit_vals * jnp.mean(grad_vals * unit_vals, axis=-1, keepdims=True)
    )


def softplus_grad(values):
    return jax.nn.sigmoid(values)


def chain_states(earlier_pair, later_pair):
    early_sum, early_id = earlier_pair
    late_sum, late_id = later_pair
    joined = (late_id == early_id) | (late_id < 0)
    summed = late_sum + jnp.where(joined[:, None, None, None], early_sum, 0.0)
    return (summed, jnp.where(late_id < 0, early_id, late_id))


def local(
    inputs,
    doc_ids,
    w_query,
    w_key,
    w_value,
    w_outgate,
    w_output,
    w_gate,
    w_up,
    w_down,
    head_gain,
    cotangent,
):
    row_count, block_len, feat_width = inputs.shape
    token_count = row_count * block_len
    heads_shape = (row_count, block_len, HEADS, HEAD_DIM)
    in_flat = inputs.reshape(token_count, feat_width).astype(jnp.float32)
    scale_in = rms_scale(in_flat)
    unit_in = in_flat * scale_in
    normed_in = unit_in.astype(jnp.bfloat16)
    pre_query = project(normed_in, w_query)
    pre_key = project(normed_in, w_key)
    pre_value = project(normed_in, w_value)
    pre_outgate = project(normed_in, w_outgate)
    queries = jax.nn.softplus(pre_query).astype(jnp.bfloat16).reshape(heads_shape)
    key_heads = jax.nn.softplus(pre_key).astype(jnp.bfloat16).reshape(heads_shape)
    val_heads = pre_value.astype(jnp.bfloat16).reshape(heads_shape)
    out_gate = jax.nn.sigmoid(pre_outgate)
    ids_float = doc_ids.astype(jnp.float32)
    places = jnp.arange(block_len, dtype=jnp.int32)
    allowed = (places[:, None] >= places[None, :])[None] & (
        doc_ids[:, :, None] == doc_ids[:, None, :]
    )

    def block_scores():
        raw_scores = jnp.einsum(
            "rthd,rshd->rhts", queries, key_heads, preferred_element_type=jnp.float32
        )
        return jnp.where(allowed[:, None], raw_scores, 0.0).astype(jnp.bfloat16)

    last_ids = ids_float[:, -1]
    first_ids = ids_float[:, 0]
    in_last = (ids_float == last_ids[:, None]).astype(jnp.bfloat16)
    local_state = jnp.einsum(
        "rthd,rthe->rhde",
        key_heads * in_last[:, :, None, None],
        val_heads,
        preferred_element_type=jnp.float32,
    )
    empty_pair = (jnp.zeros_like(local_state), -jnp.ones_like(last_ids))
    carried, carried_id = prefix((local_state, last_ids), "seq", chain_states, empty_pair, False)
    matched = (ids_float == carried_id[:, None])[:, :, None, None]
    carried_low = carried.astype(jnp.bfloat16)
    attn_probs = block_scores()
    attended = jnp.einsum(
        "rhts,rshd->rthd", attn_probs, val_heads, preferred_element_type=jnp.float32
    )
    attended = attended + jnp.where(
        matched,
        jnp.einsum("rthd,rhde->rthe", queries, carried_low, preferred_element_type=jnp.float32),
        0.0,
    )
    head_scale = rms_scale(attended)
    unit_heads = (attended * head_scale).reshape(token_count, feat_width)
    normed_heads = unit_heads * head_gain
    gated_out = (normed_heads * out_gate).astype(jnp.bfloat16)
    hidden_sum = in_flat + project(gated_out, w_output)
    scale_mid = rms_scale(hidden_sum)
    unit_mid = hidden_sum * scale_mid
    normed_mid = unit_mid.astype(jnp.bfloat16)
    gate_pre = project(normed_mid, w_gate)
    up_pre = project(normed_mid, w_up)
    product = (gate_pre * up_pre).astype(jnp.bfloat16)
    out_flat = hidden_sum + project(product, w_down)
    block_out = out_flat.astype(jnp.bfloat16).reshape(inputs.shape)
    cot_flat = cotangent.reshape(token_count, feat_width)
    cot_float = cot_flat.astype(jnp.float32)
    grad_down = outer_sum(product, cot_flat)
    back_product = project_back(cot_flat, w_down)
    back_gate = (back_product * up_pre).astype(jnp.bfloat16)
    back_up = (back_product * gate_pre).astype(jnp.bfloat16)
    grad_gate = outer_sum(normed_mid, back_gate)
    grad_up = outer_sum(normed_mid, back_up)
    back_mid = project_back(back_gate, w_gate) + project_back(back_up, w_up)
    back_hidden = cot_float + norm_back(unit_mid, scale_mid, back_mid)
    back_branch = back_hidden.astype(jnp.bfloat16)
    grad_output = outer_sum(gated_out, back_branch)
    back_gated = project_back(back_branch, w_output)
    back_outgate = (back_gated * normed_heads * out_gate * (1.0 - out_gate)).astype(jnp.bfloat16)
    back_normed = back_gated * out_gate
    grad_gain = jnp.sum(unit_heads * back_normed, axis=0)
    back_unit = (back_normed * head_gain).reshape(heads_shape)
    back_attended = norm_back(unit_heads.reshape(heads_shape), head_scale, back_unit).astype(
        jnp.bfloat16
    )
    in_first = (ids_float == first_ids[:, None]).astype(jnp.bfloat16)
    local_grad = jnp.einsum(
        "rthd,rthe->rhde",
        queries * in_first[:, :, None, None],
        back_attended,
        preferred_element_type=jnp.float32,
    )
    grad_in, grad_id = prefix((local_grad, first_ids), "seq", chain_states, empty_pair, True)
    attn_probs = block_scores()
    back_scores = jnp.where(
        allowed[:, None],
        jnp.einsum("rthd,rshd->rhts", back_attended, val_heads, preferred_element_type=jnp.float32),
        0.0,
    ).astype(jnp.bfloat16)
    grad_low = grad_in.astype(jnp.bfloat16)
    uses_grad = (ids_float == grad_id[:, None])[:, :, None, None]
    back_queries = jnp.einsum(
        "rhts,rshd->rthd", back_scores, key_heads, preferred_element_type=jnp.float32
    )
    back_queries = back_queries + jnp.where(
        matched,
        jnp.einsum(
            "rthe,rhde->rthd", back_attended, carried_low, preferred_element_type=jnp.float32
        ),
        0.0,
    )
    back_keys = jnp.einsum(
        "rhts,rthd->rshd", back_scores, queries, preferred_element_type=jnp.float32
    )
    back_keys = back_keys + jnp.where(
        uses_grad,
        jnp.einsum("rthe,rhde->rthd", val_heads, grad_low, preferred_element_type=jnp.float32),
        0.0,
    )
    back_values = jnp.einsum(
        "rhts,rthd->rshd", attn_probs, back_attended, preferred_element_type=jnp.float32
    )
    back_values = back_values + jnp.where(
        uses_grad,
        jnp.einsum("rthd,rhde->rthe", key_heads, grad_low, preferred_element_type=jnp.float32),
        0.0,
    )
    back_query = (back_queries.reshape(token_count, feat_width) * softplus_grad(pre_query)).astype(
        jnp.bfloat16
    )
    back_key = (back_keys.reshape(token_count, feat_width) * softplus_grad(pre_key)).astype(
        jnp.bfloat16
    )
    back_value = back_values.reshape(token_count, feat_width).astype(jnp.bfloat16)
    grad_query = outer_sum(normed_in, back_query)
    grad_key = outer_sum(normed_in, back_key)
    grad_value = outer_sum(normed_in, back_value)
    grad_outgate = outer_sum(normed_in, back_outgate)
    back_in = project_back(back_query, w_query) + project_back(back_key, w_key)
    back_in = back_in + project_back(back_value, w_value) + project_back(back_outgate, w_outgate)
    input_grad = (
        (back_hidden + norm_back(unit_in, scale_in, back_in))
        .astype(jnp.bfloat16)
        .reshape(inputs.shape)
    )
    all_shards = tuple(
        (
            lax.psum_scatter(grad_query, ("batch", "seq"), scatter_dimension=0, tiled=True),
            lax.psum_scatter(grad_key, ("batch", "seq"), scatter_dimension=0, tiled=True),
            lax.psum_scatter(grad_value, ("batch", "seq"), scatter_dimension=0, tiled=True),
            lax.psum_scatter(grad_outgate, ("batch", "seq"), scatter_dimension=0, tiled=True),
            lax.psum_scatter(grad_output, ("batch", "seq"), scatter_dimension=0, tiled=True),
            lax.psum_scatter(grad_gate, ("batch", "seq"), scatter_dimension=0, tiled=True),
            lax.psum_scatter(grad_up, ("batch", "seq"), scatter_dimension=0, tiled=True),
            lax.psum_scatter(grad_down, ("batch", "seq"), scatter_dimension=0, tiled=True),
            lax.psum_scatter(grad_gain, ("batch", "seq"), scatter_dimension=0, tiled=True),
        )
    )
    return (block_out, input_grad) + all_shards


def solution(mesh):
    return jax.shard_map(
        local,
        mesh=mesh,
        in_specs=(
            P("batch", "seq", None),
            P("batch", "seq"),
            P(),
            P(),
            P(),
            P(),
            P(),
            P(),
            P(),
            P(),
            P(),
            P("batch", "seq", None),
        ),
        out_specs=(
            P("batch", "seq", None),
            P("batch", "seq", None),
            P(("batch", "seq"), None),
            P(("batch", "seq"), None),
            P(("batch", "seq"), None),
            P(("batch", "seq"), None),
            P(("batch", "seq"), None),
            P(("batch", "seq"), None),
            P(("batch", "seq"), None),
            P(("batch", "seq"), None),
            P(("batch", "seq")),
        ),
        check_vma=False,
    )
```

profile of v0, /device:TPU:0, one launch (start us, length us, event | category | flops | bytes accessed | tf_op | source)
XLA Modules:
  0.0 2092.5 jit_solution(16201225515913736956)
XLA Ops:
  17.7 6.4 reshape.163
  24.1 5.4 copy.75
  29.5 8.8 fusion.1
  51.0 8.7 fusion
  70.0 45.2 %all-reduce.3 = (f32[32]{0:T(128)S(1)}, f32[32]{0:T(128)}) all-reduce(f32[32]{0:T(128)S(1)} %dynamic-update-slice, f32[32]{0:T(128)S(1)} %dynamic-update-slice.1), channel_id=3, replica_groups=mesh['batch'=2,'seq'=16] {'seq'}, use_global_device_ids=true, to_apply=%add | all-reduce | flops 64 | bytes 512
  119.4 8.2 select_convert_fusion.1
  127.7 13.8 fusion.35
  141.4 104.4 %all-gather.7.cloned.1.call-done = f32[32,16,64,64]{3,2,1,0:T(8,128)} async-done(((f32[2,16,64,64]{3,2,1,0:T(8,128)}), f32[32,16,64,64]{3,2,1,0:T(8,128)}) %all-gather.7.cloned.1.call-update) | async-done | bytes 8388624 | tf_op jit(solution)/shard_map/all_gather | solution.py:17
  255.3 8.1 copy.104
  263.4 7.6 reshape.164
  271.0 8.4 multiply_convert_fusion.7
  284.4 8.8 fusion.36
  293.2 8.8 fusion.37
  302.0 18.2 multiply_convert_fusion
  320.3 10.0 fusion.38
  330.4 9.9 multiply_reduce_fusion.2
  346.1 5.8 multiply_reduce_fusion
  351.9 7.3 reshape.165
  359.2 6.8 copy.84
  366.0 4.9 multiply_reduce_fusion.1
  375.3 10.1 select_convert_fusion
  385.4 13.5 fusion.19
  399.0 4.9 add_bitcast_fusion.1
  403.8 8.2 copy.100
  412.0 7.6 reshape.161
  419.6 4.8 multiply_convert_fusion.5
  431.7 5.9 fusion.46
  439.8 6.6 fusion.26
  448.0 11.6 fusion.47
  459.7 11.7 fusion.48
  473.1 11.6 fusion.49
  486.3 10.5 fusion.22
  496.7 92.7 %all-gather.9.cloned.1.call-done = f32[32,16,64,64]{3,2,1,0:T(8,128)} async-done(((f32[2,16,64,64]{3,2,1,0:T(8,128)}), f32[32,16,64,64]{3,2,1,0:T(8,128)}) %all-gather.9.cloned.1.call-update) | async-done | bytes 8388624 | tf_op jit(solution)/shard_map/all_gather | solution.py:17
  589.5 24.4 %while.27 = (s32[]{:T(128)}, f32[2,16,64,64]{3,2,1,0:T(8,128)S(1)}, f32[2]{0:T(128)S(1)}, s32[]{:T(128)}, f32[16,2,16,64,64]{4,3,2,1,0:T(8,128)}, /*index=5*/f32...) while((s32[]{:T(128)}, f32[2,16,64,64]{3,2,1,0:T(8,128)S(1)}, f32[2]{0:T(128)S(1)}, ...), condition=%wide.region_8.9_spmd, body=%wide.region_7.8_spmd.sunk | while | flops 262160 | bytes 1573075 | solution.py:26
  614.0 5.5 add_bitcast_fusion
  619.5 8.2 copy.101
  627.7 7.7 reshape.162
  648.6 9.6 fusion.41
  668.1 38.5 %all-reduce.2 = f32[1024]{0:T(1024)S(1)} all-reduce(f32[1024]{0:T(1024)S(1)} %copy-done.44), channel_id=14, replica_groups=mesh['batch'=2,'seq'=16] {'batch','seq'}, use_global_device_ids=true, to_apply=%region_19.20.clone | all-reduce | flops 1024 | bytes 8192
  711.3 11.0 add_convert_fusion.1
  732.5 5.4 reduce-scatter.9.cloned.1.call-done
  737.9 145.1 %reduce-scatter.15.cloned.1.call-done = f32[32,1024]{1,0:T(8,128)} async-done(((f32[1024,1024]{1,0:T(8,128)}), f32[32,1024]{1,0:T(8,128)}) %reduce-scatter.15.cloned.1.call-update) | async-done | bytes 131088 | tf_op jit(solution)/shard_map/reduce_scatter | solution.py:228
  882.9 148.8 %reduce-scatter.17.cloned.1.call-done = f32[32,1024]{1,0:T(8,128)} async-done(((f32[1024,1024]{1,0:T(8,128)}), f32[32,1024]{1,0:T(8,128)}) %reduce-scatter.17.cloned.1.call-update) | async-done | bytes 131088 | tf_op jit(solution)/shard_map/reduce_scatter | solution.py:229
  1031.7 248.9 %reduce-scatter.19.cloned.1.call-done = f32[32,2816]{1,0:T(8,128)} async-done(((f32[1024,2816]{1,0:T(8,128)}), f32[32,2816]{1,0:T(8,128)}) %reduce-scatter.19.cloned.1.call-update) | async-done | bytes 360464 | tf_op jit(solution)/shard_map/reduce_scatter | solution.py:230
  1280.6 253.5 %reduce-scatter.21.cloned.1.call-done = f32[32,2816]{1,0:T(8,128)} async-done(((f32[1024,2816]{1,0:T(8,128)}), f32[32,2816]{1,0:T(8,128)}) %reduce-scatter.21.cloned.1.call-update) | async-done | bytes 360464 | tf_op jit(solution)/shard_map/reduce_scatter | solution.py:231
  1534.1 253.5 %reduce-scatter.23.cloned.1.call-done = f32[88,1024]{1,0:T(8,128)} async-done(((f32[2816,1024]{1,0:T(8,128)}), f32[88,1024]{1,0:T(8,128)}) %reduce-scatter.23.cloned.1.call-update) | async-done | bytes 360464 | tf_op jit(solution)/shard_map/reduce_scatter | solution.py:232
  1787.6 150.9 %reduce-scatter.11.cloned.1.call-done = f32[32,1024]{1,0:T(8,128)} async-done(((f32[1024,1024]{1,0:T(8,128)}), f32[32,1024]{1,0:T(8,128)}) %reduce-scatter.11.cloned.1.call-update) | async-done | bytes 131088 | tf_op jit(solution)/shard_map/reduce_scatter | solution.py:226
  1938.5 146.7 %reduce-scatter.13.cloned.1.call-done = f32[32,1024]{1,0:T(8,128)} async-done(((f32[1024,1024]{1,0:T(8,128)}), f32[32,1024]{1,0:T(8,128)}) %reduce-scatter.13.cloned.1.call-update) | async-done | bytes 131088 | tf_op jit(solution)/shard_map/reduce_scatter | solution.py:227
  (240 shorter events, 137.7 us)
Async XLA Ops:
  7.2 272.2 %copy-start = (bf16[1024,1024]{1,0:T(8,128)(2,1)S(1)}, bf16[1024,1024]{1,0:T(8,128)(2,1)}, u32[]{:S(2)}) copy-start(bf16[1024,1024]{1,0:T(8,128)(2,1)} %param.22) | copy-start | bytes 6291460
  7.2 238.6 %all-gather.7.cloned.1.call-start = ((), (), s32[]{:S(2)}) async-start(), calls=%async_computation.16 | async-start | bytes 17825792 | tf_op jit(solution)/shard_map/all_gather | solution.py:17
  7.2 6.8 copy-start.47
  38.3 8.5 copy-start.39
  50.7 538.7 %all-gather.9.cloned.1.call-start = ((), (), s32[]{:S(2)}) async-start(), calls=%async_computation.17 | async-start | bytes 17825792 | tf_op jit(solution)/shard_map/all_gather | solution.py:17
  59.7 8.6 copy-start.50
  115.3 4.1 copy-start.6
  115.3 4.1 copy-start.12
  115.8 3.6 copy-start.38
  263.4 7.6 copy-start.45
  271.0 8.4 copy-start.4
  279.4 2.5 copy-start.51
  279.4 4.9 slice-start
  279.4 4.9 slice-start.1
  284.0 9.2 slice-start.2
  284.4 8.9 copy-start.35
  284.4 8.9 slice-start.3
  320.3 10.0 copy-start.17
  320.3 10.0 copy-start.21
  330.3 9.9 copy-start.19
  340.3 3.4 copy-start.15
  340.3 5.8 copy-start.25
  343.5 8.3 copy-start.9
  366.0 4.9 copy-start.3
  366.0 5.9 copy-start.11
  373.4 25.6 %copy-start.8 = (bf16[2,512,16,64]{1,3,2,0:T(8,128)(2,1)}, bf16[2,512,16,64]{1,3,2,0:T(8,128)(2,1)S(1)}, u32[]{:S(2)}) copy-start(bf16[2,512,16,64]{1,3,2,0:T(8,128)(2,1)S(1)} %multiply_convert_fusion.6) | copy-start | bytes 6291460
  375.2 362.6 %reduce-scatter.9.cloned.1.call-start = ((), (), s32[]{:S(2)}) async-start(), calls=%async_computation.8 | async-start | bytes 4325376 | tf_op jit(solution)/shard_map/reduce_scatter | solution.py:225
  419.6 6.1 copy-start.31
  430.1 452.8 %reduce-scatter.15.cloned.1.call-start = ((), (), s32[]{:S(2)}) async-start(), calls=%async_computation.11 | async-start | bytes 4325376 | tf_op jit(solution)/shard_map/reduce_scatter | solution.py:228
  437.7 594.1 %reduce-scatter.17.cloned.1.call-start = ((), (), s32[]{:S(2)}) async-start(), calls=%async_computation.12 | async-start | bytes 4325376 | tf_op jit(solution)/shard_map/reduce_scatter | solution.py:229
  446.5 834.2 %reduce-scatter.19.cloned.1.call-start = ((), (), s32[]{:S(2)}) async-start(), calls=%async_computation.13 | async-start | bytes 11894784 | tf_op jit(solution)/shard_map/reduce_scatter | solution.py:230
  459.6 1074.5 %reduce-scatter.21.cloned.1.call-start = ((), (), s32[]{:S(2)}) async-start(), calls=%async_computation.14 | async-start | bytes 11894784 | tf_op jit(solution)/shard_map/reduce_scatter | solution.py:231
  471.4 1316.2 %reduce-scatter.23.cloned.1.call-start = ((), (), s32[]{:S(2)}) async-start(), calls=%async_computation.15 | async-start | bytes 11894784 | tf_op jit(solution)/shard_map/reduce_scatter | solution.py:232
  484.7 1453.8 %reduce-scatter.11.cloned.1.call-start = ((), (), s32[]{:S(2)}) async-start(), calls=%async_computation.9 | async-start | bytes 4325376 | tf_op jit(solution)/shard_map/reduce_scatter | solution.py:226
  589.5 24.4 %copy-start.40 = (s32[2,512]{1,0:T(2,128)S(1)}, s32[2,512]{1,0:T(2,128)}, u32[]{:S(2)}) copy-start(s32[2,512]{1,0:T(2,128)} %param.17) | copy-start | bytes 12292
  635.4 6.1 copy-start.32
  645.9 1439.3 %reduce-scatter.13.cloned.1.call-start = ((), (), s32[]{:S(2)}) async-start(), calls=%async_computation.10 | async-start | bytes 4325376 | tf_op jit(solution)/shard_map/reduce_scatter | solution.py:227
  648.6 9.6 copy-start.13
  667.4 39.7 %copy-start.27 = (bf16[1024,1024]{1,0:T(8,128)(2,1)S(1)}, bf16[1024,1024]{1,0:T(8,128)(2,1)}, u32[]{:S(2)}) copy-start(bf16[1024,1024]{1,0:T(8,128)(2,1)} %copy-done.26) | copy-start | bytes 6291460
  707.1 4.1 copy-start.18
  711.3 11.0 copy-start.34
  711.3 11.0 copy-start.48
  722.3 2.4 copy-start.49
  724.7 2.4 copy-start.5
  724.7 2.8 copy-start.37
  724.7 2.8 copy-start.42
  727.6 2.7 copy-start.10
  730.3 1354.9 %copy-start.1 = (bf16[1024,1024]{1,0:T(8,128)(2,1)S(1)}, bf16[1024,1024]{1,0:T(8,128)(2,1)}, u32[]{:S(2)}) copy-start(bf16[1024,1024]{1,0:T(8,128)(2,1)} %param.22) | copy-start | bytes 6291460
  (19 other events, 29.3 us)
Sparse Core Ops, SparseCore 0:
  50.8 194.9 all-gather.6
  375.3 214.0 all-gather.8
  592.2 145.5 reduce-scatter.8
  740.6 142.3 reduce-scatter.14
  885.6 146.0 reduce-scatter.16
  1034.5 246.1 reduce-scatter.18
  1283.5 250.5 reduce-scatter.20
  1537.0 250.5 reduce-scatter.22
  1790.4 147.9 reduce-scatter.10
  1941.2 143.9 reduce-scatter.12
where the time goes:
time: 2100 us; the launch traced here: 2090 us
  waiting for transfers between devices  1550 us (74%)
  matrix products  261 us (12%)
  local copies, waits for them, and re-layouts  118 us (6%)
  blocking collectives  83.6 us (4%)
  other arithmetic  61.2 us (3%)
    reduce_scatter x1, waiting for transfers between devices, local(): lax.psum_scatter(grad_up, ('batch', 'seq'), scatter_dimension=0, tiled=True)  253 us
    reduce_scatter x1, waiting for transfers between devices, local(): lax.psum_scatter(grad_down, ('batch', 'seq'), scatter_dimension=0, tiled=...  253 us
    reduce_scatter x1, waiting for transfers between devices, local(): lax.psum_scatter(grad_gate, ('batch', 'seq'), scatter_dimension=0, tiled=...  249 us
    all_gather x2, waiting for transfers between devices, prefix(): gathered = jax.tree.map(lambda a: lax.all_gather(a, axis), part)  197 us
    reduce_scatter x1, waiting for transfers between devices, local(): lax.psum_scatter(grad_key, ('batch', 'seq'), scatter_dimension=0, tiled=T...  151 us
    reduce_scatter x1, waiting for transfers between devices, local(): lax.psum_scatter(grad_output, ('batch', 'seq'), scatter_dimension=0, tile...  149 us
    reduce_scatter x1, waiting for transfers between devices, local(): lax.psum_scatter(grad_value, ('batch', 'seq'), scatter_dimension=0, tiled...  147 us
    reduce_scatter x1, waiting for transfers between devices, local(): lax.psum_scatter(grad_outgate, ('batch', 'seq'), scatter_dimension=0, til...  145 us
  transfers between devices with their start and end apart: 10, of which 10 were waited for; matrix products, arithmetic and copies ran while one was open for 12% of the time, Pallas kernels for 0%

commit v1 on v0

--- a/solution.py
+++ b/solution.py
@@ -10,20 +10,150 @@
 epsilon = 1e-06
 
 
-def prefix(part, axis, combine, identity, reverse):
-    count = lax.axis_size(axis)
-    place = lax.axis_index(axis)
-    ahead = count - 1 - place if reverse else place
-    gathered = jax.tree.map(lambda a: lax.all_gather(a, axis), part)
-    state = jax.tree.map(lambda a, e: jnp.zeros_like(a) + jnp.asarray(e, a.dtype), part, identity)
-
-    def one(turn, state):
-        source = count - 1 - turn if reverse else turn
-        return combine(
-            state, jax.tree.map(lambda a: lax.dynamic_index_in_dim(a, source, 0, False), gathered)
-        )
-
-    return lax.fori_loop(0, ahead, one, state)
+def chip_grid(count):
+    bits = count.bit_length() - 1
+    z_bits = min(bits, 2)
+    y_bits = (bits - z_bits + 1) // 2
+    return z_bits, y_bits, bits - z_bits - y_bits
+
+
+def seq_bit(position, bits, place):
+    return (position >> (bits - 1 - place)) & 1
+
+
+def piece(array, axes, picks):
+    starts = [picks.get(a, 0) for a in axes] + [0] * (array.ndim - len(axes))
+    sizes = [1 if a in picks else 2 for a in axes] + list(array.shape[len(axes):])
+    taken = lax.dynamic_slice(array, starts, sizes)
+    left = tuple(a for a in axes if a not in picks)
+    return taken.reshape((2,) * len(left) + array.shape[len(axes):])
+
+
+def scatter_sum(grad, order):
+    count = lax.axis_size("seq")
+    bits = count.bit_length() - 1
+    axes = ("batch",) + tuple(range(bits))
+    rows = grad.shape[0] // (2 * count)
+    position = lax.axis_index("seq")
+    mine = {"batch": lax.axis_index("batch")}
+    for place in range(bits):
+        mine[place] = seq_bit(position, bits, place)
+    parts = [(grad.reshape((2,) * len(axes) + (rows,) + grad.shape[1:]), axes)]
+    done = {}
+    for axis in order:
+        away = dict(done)
+        away[axis] = 1 - mine[axis]
+        outgoing = sum_pieces(parts, away)
+        if axis == "batch":
+            incoming = lax.ppermute(outgoing, "batch", [(0, 1), (1, 0)])
+        else:
+            flip = 1 << (bits - 1 - axis)
+            incoming = lax.ppermute(outgoing, "seq", [(i, i ^ flip) for i in range(count)])
+        done[axis] = mine[axis]
+        parts.append((incoming, tuple(a for a in axes if a not in done)))
+    return sum_pieces(parts, done)
+
+
+def sum_pieces(parts, picks):
+    total = None
+    for array, axes in parts:
+        one = piece(array, axes, {a: v for a, v in picks.items() if a in axes})
+        total = one if total is None else total + one
+    return total
+
+
+def orders(count):
+    z_bits, y_bits, x_bits = chip_grid(count)
+    z_axes = list(range(z_bits))[::-1]
+    y_axes = list(range(z_bits, z_bits + y_bits))[::-1]
+    x_axes = list(range(z_bits + y_bits, z_bits + y_bits + x_bits))[::-1]
+    return (
+        ["batch"] + x_axes + y_axes + z_axes,
+        ["batch"] + y_axes + x_axes + z_axes,
+        ["batch"] + z_axes + x_axes + y_axes,
+    )
+
+
+def gather_ids(ids):
+    count = lax.axis_size("seq")
+    bits = count.bit_length() - 1
+    position = lax.axis_index("seq")
+    held = ids[None]
+    for step in range(bits):
+        flip = 1 << step
+        other = lax.ppermute(held, "seq", [(i, i ^ flip) for i in range(count)])
+        low = (position & flip) == 0
+        held = jnp.concatenate([jnp.where(low, held, other), jnp.where(low, other, held)], axis=0)
+    return held
+
+
+def prefix(state, ids, reverse):
+    count = lax.axis_size("seq")
+    position = lax.axis_index("seq")
+    z_bits, y_bits, x_bits = chip_grid(count)
+    planes = 1 << z_bits
+    plane = 1 << (y_bits + x_bits)
+    row_count, heads = state.shape[:2]
+    share = heads // plane
+    z_at, at = position // plane, position % plane
+    shape = (row_count, plane, share) + state.shape[2:]
+    cut = state.reshape(shape)
+
+    def pairs(k):
+        return [(i, (i // plane) * plane + ((i % plane) ^ k)) for i in range(count)]
+
+    def take(array, index):
+        return lax.dynamic_index_in_dim(array, index, 1, False)
+
+    swapped = [take(cut, at)]
+    for k in range(1, plane):
+        swapped.append(lax.ppermute(take(cut, at ^ k), "seq", pairs(k)))
+    ids_plane = lax.dynamic_slice_in_dim(ids, z_at * plane, plane, 0)
+    end = 0 if reverse else plane - 1
+
+    def masked(flag, array):
+        return jnp.where(flag[:, None, None, None], array, 0.0)
+
+    def id_of(index):
+        return lax.dynamic_index_in_dim(ids, jnp.clip(index, 0, count - 1), 0, False)
+
+    total = None
+    for k in range(plane):
+        one = masked(lax.dynamic_index_in_dim(ids_plane, at ^ k, 0, False) == ids_plane[end], swapped[k])
+        total = one if total is None else total + one
+    passed = []
+    for step in range(1, planes):
+        shift = -step * plane if reverse else step * plane
+        moves = [(i, i + shift) for i in range(count) if 0 <= i + shift < count]
+        source = z_at + step if reverse else z_at - step
+        passed.append((lax.ppermute(total, "seq", moves), source))
+    results = []
+    for k in range(plane):
+        target_at = at ^ k
+        target = z_at * plane + target_at
+        near = target + 1 if reverse else target - 1
+        near_id = id_of(near)
+        summed = jnp.zeros_like(total)
+        for j in range(plane):
+            source_at = at ^ j
+            before = source_at > target_at if reverse else source_at < target_at
+            same = lax.dynamic_index_in_dim(ids_plane, source_at, 0, False) == near_id
+            summed = summed + masked(before & same, swapped[j])
+        for array, source in passed:
+            there = (source < planes) if reverse else (source >= 0)
+            same = id_of(source * plane + end) == near_id
+            summed = summed + masked(there & same, array)
+        results.append(summed)
+    back = [results[0]]
+    for k in range(1, plane):
+        back.append(lax.ppermute(results[k], "seq", pairs(k)))
+    stacked = jnp.stack(back, axis=0)
+    ordered = [lax.dynamic_index_in_dim(stacked, at ^ j, 0, False) for j in range(plane)]
+    carried = jnp.stack(ordered, axis=1).reshape(state.shape)
+    near = position + 1 if reverse else position - 1
+    exists = (near < count) & (near >= 0)
+    carried = carried * exists.astype(carried.dtype)
+    return carried, jnp.where(exists, id_of(near), -1.0)
 
 
 def project(activations, weight):
@@ -54,14 +184,6 @@
 
 def softplus_grad(values):
     return jax.nn.sigmoid(values)
-
-
-def chain_states(earlier_pair, later_pair):
-    early_sum, early_id = earlier_pair
-    late_sum, late_id = later_pair
-    joined = (late_id == early_id) | (late_id < 0)
-    summed = late_sum + jnp.where(joined[:, None, None, None], early_sum, 0.0)
-    return (summed, jnp.where(late_id < 0, early_id, late_id))
 
 
 def local(
@@ -114,8 +236,8 @@
         val_heads,
         preferred_element_type=jnp.float32,
     )
-    empty_pair = (jnp.zeros_like(local_state), -jnp.ones_like(last_ids))
-    carried, carried_id = prefix((local_state, last_ids), "seq", chain_states, empty_pair, False)
+    edge_ids = gather_ids(jnp.concatenate([first_ids, last_ids]))
+    carried, carried_id = prefix(local_state, edge_ids[:, row_count:], False)
     matched = (ids_float == carried_id[:, None])[:, :, None, None]
     carried_low = carried.astype(jnp.bfloat16)
     attn_probs = block_scores()
@@ -167,7 +289,7 @@
         back_attended,
         preferred_element_type=jnp.float32,
     )
-    grad_in, grad_id = prefix((local_grad, first_ids), "seq", chain_states, empty_pair, True)
+    grad_in, grad_id = prefix(local_grad, edge_ids[:, :row_count], True)
     attn_probs = block_scores()
     back_scores = jnp.where(
         allowed[:, None],
@@ -220,18 +342,17 @@
         .astype(jnp.bfloat16)
         .reshape(inputs.shape)
     )
-    all_shards = tuple(
-        (
-            lax.psum_scatter(grad_query, ("batch", "seq"), scatter_dimension=0, tiled=True),
-            lax.psum_scatter(grad_key, ("batch", "seq"), scatter_dimension=0, tiled=True),
-            lax.psum_scatter(grad_value, ("batch", "seq"), scatter_dimension=0, tiled=True),
-            lax.psum_scatter(grad_outgate, ("batch", "seq"), scatter_dimension=0, tiled=True),
-            lax.psum_scatter(grad_output, ("batch", "seq"), scatter_dimension=0, tiled=True),
-            lax.psum_scatter(grad_gate, ("batch", "seq"), scatter_dimension=0, tiled=True),
-            lax.psum_scatter(grad_up, ("batch", "seq"), scatter_dimension=0, tiled=True),
-            lax.psum_scatter(grad_down, ("batch", "seq"), scatter_dimension=0, tiled=True),
-            lax.psum_scatter(grad_gain, ("batch", "seq"), scatter_dimension=0, tiled=True),
-        )
+    x_first, y_first, z_first = orders(lax.axis_size("seq"))
+    all_shards = (
+        scatter_sum(grad_query, z_first),
+        scatter_sum(grad_key, x_first),
+        scatter_sum(grad_value, y_first),
+        scatter_sum(grad_outgate, z_first),
+        scatter_sum(grad_output, z_first),
+        scatter_sum(grad_gate, y_first),
+        scatter_sum(grad_up, x_first),
+        scatter_sum(grad_down, x_first),
+        scatter_sum(grad_gain, x_first),
     )
     return (block_out, input_grad) + all_shards
 

time: 2100 us -> 903 us (0.43)
  waiting for transfers between devices: 1550 us -> 291 us
  starting transfers between devices: 1.42 us -> 96 us
  blocking collectives: 83.6 us -> 0 us
  other arithmetic: 61.2 us -> 111 us
  local copies, waits for them, and re-layouts: 118 us -> 152 us
    reduce_scatter x8 -> x0, waiting for transfers between devices: 1350 us -> none  [the longest x1 253 us: local(): lax.psum_scatter(grad_up, ('batch', 'seq'), scatter_dimension=0, tiled=True)]
    ppermute x0 -> x67, waiting for transfers between devices: none -> 291 us  [the longest x36 243 us: scatter_sum(): lax.ppermute(outgoing, 'seq', [(i, i ^ flip) for i in range(count)])]
    all_gather x2 -> x0, waiting for transfers between devices: 197 us -> none  [prefix(): gathered = jax.tree.map(lambda a: lax.all_gather(a, axis), part)]
    ppermute x0 -> x67, starting transfers between devices: none -> 96 us  [the longest x36 58.4 us: scatter_sum(): lax.ppermute(outgoing, 'seq', [(i, i ^ flip) for i in range(count)])]
    unnamed x2 -> x0, blocking collectives: 83.6 us -> none
    add x15 -> x53, other arithmetic: 23.4 us -> 72.6 us  [the longest x45 67.1 us: sum_pieces(): total = one if total is None else total + one]
  transfers between devices with their start and end apart: 10 -> 67, of which waited for: 10 -> 36; matrix products, arithmetic and copies ran while one was open for 12% -> 32% of each run, Pallas kernels for 0% -> 0%
where the time goes in v1:
time: 903 us; the launch traced here: 897 us
  waiting for transfers between devices  291 us (32%)
  matrix products  244 us (27%)
  local copies, waits for them, and re-layouts  152 us (17%)
  other arithmetic  111 us (12%)
  starting transfers between devices  96 us (11%)
    ppermute x36, waiting for transfers between devices, scatter_sum(): lax.ppermute(outgoing, 'seq', [(i, i ^ flip) for i in range(count)])  243 us
    add x45, other arithmetic, sum_pieces(): total = one if total is None else total + one  67.1 us
    dot_general x8, matrix products, project_back(): lax.dot_general(grads_in, weight, (((1,), (1,)), ((), ())), preferred_ele...  63.2 us
    ppermute x36, starting transfers between devices, scatter_sum(): lax.ppermute(outgoing, 'seq', [(i, i ^ flip) for i in range(count)])  58.4 us
    dot_general x8, matrix products, project(): return jnp.dot(activations, weight, preferred_element_type=jnp.float32)  57.3 us
    dot_general x8, matrix products, outer_sum(): lax.dot_general(activations, grads_in, (((0,), (0,)), ((), ())), preferre...  43.7 us
    unnamed x256, local copies, waits for them, and re-layouts  25.6 us
    ppermute x6, waiting for transfers between devices, prefix(): passed.append((lax.ppermute(total, 'seq', moves), source))  22.8 us
  transfers between devices with their start and end apart: 67, of which 36 were waited for; matrix products, arithmetic and copies ran while one was open for 32% of the time, Pallas kernels for 0%

profile of v1, /device:TPU:0, one launch (start us, length us, event | category | flops | bytes accessed | tf_op | source)
XLA Modules:
  0.0 897.4 jit_solution(13840016693040438077)
XLA Ops:
  14.8 6.6 reshape.1632
  21.4 5.5 copy.128
  27.3 9.0 fusion.1
  44.7 8.7 fusion
  65.8 10.4 %select_convert_fusion.1 = bf16[2,16,512,512]{3,2,1,0:T(8,128)(2,1)} fusion(pred[2,512,512]{2,1,0:T(8,128)(4,1)S(1)} %compare_and_fusion, bf16[2,512,16,64]{1,0,3,2:T(2,128)(2,1)} %reshape.1430, bf16[2,512,16,64]{1,0,3,2:T(2,128)(2,1)} %reshape.1429), kind=kOutput, calls=%fused_computation.1 | convolution fusion | flops 1090519040 | bytes 21495808 | tf_op jit(solution)/shard_map/rthd,rshd->rhts/dot_general | solution.py:225
  76.2 13.5 %fusion.108 = f32[2,16,64,512]{3,2,1,0:T(8,128)} fusion(bf16[2,512,16,64]{1,3,2,0:T(8,128)(2,1)} %copy.128, bf16[2,16,512,512]{3,2,1,0:T(8,128)(2,1)} %select_convert_fusion.1), kind=kOutput, calls=%fused_computation.422 | convolution fusion | flops 1073741824 | bytes 23068672 | tf_op jit(solution)/shard_map/rhts,rshd->rthd/dot_general | solution.py:244
  116.7 5.5 collective-permute-start.9
  128.9 5.0 collective-permute-done.8
  158.4 8.6 copy.172
  167.0 7.6 reshape.1633
  174.6 8.4 multiply_convert_fusion.7
  187.9 8.9 fusion.109
  196.7 8.8 fusion.110
  205.6 18.2 %multiply_convert_fusion = (bf16[1024,2816]{1,0:T(8,128)(2,1)}, bf16[1024,2816]{1,0:T(8,128)(2,1)}, bf16[1024,2816]{1,0:T(8,128)(2,1)}) fusion(f32[1024,2816]{1,0:T(8,128)} %fusion.109, f32[1024,2816]{1,0:T(8,128)} %fusion.110, bf16[1024,1024]{1,0:T(8,128)(2,1)} %bitcast.827, bf16[2816,1024]{1,0:T(8,128)(2,1)} %param.21), kind=kOutput, calls=%fused_computation.4 | convolution fusion | flops 5922881536 | bytes 48234496 | tf_op jit(solution)/shard_map/dot_general | solution.py:170
  223.8 10.0 %fusion.111 = f32[1024,1024]{1,0:T(8,128)S(1)} fusion(bf16[1024,2816]{1,0:T(8,128)(2,1)} %get-tuple-element.97, bf16[1024,2816]{1,0:T(8,128)(2,1)} %param.19), kind=kOutput, calls=%fused_computation.425 | convolution fusion | flops 5905580032 | bytes 15728640 | tf_op jit(solution)/shard_map/dot_general | solution.py:170
  233.9 8.6 multiply_reduce_fusion.2
  247.5 5.1 multiply_reduce_fusion
  252.6 7.4 reshape.1634
  259.9 7.0 copy.142
  274.4 11.5 %fusion.114 = f32[2,16,64,512]{3,2,1,0:T(8,128)} fusion(bf16[2,512,16,64]{1,3,2,0:T(8,128)(2,1)S(1)} %multiply_convert_fusion.6, bf16[2,16,512,512]{3,2,1,0:T(8,128)(2,1)} %select_convert_fusion.1), kind=kOutput, calls=%fused_computation.428 | convolution fusion | flops 1073741824 | bytes 23068672 | tf_op jit(solution)/shard_map/rhts,rthd->rshd/dot_general | solution.py:319
  285.9 8.5 select_convert_fusion
  294.4 13.7 %fusion.26 = f32[2,16,64,512]{3,2,1,0:T(8,128)} fusion(bf16[2,16,512,512]{3,2,1,0:T(8,128)(2,1)} %select_convert_fusion, bf16[2,512,16,64]{1,0,3,2:T(2,128)(2,1)} %reshape.1430), kind=kOutput, calls=%fused_computation.71 | convolution fusion | flops 1073741824 | bytes 23068672 | tf_op jit(solution)/shard_map/rhts,rshd->rthd/dot_general | solution.py:301
  308.1 10.6 %fusion.29 = f32[2,16,64,512]{3,2,1,0:T(8,128)} fusion(bf16[2,16,512,512]{3,2,1,0:T(8,128)(2,1)} %select_convert_fusion, bf16[2,512,16,64]{1,0,3,2:T(2,128)(2,1)S(1)} %copy-done.5), kind=kOutput, calls=%fused_computation.74 | convolution fusion | flops 1073741824 | bytes 23068672 | tf_op jit(solution)/shard_map/rhts,rthd->rshd/dot_general | solution.py:311
  323.0 11.7 %fusion.116 = f32[1024,2816]{1,0:T(8,128)} fusion(bf16[1024,1024]{1,0:T(8,128)(2,1)S(1)} %copy-done.53, bf16[1024,2816]{1,0:T(8,128)(2,1)} %get-tuple-element.97), kind=kOutput, calls=%fused_computation.430 | convolution fusion | flops 5905580032 | bytes 19398656 | tf_op jit(solution)/shard_map/dot_general | solution.py:164
  334.7 9.6 %fusion.117 = f32[1024,2816]{1,0:T(8,128)} fusion(bf16[1024,1024]{1,0:T(8,128)(2,1)S(1)} %copy-done.53, bf16[1024,2816]{1,0:T(8,128)(2,1)S(1)} %bitcast.830), kind=kOutput, calls=%fused_computation.431 | convolution fusion | flops 5905580032 | bytes 19398656 | tf_op jit(solution)/shard_map/dot_general | solution.py:164
  352.2 8.1 copy.167
  360.3 7.8 reshape.1630
  395.5 8.4 copy.158
  404.0 8.7 fusion.118
  427.4 10.5 %collective-permute-start.65 = (f32[2,32]{1,0:T(2,128)S(1)}, f32[2,32]{1,0:T(2,128)S(1)}, u32[]{:S(2)}, u32[]{:S(2)}) collective-permute-start(f32[2,32]{1,0:T(2,128)S(1)} %add_add_fusion.2), channel_id=1, source_target_pairs={{0,4},{1,5},{2,6},{3,7},{4,0},{5,1},{6,2},{7,3},{8,12},{9,13},{10,... | collective-permute-start | bytes 776 | tf_op jit(solution)/shard_map/ppermute | solution.py:51
  446.3 5.9 collective-permute-done.18
  452.2 7.9 collective-permute-done.17
  476.1 5.1 collective-permute-start.66
  484.3 8.1 copy.168
  492.4 7.6 reshape.1631
  523.0 7.4 add_convert_fusion.1
  550.0 10.7 %collective-permute-done.23 = f32[2,2,2,32,1024]{4,3,2,1,0:T(8,128)S(1)} collective-permute-done((f32[2,2,2,32,1024]{4,3,2,1,0:T(8,128)S(1)}, f32[2,2,2,32,1024]{4,3,2,1,0:T(8,128)S(1)}, u32[]{:S(2)}, u32[]{:S(2)}) %collective-permute-start.23) | collective-permute-done | bytes 1048608 | tf_op jit(solution)/shard_map/ppermute | solution.py:51
  561.7 21.5 %collective-permute-done.38 = f32[2,2,2,32,1024]{4,3,2,1,0:T(8,128)S(1)} collective-permute-done((f32[2,2,2,32,1024]{4,3,2,1,0:T(8,128)S(1)}, f32[2,2,2,32,1024]{4,3,2,1,0:T(8,128)S(1)}, u32[]{:S(2)}, u32[]{:S(2)}) %collective-permute-start.38) | collective-permute-done | bytes 1048608 | tf_op jit(solution)/shard_map/ppermute | solution.py:51
  599.0 17.3 %collective-permute-done.43 = f32[2,2,2,32,1024]{4,3,2,1,0:T(8,128)S(1)} collective-permute-done((f32[2,2,2,32,1024]{4,3,2,1,0:T(8,128)S(1)}, f32[2,2,2,32,1024]{4,3,2,1,0:T(8,128)S(1)}, u32[]{:S(2)}, u32[]{:S(2)}) %collective-permute-start.43) | collective-permute-done | bytes 1048608 | tf_op jit(solution)/shard_map/ppermute | solution.py:51
  620.6 8.0 fusion.6
  634.9 19.2 %collective-permute-done.39 = f32[2,2,32,1024]{3,2,1,0:T(8,128)S(1)} collective-permute-done((f32[2,2,32,1024]{3,2,1,0:T(8,128)}, f32[2,2,32,1024]{3,2,1,0:T(8,128)S(1)}, u32[]{:S(2)}, u32[]{:S(2)}) %collective-permute-start.39) | collective-permute-done | bytes 524320 | tf_op jit(solution)/shard_map/ppermute | solution.py:51
  658.5 5.9 collective-permute-done.44
  668.8 83.7 %collective-permute-done.25 = f32[2,32,1024]{2,1,0:T(8,128)S(1)} collective-permute-done((f32[2,32,1024]{2,1,0:T(8,128)S(1)}, f32[2,32,1024]{2,1,0:T(8,128)S(1)}, u32[]{:S(2)}, u32[]{:S(2)}) %collective-permute-start.25) | collective-permute-done | bytes 262176 | tf_op jit(solution)/shard_map/ppermute | solution.py:51
  790.0 24.8 %collective-permute-done.46 = f32[32,1024]{1,0:T(8,128)S(1)} collective-permute-done((f32[32,1024]{1,0:T(8,128)S(1)}, f32[32,1024]{1,0:T(8,128)S(1)}, u32[]{:S(2)}, u32[]{:S(2)}) %collective-permute-start.46) | collective-permute-done | bytes 131104 | tf_op jit(solution)/shard_map/ppermute | solution.py:51
  843.5 12.1 %collective-permute-done.50 = f32[2,32,2816]{2,1,0:T(8,128)S(1)} collective-permute-done((f32[2,32,2816]{2,1,0:T(8,128)S(1)}, f32[2,32,2816]{2,1,0:T(8,128)S(1)}, u32[]{:S(2)}, u32[]{:S(2)}) %collective-permute-start.50) | collective-permute-done | bytes 720928 | tf_op jit(solution)/shard_map/ppermute | solution.py:51
  857.4 10.0 %collective-permute-done.55 = f32[2,32,2816]{2,1,0:T(8,128)S(1)} collective-permute-done((f32[2,32,2816]{2,1,0:T(8,128)S(1)}, f32[2,32,2816]{2,1,0:T(8,128)S(1)}, u32[]{:S(2)}, u32[]{:S(2)}) %collective-permute-start.55) | collective-permute-done | bytes 720928 | tf_op jit(solution)/shard_map/ppermute | solution.py:51
  869.8 10.7 %collective-permute-done.60 = f32[2,88,1024]{2,1,0:T(8,128)S(1)} collective-permute-done((f32[2,88,1024]{2,1,0:T(8,128)S(1)}, f32[2,88,1024]{2,1,0:T(8,128)S(1)}, u32[]{:S(2)}, u32[]{:S(2)}) %collective-permute-start.60) | collective-permute-done | bytes 720928 | tf_op jit(solution)/shard_map/ppermute | solution.py:51
  889.4 5.8 collective-permute-done.61
  (533 shorter events, 351.3 us)
Async XLA Ops:
  1.8 88.0 %collective-permute-start = (f32[1,4]{1,0:T(1,128)S(1)}, f32[1,4]{1,0:T(1,128)S(1)}, u32[]{:S(2)}, u32[]{:S(2)}) collective-permute-start(f32[1,4]{1,0:T(1,128)S(1)} %maximum_bitcast_fusion), channel_id=1, source_target_pairs={{0,1},{1,0},{2,3},{3,2},{4,5},{5,4},{6,7},{7,6},{8,9},{9,8},{10,11... | collective-permute-start | bytes 56 | tf_op jit(solution)/shard_map/ppermute | solution.py:84
  116.7 12.3 %collective-permute-start.9 = (f32[2,4,64,64]{3,2,1,0:T(8,128)S(1)}, f32[2,4,64,64]{3,2,1,0:T(8,128)S(1)}, u32[]{:S(2)}, u32[]{:S(2)}) collective-permute-start(f32[2,4,64,64]{3,2,1,0:T(8,128)S(1)} %fusion.62), channel_id=1, source_target_pairs={{0,12},{1,13},{2,14},{3,15},{16,28},{17,29},{18,30},{19,31}} | collective-permute-start | bytes 393224 | tf_op jit(solution)/shard_map/ppermute | solution.py:129
  123.5 13.2 %collective-permute-start.7 = (f32[2,4,64,64]{3,2,1,0:T(8,128)S(1)}, f32[2,4,64,64]{3,2,1,0:T(8,128)S(1)}, u32[]{:S(2)}, u32[]{:S(2)}) collective-permute-start(f32[2,4,64,64]{3,2,1,0:T(8,128)S(1)} %fusion.62), channel_id=1, source_target_pairs={{0,4},{1,5},{2,6},{3,7},{4,8},{5,9},{6,10},{7,11},{8,12},{9,13},{1... | collective-permute-start | bytes 393224 | tf_op jit(solution)/shard_map/ppermute | solution.py:129
  345.9 91.9 %collective-permute-start.15 = (f32[2,4,64,64]{3,2,1,0:T(8,128)}, f32[2,4,64,64]{3,2,1,0:T(8,128)S(1)}, u32[]{:S(2)}, u32[]{:S(2)}) collective-permute-start(f32[2,4,64,64]{3,2,1,0:T(8,128)} %get-tuple-element.104), channel_id=1, source_target_pairs={{0,3},{1,2},{2,1},{3,0},{4,7},{5,6},{6,5},{7,4},{8,11},{9,10},{10,... | collective-permute-start | bytes 393224 | tf_op jit(solution)/shard_map/ppermute | solution.py:110
  347.6 90.2 %collective-permute-start.14 = (f32[2,4,64,64]{3,2,1,0:T(8,128)}, f32[2,4,64,64]{3,2,1,0:T(8,128)}, u32[]{:S(2)}, u32[]{:S(2)}) collective-permute-start(f32[2,4,64,64]{3,2,1,0:T(8,128)} %get-tuple-element.105), channel_id=1, source_target_pairs={{0,2},{1,3},{2,0},{3,1},{4,6},{5,7},{6,4},{7,5},{8,10},{9,11},{10,... | collective-permute-start | bytes 393224 | tf_op jit(solution)/shard_map/ppermute | solution.py:110
  348.3 89.6 %collective-permute-start.13 = (f32[2,4,64,64]{3,2,1,0:T(8,128)}, f32[2,4,64,64]{3,2,1,0:T(8,128)}, u32[]{:S(2)}, u32[]{:S(2)}) collective-permute-start(f32[2,4,64,64]{3,2,1,0:T(8,128)} %get-tuple-element.103), channel_id=1, source_target_pairs={{0,1},{1,0},{2,3},{3,2},{4,5},{5,4},{6,7},{7,6},{8,9},{9,8},{10,11... | collective-permute-start | bytes 393224 | tf_op jit(solution)/shard_map/ppermute | solution.py:110
  381.0 138.9 %collective-permute-start.22 = (f32[2,2,2,2,32,1024]{5,4,3,2,1,0:T(8,128)}, f32[2,2,2,2,32,1024]{5,4,3,2,1,0:T(8,128)}, u32[]{:S(2)}, u32[]{:S(2)}) collective-permute-start(f32[2,2,2,2,32,1024]{5,4,3,2,1,0:T(8,128)} %dynamic-slice_bitcast_fusion.7), channel_id=1, source_target_pairs={{0,16},{16,0},{1,17},{17,1},{2,18},{18,2},{3,19},{19,3},{4,20},{20... | collective-permute-start | bytes 6291464 | tf_op jit(solution)/shard_map/ppermute | solution.py:48
  427.4 18.9 %collective-permute-start.65 = (f32[2,32]{1,0:T(2,128)S(1)}, f32[2,32]{1,0:T(2,128)S(1)}, u32[]{:S(2)}, u32[]{:S(2)}) collective-permute-start(f32[2,32]{1,0:T(2,128)S(1)} %add_add_fusion.2), channel_id=1, source_target_pairs={{0,4},{1,5},{2,6},{3,7},{4,0},{5,1},{6,2},{7,3},{8,12},{9,13},{10,... | collective-permute-start | bytes 776 | tf_op jit(solution)/shard_map/ppermute | solution.py:51
  439.1 13.0 %collective-permute-start.18 = (f32[2,4,64,64]{3,2,1,0:T(8,128)S(1)}, f32[2,4,64,64]{3,2,1,0:T(8,128)S(1)}, u32[]{:S(2)}, u32[]{:S(2)}) collective-permute-start(f32[2,4,64,64]{3,2,1,0:T(8,128)S(1)} %fusion.44), channel_id=1, source_target_pairs={{12,0},{13,1},{14,2},{15,3},{28,16},{29,17},{30,18},{31,19}} | collective-permute-start | bytes 393224 | tf_op jit(solution)/shard_map/ppermute | solution.py:129
  440.4 19.6 %collective-permute-start.17 = (f32[2,4,64,64]{3,2,1,0:T(8,128)S(1)}, f32[2,4,64,64]{3,2,1,0:T(8,128)S(1)}, u32[]{:S(2)}, u32[]{:S(2)}) collective-permute-start(f32[2,4,64,64]{3,2,1,0:T(8,128)S(1)} %fusion.44), channel_id=1, source_target_pairs={{8,0},{9,1},{10,2},{11,3},{12,4},{13,5},{14,6},{15,7},{24,16},{25,... | collective-permute-start | bytes 393224 | tf_op jit(solution)/shard_map/ppermute | solution.py:129
  441.7 18.3 %collective-permute-start.16 = (f32[2,4,64,64]{3,2,1,0:T(8,128)S(1)}, f32[2,4,64,64]{3,2,1,0:T(8,128)S(1)}, u32[]{:S(2)}, u32[]{:S(2)}) collective-permute-start(f32[2,4,64,64]{3,2,1,0:T(8,128)S(1)} %fusion.44), channel_id=1, source_target_pairs={{4,0},{5,1},{6,2},{7,3},{8,4},{9,5},{10,6},{11,7},{12,8},{13,9},{1... | collective-permute-start | bytes 393224 | tf_op jit(solution)/shard_map/ppermute | solution.py:129
  446.3 73.9 %collective-permute-start.37 = (f32[2,2,2,2,32,1024]{5,4,3,2,1,0:T(8,128)}, f32[2,2,2,2,32,1024]{5,4,3,2,1,0:T(8,128)}, u32[]{:S(2)}, u32[]{:S(2)}) collective-permute-start(f32[2,2,2,2,32,1024]{5,4,3,2,1,0:T(8,128)} %dynamic-slice_bitcast_fusion.4), channel_id=1, source_target_pairs={{0,16},{16,0},{1,17},{17,1},{2,18},{18,2},{3,19},{19,3},{4,20},{20... | collective-permute-start | bytes 6291464 | tf_op jit(solution)/shard_map/ppermute | solution.py:48
  471.5 49.0 %collective-permute-start.42 = (f32[2,2,2,2,32,1024]{5,4,3,2,1,0:T(8,128)}, f32[2,2,2,2,32,1024]{5,4,3,2,1,0:T(8,128)}, u32[]{:S(2)}, u32[]{:S(2)}) collective-permute-start(f32[2,2,2,2,32,1024]{5,4,3,2,1,0:T(8,128)} %dynamic-slice_bitcast_fusion.3), channel_id=1, source_target_pairs={{0,16},{16,0},{1,17},{17,1},{2,18},{18,2},{3,19},{19,3},{4,20},{20... | collective-permute-start | bytes 6291464 | tf_op jit(solution)/shard_map/ppermute | solution.py:48
  476.0 111.2 %collective-permute-start.47 = (f32[2,2,2,2,32,2816]{5,4,3,2,1,0:T(8,128)}, f32[2,2,2,2,32,2816]{5,4,3,2,1,0:T(8,128)}, u32[]{:S(2)}, u32[]{:S(2)}) collective-permute-start(f32[2,2,2,2,32,2816]{5,4,3,2,1,0:T(8,128)} %dynamic-slice_bitcast_fusion.2), channel_id=1, source_target_pairs={{0,16},{16,0},{1,17},{17,1},{2,18},{18,2},{3,19},{19,3},{4,20},{20... | collective-permute-start | bytes 17301512 | tf_op jit(solution)/shard_map/ppermute | solution.py:48
  476.1 38.5 %collective-permute-start.66 = (f32[32]{0:T(128)S(1)}, f32[32]{0:T(128)S(1)}, u32[]{:S(2)}, u32[]{:S(2)}) collective-permute-start(f32[32]{0:T(128)S(1)} %fusion.91), channel_id=1, source_target_pairs={{0,8},{1,9},{2,10},{3,11},{4,12},{5,13},{6,14},{7,15},{8,0},{9,1},... | collective-permute-start | bytes 392 | tf_op jit(solution)/shard_map/ppermute | solution.py:51
  514.6 79.2 %collective-permute-start.52 = (f32[2,2,2,2,32,2816]{5,4,3,2,1,0:T(8,128)}, f32[2,2,2,2,32,2816]{5,4,3,2,1,0:T(8,128)}, u32[]{:S(2)}, u32[]{:S(2)}) collective-permute-start(f32[2,2,2,2,32,2816]{5,4,3,2,1,0:T(8,128)} %dynamic-slice_bitcast_fusion.1), channel_id=1, source_target_pairs={{0,16},{16,0},{1,17},{17,1},{2,18},{18,2},{3,19},{19,3},{4,20},{20... | collective-permute-start | bytes 17301512 | tf_op jit(solution)/shard_map/ppermute | solution.py:48
  519.9 110.1 %collective-permute-start.57 = (f32[2,2,2,2,88,1024]{5,4,3,2,1,0:T(8,128)S(1)}, f32[2,2,2,2,88,1024]{5,4,3,2,1,0:T(8,128)}, u32[]{:S(2)}, u32[]{:S(2)}) collective-permute-start(f32[2,2,2,2,88,1024]{5,4,3,2,1,0:T(8,128)S(1)} %bitcast.864), channel_id=1, source_target_pairs={{0,16},{16,0},{1,17},{17,1},{2,18},{18,2},{3,19},{19,3},{4,20},{20... | collective-permute-start | bytes 17301512 | tf_op jit(solution)/shard_map/ppermute | solution.py:48
  520.2 14.5 %collective-permute-start.27 = (f32[2,2,2,2,32,1024]{5,4,3,2,1,0:T(8,128)}, f32[2,2,2,2,32,1024]{5,4,3,2,1,0:T(8,128)S(1)}, u32[]{:S(2)}, u32[]{:S(2)}) collective-permute-start(f32[2,2,2,2,32,1024]{5,4,3,2,1,0:T(8,128)} %dynamic-slice_bitcast_fusion.6), channel_id=1, source_target_pairs={{0,16},{16,0},{1,17},{17,1},{2,18},{18,2},{3,19},{19,3},{4,20},{20... | collective-permute-start | bytes 6291464 | tf_op jit(solution)/shard_map/ppermute | solution.py:48
  520.5 15.8 %collective-permute-start.32 = (f32[2,2,2,2,32,1024]{5,4,3,2,1,0:T(8,128)}, f32[2,2,2,2,32,1024]{5,4,3,2,1,0:T(8,128)S(1)}, u32[]{:S(2)}, u32[]{:S(2)}) collective-permute-start(f32[2,2,2,2,32,1024]{5,4,3,2,1,0:T(8,128)} %dynamic-slice_bitcast_fusion.5), channel_id=1, source_target_pairs={{0,16},{16,0},{1,17},{17,1},{2,18},{18,2},{3,19},{19,3},{4,20},{20... | collective-permute-start | bytes 6291464 | tf_op jit(solution)/shard_map/ppermute | solution.py:48
  534.7 26.1 %collective-permute-start.23 = (f32[2,2,2,32,1024]{4,3,2,1,0:T(8,128)S(1)}, f32[2,2,2,32,1024]{4,3,2,1,0:T(8,128)S(1)}, u32[]{:S(2)}, u32[]{:S(2)}) collective-permute-start(f32[2,2,2,32,1024]{4,3,2,1,0:T(8,128)S(1)} %bitcast_add_fusion.14), channel_id=1, source_target_pairs={{0,4},{1,5},{2,6},{3,7},{4,0},{5,1},{6,2},{7,3},{8,12},{9,13},{10,... | collective-permute-start | bytes 3145736 | tf_op jit(solution)/shard_map/ppermute | solution.py:51
  536.3 46.9 %collective-permute-start.38 = (f32[2,2,2,32,1024]{4,3,2,1,0:T(8,128)S(1)}, f32[2,2,2,32,1024]{4,3,2,1,0:T(8,128)S(1)}, u32[]{:S(2)}, u32[]{:S(2)}) collective-permute-start(f32[2,2,2,32,1024]{4,3,2,1,0:T(8,128)S(1)} %bitcast_add_fusion.11), channel_id=1, source_target_pairs={{0,4},{1,5},{2,6},{3,7},{4,0},{5,1},{6,2},{7,3},{8,12},{9,13},{10,... | collective-permute-start | bytes 3145736 | tf_op jit(solution)/shard_map/ppermute | solution.py:51
  560.8 55.5 %collective-permute-start.43 = (f32[2,2,2,32,1024]{4,3,2,1,0:T(8,128)S(1)}, f32[2,2,2,32,1024]{4,3,2,1,0:T(8,128)S(1)}, u32[]{:S(2)}, u32[]{:S(2)}) collective-permute-start(f32[2,2,2,32,1024]{4,3,2,1,0:T(8,128)S(1)} %bitcast_add_fusion.10), channel_id=1, source_target_pairs={{0,4},{1,5},{2,6},{3,7},{4,0},{5,1},{6,2},{7,3},{8,12},{9,13},{10,... | collective-permute-start | bytes 3145736 | tf_op jit(solution)/shard_map/ppermute | solution.py:51
  583.2 34.5 %collective-permute-start.28 = (f32[2,2,2,32,1024]{4,3,2,1,0:T(8,128)S(1)}, f32[2,2,2,32,1024]{4,3,2,1,0:T(8,128)S(1)}, u32[]{:S(2)}, u32[]{:S(2)}) collective-permute-start(f32[2,2,2,32,1024]{4,3,2,1,0:T(8,128)S(1)} %bitcast_add_fusion.13), channel_id=1, source_target_pairs={{0,1},{1,0},{2,3},{3,2},{4,5},{5,4},{6,7},{7,6},{8,9},{9,8},{10,11... | collective-permute-start | bytes 3145736 | tf_op jit(solution)/shard_map/ppermute | solution.py:51
  587.3 31.0 %collective-permute-start.24 = (f32[2,2,32,1024]{3,2,1,0:T(8,128)S(1)}, f32[2,2,32,1024]{3,2,1,0:T(8,128)S(1)}, u32[]{:S(2)}, u32[]{:S(2)}) collective-permute-start(f32[2,2,32,1024]{3,2,1,0:T(8,128)S(1)} %bitcast_add_fusion.32), channel_id=1, source_target_pairs={{0,8},{1,9},{2,10},{3,11},{4,12},{5,13},{6,14},{7,15},{8,0},{9,1},... | collective-permute-start | bytes 1572872 | tf_op jit(solution)/shard_map/ppermute | solution.py:51
  593.8 63.3 %collective-permute-start.33 = (f32[2,2,2,32,1024]{4,3,2,1,0:T(8,128)S(1)}, f32[2,2,2,32,1024]{4,3,2,1,0:T(8,128)}, u32[]{:S(2)}, u32[]{:S(2)}) collective-permute-start(f32[2,2,2,32,1024]{4,3,2,1,0:T(8,128)S(1)} %bitcast_add_fusion.12), channel_id=1, source_target_pairs={{0,2},{1,3},{2,0},{3,1},{4,6},{5,7},{6,4},{7,5},{8,10},{9,11},{10,... | collective-permute-start | bytes 3145736 | tf_op jit(solution)/shard_map/ppermute | solution.py:51
  616.2 37.8 %collective-permute-start.39 = (f32[2,2,32,1024]{3,2,1,0:T(8,128)}, f32[2,2,32,1024]{3,2,1,0:T(8,128)S(1)}, u32[]{:S(2)}, u32[]{:S(2)}) collective-permute-start(f32[2,2,32,1024]{3,2,1,0:T(8,128)} %bitcast_add_fusion.26), channel_id=1, source_target_pairs={{0,8},{1,9},{2,10},{3,11},{4,12},{5,13},{6,14},{7,15},{8,0},{9,1},... | collective-permute-start | bytes 1572872 | tf_op jit(solution)/shard_map/ppermute | solution.py:51
  617.7 149.2 %collective-permute-start.48 = (f32[2,2,2,32,2816]{4,3,2,1,0:T(8,128)}, f32[2,2,2,32,2816]{4,3,2,1,0:T(8,128)}, u32[]{:S(2)}, u32[]{:S(2)}) collective-permute-start(f32[2,2,2,32,2816]{4,3,2,1,0:T(8,128)} %bitcast_add_fusion.3), channel_id=1, source_target_pairs={{0,2},{1,3},{2,0},{3,1},{4,6},{5,7},{6,4},{7,5},{8,10},{9,11},{10,... | collective-permute-start | bytes 8650760 | tf_op jit(solution)/shard_map/ppermute | solution.py:51
  619.5 150.9 %collective-permute-start.53 = (f32[2,2,2,32,2816]{4,3,2,1,0:T(8,128)}, f32[2,2,2,32,2816]{4,3,2,1,0:T(8,128)}, u32[]{:S(2)}, u32[]{:S(2)}) collective-permute-start(f32[2,2,2,32,2816]{4,3,2,1,0:T(8,128)} %bitcast_add_fusion.2), channel_id=1, source_target_pairs={{0,1},{1,0},{2,3},{3,2},{4,5},{5,4},{6,7},{7,6},{8,9},{9,8},{10,11... | collective-permute-start | bytes 8650760 | tf_op jit(solution)/shard_map/ppermute | solution.py:51
  630.1 34.3 %collective-permute-start.44 = (f32[2,2,32,1024]{3,2,1,0:T(8,128)S(1)}, f32[2,2,32,1024]{3,2,1,0:T(8,128)S(1)}, u32[]{:S(2)}, u32[]{:S(2)}) collective-permute-start(f32[2,2,32,1024]{3,2,1,0:T(8,128)S(1)} %bitcast_add_fusion.24), channel_id=1, source_target_pairs={{0,8},{1,9},{2,10},{3,11},{4,12},{5,13},{6,14},{7,15},{8,0},{9,1},... | collective-permute-start | bytes 1572872 | tf_op jit(solution)/shard_map/ppermute | solution.py:51
  654.0 128.5 %collective-permute-start.58 = (f32[2,2,2,88,1024]{4,3,2,1,0:T(8,128)S(1)}, f32[2,2,2,88,1024]{4,3,2,1,0:T(8,128)S(1)}, u32[]{:S(2)}, u32[]{:S(2)}) collective-permute-start(f32[2,2,2,88,1024]{4,3,2,1,0:T(8,128)S(1)} %bitcast_add_fusion.1), channel_id=1, source_target_pairs={{0,1},{1,0},{2,3},{3,2},{4,5},{5,4},{6,7},{7,6},{8,9},{9,8},{10,11... | collective-permute-start | bytes 8650760 | tf_op jit(solution)/shard_map/ppermute | solution.py:51
  657.0 95.5 %collective-permute-start.25 = (f32[2,32,1024]{2,1,0:T(8,128)S(1)}, f32[2,32,1024]{2,1,0:T(8,128)S(1)}, u32[]{:S(2)}, u32[]{:S(2)}) collective-permute-start(f32[2,32,1024]{2,1,0:T(8,128)S(1)} %bitcast_add_fusion.70), channel_id=1, source_target_pairs={{0,1},{1,0},{2,3},{3,2},{4,5},{5,4},{6,7},{7,6},{8,9},{9,8},{10,11... | collective-permute-start | bytes 786440 | tf_op jit(solution)/shard_map/ppermute | solution.py:51
  664.4 91.9 %collective-permute-start.40 = (f32[2,32,1024]{2,1,0:T(8,128)S(1)}, f32[2,32,1024]{2,1,0:T(8,128)S(1)}, u32[]{:S(2)}, u32[]{:S(2)}) collective-permute-start(f32[2,32,1024]{2,1,0:T(8,128)S(1)} %bitcast_add_fusion.61), channel_id=1, source_target_pairs={{0,1},{1,0},{2,3},{3,2},{4,5},{5,4},{6,7},{7,6},{8,9},{9,8},{10,11... | collective-permute-start | bytes 786440 | tf_op jit(solution)/shard_map/ppermute | solution.py:51
  762.7 14.9 %collective-permute-start.34 = (f32[2,2,32,1024]{3,2,1,0:T(8,128)S(1)}, f32[2,2,32,1024]{3,2,1,0:T(8,128)S(1)}, u32[]{:S(2)}, u32[]{:S(2)}) collective-permute-start(f32[2,2,32,1024]{3,2,1,0:T(8,128)S(1)} %bitcast_add_fusion.28), channel_id=1, source_target_pairs={{0,1},{1,0},{2,3},{3,2},{4,5},{5,4},{6,7},{7,6},{8,9},{9,8},{10,11... | collective-permute-start | bytes 1572872 | tf_op jit(solution)/shard_map/ppermute | solution.py:51
  764.7 14.9 %collective-permute-start.26 = (f32[32,1024]{1,0:T(8,128)S(1)}, f32[32,1024]{1,0:T(8,128)S(1)}, u32[]{:S(2)}, u32[]{:S(2)}) collective-permute-start(f32[32,1024]{1,0:T(8,128)S(1)} %bitcast_add_fusion.105), channel_id=1, source_target_pairs={{0,2},{1,3},{2,0},{3,1},{4,6},{5,7},{6,4},{7,5},{8,10},{9,11},{10,... | collective-permute-start | bytes 393224 | tf_op jit(solution)/shard_map/ppermute | solution.py:51
  766.9 20.6 %collective-permute-start.41 = (f32[32,1024]{1,0:T(8,128)S(1)}, f32[32,1024]{1,0:T(8,128)S(1)}, u32[]{:S(2)}, u32[]{:S(2)}) collective-permute-start(f32[32,1024]{1,0:T(8,128)S(1)} %bitcast_add_fusion.81), channel_id=1, source_target_pairs={{0,2},{1,3},{2,0},{3,1},{4,6},{5,7},{6,4},{7,5},{8,10},{9,11},{10,... | collective-permute-start | bytes 393224 | tf_op jit(solution)/shard_map/ppermute | solution.py:51
  770.4 57.3 %collective-permute-start.49 = (f32[2,2,32,2816]{3,2,1,0:T(8,128)S(1)}, f32[2,2,32,2816]{3,2,1,0:T(8,128)S(1)}, u32[]{:S(2)}, u32[]{:S(2)}) collective-permute-start(f32[2,2,32,2816]{3,2,1,0:T(8,128)S(1)} %bitcast_add_fusion.8), channel_id=1, source_target_pairs={{0,1},{1,0},{2,3},{3,2},{4,5},{5,4},{6,7},{7,6},{8,9},{9,8},{10,11... | collective-permute-start | bytes 4325384 | tf_op jit(solution)/shard_map/ppermute | solution.py:51
  777.5 54.4 %collective-permute-start.54 = (f32[2,2,32,2816]{3,2,1,0:T(8,128)S(1)}, f32[2,2,32,2816]{3,2,1,0:T(8,128)S(1)}, u32[]{:S(2)}, u32[]{:S(2)}) collective-permute-start(f32[2,2,32,2816]{3,2,1,0:T(8,128)S(1)} %bitcast_add_fusion.6), channel_id=1, source_target_pairs={{0,2},{1,3},{2,0},{3,1},{4,6},{5,7},{6,4},{7,5},{8,10},{9,11},{10,... | collective-permute-start | bytes 4325384 | tf_op jit(solution)/shard_map/ppermute | solution.py:51
  779.6 35.2 %collective-permute-start.46 = (f32[32,1024]{1,0:T(8,128)S(1)}, f32[32,1024]{1,0:T(8,128)S(1)}, u32[]{:S(2)}, u32[]{:S(2)}) collective-permute-start(f32[32,1024]{1,0:T(8,128)S(1)} %bitcast_add_fusion.73), channel_id=1, source_target_pairs={{0,2},{1,3},{2,0},{3,1},{4,6},{5,7},{6,4},{7,5},{8,10},{9,11},{10,... | collective-permute-start | bytes 393224 | tf_op jit(solution)/shard_map/ppermute | solution.py:51
  782.5 36.7 %collective-permute-start.30 = (f32[2,32,1024]{2,1,0:T(8,128)S(1)}, f32[2,32,1024]{2,1,0:T(8,128)S(1)}, u32[]{:S(2)}, u32[]{:S(2)}) collective-permute-start(f32[2,32,1024]{2,1,0:T(8,128)S(1)} %bitcast_add_fusion.67), channel_id=1, source_target_pairs={{0,4},{1,5},{2,6},{3,7},{4,0},{5,1},{6,2},{7,3},{8,12},{9,13},{10,... | collective-permute-start | bytes 786440 | tf_op jit(solution)/shard_map/ppermute | solution.py:51
  787.4 50.1 %collective-permute-start.59 = (f32[2,2,88,1024]{3,2,1,0:T(8,128)S(1)}, f32[2,2,88,1024]{3,2,1,0:T(8,128)S(1)}, u32[]{:S(2)}, u32[]{:S(2)}) collective-permute-start(f32[2,2,88,1024]{3,2,1,0:T(8,128)S(1)} %bitcast_add_fusion.4), channel_id=1, source_target_pairs={{0,2},{1,3},{2,0},{3,1},{4,6},{5,7},{6,4},{7,5},{8,10},{9,11},{10,... | collective-permute-start | bytes 4325384 | tf_op jit(solution)/shard_map/ppermute | solution.py:51
  820.1 13.3 %collective-permute-start.31 = (f32[32,1024]{1,0:T(8,128)S(1)}, f32[32,1024]{1,0:T(8,128)S(1)}, u32[]{:S(2)}, u32[]{:S(2)}) collective-permute-start(f32[32,1024]{1,0:T(8,128)S(1)} %bitcast_add_fusion.97), channel_id=1, source_target_pairs={{0,8},{1,9},{2,10},{3,11},{4,12},{5,13},{6,14},{7,15},{8,0},{9,1},... | collective-permute-start | bytes 393224 | tf_op jit(solution)/shard_map/ppermute | solution.py:51
  825.8 16.1 %collective-permute-start.36 = (f32[32,1024]{1,0:T(8,128)S(1)}, f32[32,1024]{1,0:T(8,128)S(1)}, u32[]{:S(2)}, u32[]{:S(2)}) collective-permute-start(f32[32,1024]{1,0:T(8,128)S(1)} %bitcast_add_fusion.89), channel_id=1, source_target_pairs={{0,8},{1,9},{2,10},{3,11},{4,12},{5,13},{6,14},{7,15},{8,0},{9,1},... | collective-permute-start | bytes 393224 | tf_op jit(solution)/shard_map/ppermute | solution.py:51
  829.4 26.3 %collective-permute-start.50 = (f32[2,32,2816]{2,1,0:T(8,128)S(1)}, f32[2,32,2816]{2,1,0:T(8,128)S(1)}, u32[]{:S(2)}, u32[]{:S(2)}) collective-permute-start(f32[2,32,2816]{2,1,0:T(8,128)S(1)} %bitcast_add_fusion.21), channel_id=1, source_target_pairs={{0,4},{1,5},{2,6},{3,7},{4,0},{5,1},{6,2},{7,3},{8,12},{9,13},{10,... | collective-permute-start | bytes 2162696 | tf_op jit(solution)/shard_map/ppermute | solution.py:51
  833.4 34.1 %collective-permute-start.55 = (f32[2,32,2816]{2,1,0:T(8,128)S(1)}, f32[2,32,2816]{2,1,0:T(8,128)S(1)}, u32[]{:S(2)}, u32[]{:S(2)}) collective-permute-start(f32[2,32,2816]{2,1,0:T(8,128)S(1)} %bitcast_add_fusion.18), channel_id=1, source_target_pairs={{0,4},{1,5},{2,6},{3,7},{4,0},{5,1},{6,2},{7,3},{8,12},{9,13},{10,... | collective-permute-start | bytes 2162696 | tf_op jit(solution)/shard_map/ppermute | solution.py:51
  839.1 41.4 %collective-permute-start.60 = (f32[2,88,1024]{2,1,0:T(8,128)S(1)}, f32[2,88,1024]{2,1,0:T(8,128)S(1)}, u32[]{:S(2)}, u32[]{:S(2)}) collective-permute-start(f32[2,88,1024]{2,1,0:T(8,128)S(1)} %bitcast_add_fusion.15), channel_id=1, source_target_pairs={{0,4},{1,5},{2,6},{3,7},{4,0},{5,1},{6,2},{7,3},{8,12},{9,13},{10,... | collective-permute-start | bytes 2162696 | tf_op jit(solution)/shard_map/ppermute | solution.py:51
  856.9 27.0 %collective-permute-start.51 = (f32[32,2816]{1,0:T(8,128)S(1)}, f32[32,2816]{1,0:T(8,128)S(1)}, u32[]{:S(2)}, u32[]{:S(2)}) collective-permute-start(f32[32,2816]{1,0:T(8,128)S(1)} %bitcast_add_fusion.50), channel_id=1, source_target_pairs={{0,8},{1,9},{2,10},{3,11},{4,12},{5,13},{6,14},{7,15},{8,0},{9,1},... | collective-permute-start | bytes 1081352 | tf_op jit(solution)/shard_map/ppermute | solution.py:51
  868.7 18.8 %collective-permute-start.56 = (f32[32,2816]{1,0:T(8,128)S(1)}, f32[32,2816]{1,0:T(8,128)S(1)}, u32[]{:S(2)}, u32[]{:S(2)}) collective-permute-start(f32[32,2816]{1,0:T(8,128)S(1)} %bitcast_add_fusion.42), channel_id=1, source_target_pairs={{0,8},{1,9},{2,10},{3,11},{4,12},{5,13},{6,14},{7,15},{8,0},{9,1},... | collective-permute-start | bytes 1081352 | tf_op jit(solution)/shard_map/ppermute | solution.py:51
  881.9 13.3 %collective-permute-start.61 = (f32[88,1024]{1,0:T(8,128)S(1)}, f32[88,1024]{1,0:T(8,128)S(1)}, u32[]{:S(2)}, u32[]{:S(2)}) collective-permute-start(f32[88,1024]{1,0:T(8,128)S(1)} %bitcast_add_fusion.34), channel_id=1, source_target_pairs={{0,8},{1,9},{2,10},{3,11},{4,12},{5,13},{6,14},{7,15},{8,0},{9,1},... | collective-permute-start | bytes 1081352 | tf_op jit(solution)/shard_map/ppermute | solution.py:51
  (145 other events, 2410.0 us)

commit v2 on v0

v2 whole, which is shorter than its diff:
```python
import functools

import jax
import jax.numpy as jnp
from jax import lax
from jax.experimental import pallas as pl
from jax.experimental.pallas import tpu as pltpu
from jax.sharding import PartitionSpec as P

HEADS = 16
HEAD_DIM = 64
GROUP = 4 * HEAD_DIM
TILE = 256
EPSILON = 1e-06
F32 = jnp.float32
BF16 = jnp.bfloat16
VMEM_BYTES = 56 << 20


def chip_grid(count):
    bits = count.bit_length() - 1
    z_bits = min(bits, 2)
    y_bits = (bits - z_bits + 1) // 2
    return z_bits, y_bits, bits - z_bits - y_bits


def orders(count):
    z_bits, y_bits, x_bits = chip_grid(count)
    z_axes = list(range(z_bits))[::-1]
    y_axes = list(range(z_bits, z_bits + y_bits))[::-1]
    x_axes = list(range(z_bits + y_bits, z_bits + y_bits + x_bits))[::-1]
    return x_axes + y_axes + z_axes, y_axes + x_axes + z_axes, z_axes + x_axes + y_axes


def piece(array, axes, picks, columns):
    held = len(axes)
    starts = [picks.get(a, 0) for a in axes] + [0] * (array.ndim - held)
    sizes = [1 if a in picks else 2 for a in axes] + list(array.shape[held:])
    if columns is not None:
        starts[-1] = columns[0]
        sizes[-1] = columns[1] - columns[0]
    taken = lax.dynamic_slice(array, starts, sizes)
    left = sum(a not in picks for a in axes)
    return taken.reshape((2,) * left + tuple(sizes[held:]))


def sum_pieces(parts, picks):
    total = None
    for array, axes, columns in parts:
        one = piece(array, axes, {a: v for a, v in picks.items() if a in axes}, columns)
        total = one if total is None else total + one
    return total


def scatter_seq(halves, order, columns=None):
    count = lax.axis_size("seq")
    bits = count.bit_length() - 1
    axes = tuple(range(bits))
    position = lax.axis_index("seq")
    mine = {a: (position >> (bits - 1 - a)) & 1 for a in axes}
    rows = halves[0].shape[0] // count
    parts = [(h.reshape((2,) * bits + (rows,) + h.shape[1:]), axes, columns) for h in halves]
    done = {}
    for axis in order:
        outgoing = sum_pieces(parts, {**done, axis: 1 - mine[axis]})
        flip = 1 << (bits - 1 - axis)
        incoming = lax.ppermute(outgoing, "seq", [(i, i ^ flip) for i in range(count)])
        done[axis] = mine[axis]
        parts.append((incoming, tuple(a for a in axes if a not in done), None))
    return sum_pieces(parts, done)


def to_core(array):
    return lax.ppermute(array, "batch", [(0, 1), (1, 0)])


def call(kernel, grid, in_specs, out_specs, out_shape, scratch=(), prefetch=0, flops=0, bytes_accessed=0):
    spec = pltpu.PrefetchScalarGridSpec(
        num_scalar_prefetch=prefetch,
        grid=grid,
        in_specs=in_specs,
        out_specs=out_specs,
        scratch_shapes=scratch,
    )
    return pl.pallas_call(
        kernel,
        grid_spec=spec,
        out_shape=out_shape,
        compiler_params=pltpu.CompilerParams(vmem_limit_bytes=VMEM_BYTES),
        cost_estimate=pl.CostEstimate(flops=flops, bytes_accessed=bytes_accessed, transcendentals=0),
    )


def shape(dims, dtype):
    return jax.ShapeDtypeStruct(dims, dtype)


def dot(a, b):
    return lax.dot_general(a, b, (((1,), (0,)), ((), ())), preferred_element_type=F32)


def dot_nt(a, b):
    return lax.dot_general(a, b, (((1,), (1,)), ((), ())), preferred_element_type=F32)


def dot_tn(a, b):
    return lax.dot_general(a, b, (((0,), (0,)), ((), ())), preferred_element_type=F32)


def grad_half(acts, grads, half, extra=None):
    tokens, width = acts.shape
    wide = width // 2
    cols = grads.shape[1]
    tile = 512 if cols % 512 == 0 else 256
    given = [extra] if extra is not None else []

    def kernel(half_ref, a_ref, g_ref, *rest):
        total = dot_tn(a_ref[...], g_ref[...])
        if given:
            total = total + rest[0][...]
        rest[-1][...] = total

    out_block = pl.BlockSpec((wide, tile), lambda j, s: (0, j))
    return call(
        kernel,
        (cols // tile,),
        [
            pl.BlockSpec((tokens, wide), lambda j, s: (0, s[0])),
            pl.BlockSpec((tokens, tile), lambda j, s: (0, j)),
        ]
        + [out_block] * len(given),
        out_block,
        shape((wide, cols), F32),
        prefetch=1,
        flops=2 * tokens * wide * cols,
        bytes_accessed=2 * tokens * (wide + cols) + 4 * wide * cols * (1 + len(given)),
    )(half, acts, grads, *given)


def gather_ids(ids):
    count = lax.axis_size("seq")
    bits = count.bit_length() - 1
    position = lax.axis_index("seq")
    held = ids[None]
    for step in range(bits):
        flip = 1 << step
        other = lax.ppermute(held, "seq", [(i, i ^ flip) for i in range(count)])
        low = (position & flip) == 0
        held = jnp.concatenate([jnp.where(low, held, other), jnp.where(low, other, held)], axis=0)
    return held


def weighted_sums(weights, arrays):
    outs, count, row_count = weights.shape

    def kernel(w_ref, *refs):
        for k in range(outs):
            for r in range(row_count):
                total = None
                for j in range(count):
                    flag = w_ref[(k * count + j) * row_count + r]
                    one = jnp.where(flag > 0.0, refs[j][r], 0.0)
                    total = one if total is None else total + one
                refs[count + k][r] = total

    whole = pl.BlockSpec(memory_space=pltpu.VMEM)
    return pl.pallas_call(
        kernel,
        in_specs=[pl.BlockSpec(memory_space=pltpu.SMEM)] + [whole] * count,
        out_specs=[whole] * outs,
        out_shape=[shape(arrays[0].shape, F32)] * outs,
    )(weights.reshape(-1), *arrays)


def split_shares(state, at, plane):
    row_count, depth, lanes = state.shape
    size = depth // plane

    def kernel(at_ref, s_ref, *outs):
        for k in range(plane):
            begin = pl.multiple_of((at_ref[0] ^ k) * size, size)
            outs[k][...] = s_ref[:, pl.ds(begin, size), :]

    whole = pl.BlockSpec(memory_space=pltpu.VMEM)
    return pl.pallas_call(
        kernel,
        in_specs=[pl.BlockSpec(memory_space=pltpu.SMEM), whole],
        out_specs=[whole] * plane,
        out_shape=[shape((row_count, size, lanes), F32)] * plane,
    )(at, state)


def join_shares(shares, at):
    plane = len(shares)
    row_count, size, lanes = shares[0].shape

    def kernel(at_ref, *refs):
        for k in range(plane):
            begin = pl.multiple_of((at_ref[0] ^ k) * size, size)
            refs[plane][:, pl.ds(begin, size), :] = refs[k][...]

    whole = pl.BlockSpec(memory_space=pltpu.VMEM)
    return pl.pallas_call(
        kernel,
        in_specs=[pl.BlockSpec(memory_space=pltpu.SMEM)] + [whole] * plane,
        out_specs=whole,
        out_shape=shape((row_count, size * plane, lanes), F32),
    )(at, *shares)


def prefix_plan(ids, reverse):
    count = lax.axis_size("seq")
    position = lax.axis_index("seq")
    z_bits, y_bits, x_bits = chip_grid(count)
    planes = 1 << z_bits
    plane = 1 << (y_bits + x_bits)
    z_at, at = position // plane, position % plane
    end = 0 if reverse else plane - 1

    def id_of(index):
        return lax.dynamic_index_in_dim(ids, jnp.clip(index, 0, count - 1), 0, False)

    last = id_of(z_at * plane + end)
    in_plane = [id_of(z_at * plane + (at ^ k)) for k in range(plane)]
    to_total = jnp.stack([one == last for one in in_plane])[None]
    rows = []
    for k in range(plane):
        target_at = at ^ k
        target = z_at * plane + target_at
        near_id = id_of(target + 1 if reverse else target - 1)
        row = []
        for j in range(plane):
            source_at = at ^ j
            before = source_at > target_at if reverse else source_at < target_at
            row.append(before & (in_plane[j] == near_id))
        for step in range(1, planes):
            source = z_at + step if reverse else z_at - step
            there = (source >= 0) & (source < planes)
            row.append(there & (id_of(source * plane + end) == near_id))
        rows.append(jnp.stack(row))
    near = position + 1 if reverse else position - 1
    near_id = jnp.where((near < count) & (near >= 0), id_of(near), -1.0)
    return to_total.astype(F32), jnp.stack(rows).astype(F32), near_id


def prefix(state, to_total, to_results, reverse):
    count = lax.axis_size("seq")
    z_bits, y_bits, x_bits = chip_grid(count)
    planes = 1 << z_bits
    plane = 1 << (y_bits + x_bits)
    at = (lax.axis_index("seq") % plane).astype(jnp.int32).reshape(1)

    def swap(shares):
        return [shares[0]] + [
            lax.ppermute(
                shares[k], "seq", [(i, (i // plane) * plane + ((i % plane) ^ k)) for i in range(count)]
            )
            for k in range(1, plane)
        ]

    swapped = swap(split_shares(state, at, plane))
    (total,) = weighted_sums(to_total, swapped)
    passed = []
    for step in range(1, planes):
        shift = -step * plane if reverse else step * plane
        moves = [(i, i + shift) for i in range(count) if 0 <= i + shift < count]
        passed.append(lax.ppermute(total, "seq", moves))
    return join_shares(swap(weighted_sums(to_results, swapped + passed)), at)


def softplus(v):
    return jnp.maximum(v, 0.0) + jnp.log1p(jnp.exp(-jnp.abs(v)))


def sigmoid(v):
    return 1.0 / (1.0 + jnp.exp(-v))


def sigmoid_of_softplus(s):
    return jnp.where(s < 0.01, s * (1.0 - s * (0.5 - s * (1.0 / 6.0))), 1.0 - jnp.exp(-s))


def mean_square(v):
    return jnp.mean(v * v, axis=-1, keepdims=True)


def head_ones():
    a = lax.broadcasted_iota(jnp.int32, (GROUP, GROUP), 0) >> 6
    b = lax.broadcasted_iota(jnp.int32, (GROUP, GROUP), 1) >> 6
    return jnp.where(a == b, 1.0 / HEAD_DIM, 0.0).astype(BF16)


def head_mean(v, ones):
    high = v.astype(BF16)
    low = (v - high.astype(F32)).astype(BF16)
    return dot(high, ones) + dot(low, ones)


def one_head(block, h):
    lanes = lax.broadcasted_iota(jnp.int32, (1, GROUP), 1) >> 6
    return jnp.where(lanes == h, block, jnp.zeros_like(block))


def pack_state(full):
    left = lax.broadcasted_iota(jnp.int32, (HEAD_DIM, 128), 1) < HEAD_DIM
    pairs = []
    for p in range(2):
        block = full[128 * p : 128 * p + 128, 128 * p : 128 * p + 128]
        pairs.append(jnp.where(left, block[:HEAD_DIM], block[HEAD_DIM:]))
    return jnp.concatenate(pairs, axis=0)


def unpack_state(packed):
    left = lax.broadcasted_iota(jnp.int32, (HEAD_DIM, 128), 1) < HEAD_DIM
    none = jnp.zeros((128, 128), F32)
    rows = []
    for p in range(2):
        block = packed[HEAD_DIM * p : HEAD_DIM * p + HEAD_DIM]
        square = jnp.concatenate([jnp.where(left, block, 0.0), jnp.where(left, 0.0, block)], axis=0)
        rows.append(jnp.concatenate([square, none] if p == 0 else [none, square], axis=1))
    return jnp.concatenate(rows, axis=0).astype(BF16)


def full_spec(dims):
    return pl.BlockSpec(dims, lambda *_: (0,) * len(dims))


def column_spec(tokens, tile):
    return pl.BlockSpec((tokens, tile), lambda j, *_: (0, j))


def row_spec(tile, width):
    return pl.BlockSpec((tile, width), lambda i, *_: (i, 0))


SMEM = pl.BlockSpec(memory_space=pltpu.SMEM)


def project_keys(inputs, ids_col, last_ids, w_key, w_value, row_count):
    tokens, width = inputs.shape
    block = tokens // row_count

    def kernel(last_ref, x_ref, id_ref, wk_ref, wv_ref, xn_ref, k_ref, v_ref, s_ref):
        @pl.when(pl.program_id(0) == 0)
        def _():
            for i in range(tokens // TILE):
                x = x_ref[pl.ds(i * TILE, TILE), :].astype(F32)
                xn_ref[pl.ds(i * TILE, TILE), :] = (x * lax.rsqrt(mean_square(x) + EPSILON)).astype(BF16)

        xn = xn_ref[...]
        keys = softplus(dot(xn, wk_ref[...])).astype(BF16)
        values = dot(xn, wv_ref[...]).astype(BF16)
        k_ref[...] = keys
        v_ref[...] = values
        for r in range(row_count):
            at = slice(r * block, (r + 1) * block)
            kept = jnp.where(id_ref[at] == last_ref[r], keys[at], jnp.zeros((), BF16))
            s_ref[r] = pack_state(dot_tn(kept, values[at]))

    return call(
        kernel,
        (width // GROUP,),
        [SMEM, full_spec((tokens, width)), full_spec((tokens, 1)), column_spec(width, GROUP), column_spec(width, GROUP)],
        [
            full_spec((tokens, width)),
            column_spec(tokens, GROUP),
            column_spec(tokens, GROUP),
            pl.BlockSpec((row_count, GROUP // 2, 128), lambda j: (0, j, 0)),
        ],
        [shape((tokens, width), BF16)] * 3 + [shape((row_count, width // 2, 128), F32)],
        flops=4 * tokens * width * width,
        bytes_accessed=12 * tokens * width,
    )(last_ids, inputs, ids_col, w_key, w_value)


def block_mask(id_col, id_row, first, transposed):
    dims = (id_col.shape[0], id_row.shape[1])
    a = lax.broadcasted_iota(jnp.int32, dims, 0) + first
    b = lax.broadcasted_iota(jnp.int32, dims, 1)
    causal = b >= a if transposed else a >= b
    return jnp.where(causal & (id_col == id_row), 1.0, 0.0).astype(BF16)


def attend(normed, keys, values, ids_col, ids_row, w_query, w_outgate):
    tokens, width = normed.shape
    row_count, _, block = ids_row.shape

    def kernel(xn_ref, k_ref, v_ref, ic_ref, ir_ref, wq_ref, wg_ref, q_ref, g_ref, o_ref, mask_ref):
        @pl.when(pl.program_id(0) == 0)
        def _():
            for r in range(row_count):
                for i in range(block // TILE):
                    at = pl.ds(r * block + i * TILE, TILE)
                    mask_ref[at, :] = block_mask(ic_ref[at, :], ir_ref[r], i * TILE, False)

        xn = xn_ref[...]
        q_ref[...] = softplus(dot(xn, wq_ref[...])).astype(BF16)
        g_ref[...] = sigmoid(dot(xn, wg_ref[...])).astype(BF16)
        for r in range(row_count):
            base = r * block
            for i in range(block // TILE):
                rows = pl.ds(base + i * TILE, TILE)
                seen = (i + 1) * TILE
                q = q_ref[rows, :]
                mask = mask_ref[rows, pl.ds(0, seen)]
                total = None
                for h in range(4):
                    k = one_head(k_ref[pl.ds(base, seen), :], h)
                    v = one_head(v_ref[pl.ds(base, seen), :], h)
                    scores = dot_nt(q, k).astype(BF16) * mask
                    one = dot(scores, v)
                    total = one if total is None else total + one
                o_ref[rows, :] = total

    return call(
        kernel,
        (width // GROUP,),
        [
            full_spec((tokens, width)),
            column_spec(tokens, GROUP),
            column_spec(tokens, GROUP),
            full_spec((tokens, 1)),
            full_spec((row_count, 1, block)),
            column_spec(width, GROUP),
            column_spec(width, GROUP),
        ],
        [column_spec(tokens, GROUP)] * 3,
        [shape((tokens, width), BF16)] * 2 + [shape((tokens, width), F32)],
        scratch=[pltpu.VMEM((tokens, block), BF16)],
        flops=4 * tokens * width * width + 16 * tokens * block * width // 2,
        bytes_accessed=18 * tokens * width,
    )(normed, keys, values, ids_col, ids_row, w_query, w_outgate)


def combine(queries, inside, gates, inputs, carried, near_ids, ids_col, head_gain, w_output):
    tokens, width = queries.shape
    row_count = carried.shape[0]
    block = tokens // row_count
    per_row = block // TILE

    def kernel(near_ref, q_ref, in_ref, g_ref, x_ref, c_ref, id_ref, gain_ref, wo_ref, at_ref, go_ref, h_ref, nm_ref):
        near = near_ref[pl.program_id(0) // per_row]
        matched = id_ref[...] == near
        ones = head_ones()
        for j in range(width // GROUP):
            cols = pl.ds(j * GROUP, GROUP)
            state = unpack_state(c_ref[0, pl.ds(j * GROUP // 2, GROUP // 2), :])
            across = dot(q_ref[:, cols], state)
            attended = in_ref[:, cols] + jnp.where(matched, across, 0.0)
            at_ref[:, cols] = attended.astype(BF16)
            unit = attended * lax.rsqrt(head_mean(attended * attended, ones) + EPSILON)
            go_ref[:, cols] = (unit * gain_ref[:, cols] * g_ref[:, cols].astype(F32)).astype(BF16)
        hidden = x_ref[...].astype(F32) + dot(go_ref[...], wo_ref[...])
        h_ref[...] = hidden
        nm_ref[...] = (hidden * lax.rsqrt(mean_square(hidden) + EPSILON)).astype(BF16)

    tile = row_spec(TILE, width)
    return call(
        kernel,
        (tokens // TILE,),
        [
            SMEM,
            tile,
            tile,
            tile,
            tile,
            pl.BlockSpec((1, width // 2, 128), lambda i: (i // per_row, 0, 0)),
            row_spec(TILE, 1),
            full_spec((1, width)),
            full_spec((width, width)),
        ],
        [tile] * 4,
        [shape((tokens, width), BF16)] * 2 + [shape((tokens, width), F32), shape((tokens, width), BF16)],
        flops=2 * tokens * width * width,
        bytes_accessed=20 * tokens * width + 2 * width * width,
    )(near_ids, queries, inside, gates, inputs, carried, ids_col, head_gain, w_output)


def gate_up(normed, w_gate, w_up):
    tokens, width = normed.shape
    wide = w_gate.shape[1]

    def kernel(n_ref, wg_ref, wu_ref, g_ref, u_ref, p_ref):
        n = n_ref[...]
        gate = dot(n, wg_ref[...])
        up = dot(n, wu_ref[...])
        g_ref[...] = gate.astype(BF16)
        u_ref[...] = up.astype(BF16)
        p_ref[...] = (gate * up).astype(BF16)

    return call(
        kernel,
        (wide // TILE,),
        [full_spec((tokens, width)), column_spec(width, TILE), column_spec(width, TILE)],
        [column_spec(tokens, TILE)] * 3,
        [shape((tokens, wide), BF16)] * 3,
        flops=4 * tokens * width * wide,
        bytes_accessed=4 * width * wide + 6 * tokens * wide,
    )(normed, w_gate, w_up)


def back_gate_up(cotangent, w_down, gate, up, begin, end):
    tokens, width = cotangent.shape
    count = end - begin

    def kernel(c_ref, wd_ref, g_ref, u_ref, o_ref):
        back = dot_nt(c_ref[...], wd_ref[...])
        o_ref[:, pl.ds(0, TILE)] = (back * u_ref[...].astype(F32)).astype(BF16)
        o_ref[:, pl.ds(TILE, TILE)] = (back * g_ref[...].astype(F32)).astype(BF16)

    part = pl.BlockSpec((tokens, TILE), lambda j: (0, j + begin))
    return call(
        kernel,
        (count,),
        [full_spec((tokens, width)), pl.BlockSpec((TILE, width), lambda j: (j + begin, 0)), part, part],
        column_spec(tokens, 2 * TILE),
        shape((tokens, 2 * TILE * count), BF16),
        flops=2 * tokens * width * TILE * count,
        bytes_accessed=(8 * tokens + 2 * width) * TILE * count,
    )(cotangent, w_down, gate, up)


def block_output(hidden, product, w_down):
    tokens, width = hidden.shape
    wide = product.shape[1]

    def kernel(h_ref, p_ref, w_ref, o_ref):
        o_ref[...] = (h_ref[...] + dot(p_ref[...], w_ref[...])).astype(BF16)

    return call(
        kernel,
        (tokens // TILE,),
        [row_spec(TILE, width), row_spec(TILE, wide), full_spec((wide, width))],
        row_spec(TILE, width),
        shape((tokens, width), BF16),
        flops=2 * tokens * width * wide,
        bytes_accessed=6 * tokens * width + 2 * wide * (tokens + width),
    )(hidden, product, w_down)


def norm_back(unit, scale, grad):
    return scale * (grad - unit * jnp.mean(grad * unit, axis=-1, keepdims=True))


def back_mid_heads(
    backs, w_gate, w_up, cotangent, hidden, w_output, attended, gates, head_gain, queries, first_ids, ids_col, row_count
):
    tokens, width = cotangent.shape
    block = tokens // row_count
    per_row = block // TILE
    counts = [b.shape[1] // (2 * TILE) for b in backs]
    steps = sum(counts)
    begins = [sum(counts[:i]) for i in range(len(counts))]
    number = len(backs)

    def kernel(first_ref, *refs):
        b_refs = refs[:number]
        (wg_ref, wu_ref, c_ref, h_ref, wo_ref, at_ref, g_ref, gain_ref, q_ref, id_ref) = refs[number : number + 10]
        (bb_ref, bo_ref, ba_ref, gg_ref, s_ref, acc_ref) = refs[number + 10 :]
        step = pl.program_id(0)

        @pl.when(step == 0)
        def _():
            acc_ref[...] = jnp.zeros_like(acc_ref)

        for b_ref, begin, count in zip(b_refs, begins, counts):

            @pl.when((step >= begin) & (step < begin + count))
            def _(b_ref=b_ref):
                w = jnp.concatenate([wg_ref[...], wu_ref[...]], axis=1)
                acc_ref[...] += dot_nt(b_ref[...], w)

        @pl.when(step == steps - 1)
        def _():
            ones = head_ones()
            gains = [jnp.zeros((1, GROUP), F32)] * (width // GROUP)
            for r in range(row_count):
                sums = [None] * (width // GROUP)
                for i in range(per_row):
                    rows = pl.ds(r * block + i * TILE, TILE)
                    h = h_ref[rows, :]
                    scale = lax.rsqrt(mean_square(h) + EPSILON)
                    back = c_ref[rows, :].astype(F32) + norm_back(h * scale, scale, acc_ref[rows, :])
                    bb_ref[rows, :] = back.astype(BF16)
                    acc_ref[rows, :] = dot_nt(bb_ref[rows, :], wo_ref[...])
                    in_first = id_ref[rows, :] == first_ref[r]
                    for j in range(width // GROUP):
                        cols = pl.ds(j * GROUP, GROUP)
                        attended = at_ref[rows, cols].astype(F32)
                        scale_h = lax.rsqrt(head_mean(attended * attended, ones) + EPSILON)
                        unit = attended * scale_h
                        gate = g_ref[rows, cols].astype(F32)
                        gain = gain_ref[:, cols]
                        gated = acc_ref[rows, cols] * gate
                        along = unit * gated
                        gains[j] = gains[j] + jnp.sum(along, axis=0, keepdims=True)
                        bo_ref[rows, cols] = (along * gain * (1.0 - gate)).astype(BF16)
                        back_unit = gated * gain
                        mean = head_mean(back_unit * unit, ones)
                        ba = (scale_h * (back_unit - unit * mean)).astype(BF16)
                        ba_ref[rows, cols] = ba
                        q = jnp.where(in_first, q_ref[rows, cols], jnp.zeros((), BF16))
                        one = dot_tn(q, ba)
                        sums[j] = one if sums[j] is None else sums[j] + one
                for j in range(width // GROUP):
                    s_ref[r, pl.ds(j * GROUP // 2, GROUP // 2), :] = pack_state(sums[j])
            for j in range(width // GROUP):
                gg_ref[:, pl.ds(j * GROUP, GROUP)] = gains[j]

    def chunk_spec(begin, count):
        return pl.BlockSpec((tokens, 2 * TILE), lambda j: (0, jnp.clip(j - begin, 0, count - 1)))

    whole = full_spec((tokens, width))
    weights = column_spec(width, TILE)
    return call(
        kernel,
        (steps,),
        [SMEM]
        + [chunk_spec(b, c) for b, c in zip(begins, counts)]
        + [weights, weights, whole, whole, full_spec((width, width)), whole, whole, full_spec((1, width)), whole]
        + [full_spec((tokens, 1))],
        [whole] * 3 + [full_spec((1, width)), full_spec((row_count, width // 2, 128))],
        [shape((tokens, width), BF16)] * 3 + [shape((1, width), F32), shape((row_count, width // 2, 128), F32)],
        scratch=[pltpu.VMEM((tokens, width), F32)],
        flops=4 * tokens * width * TILE * steps + 2 * tokens * width * width,
        bytes_accessed=4 * (tokens + width) * TILE * steps + 24 * tokens * width,
    )(first_ids, *backs, w_gate, w_up, cotangent, hidden, w_output, attended, gates, head_gain, queries, ids_col)


def attend_back(queries, keys, values, back_attended, carried, near_ids, ids_col, ids_row):
    tokens, width = queries.shape
    row_count, _, block = ids_row.shape

    def kernel(near_ref, q_ref, k_ref, v_ref, a_ref, c_ref, ic_ref, ir_ref, bq_ref, bk_ref, bv_ref, mask_ref, flip_ref):
        @pl.when(pl.program_id(0) == 0)
        def _():
            for r in range(row_count):
                for i in range(block // TILE):
                    at = pl.ds(r * block + i * TILE, TILE)
                    mask_ref[at, :] = block_mask(ic_ref[at, :], ir_ref[r], i * TILE, False)
                    flip_ref[at, :] = block_mask(ic_ref[at, :], ir_ref[r], i * TILE, True)

        for r in range(row_count):
            base = r * block
            state = unpack_state(c_ref[r])
            for i in range(block // TILE):
                rows = pl.ds(base + i * TILE, TILE)
                seen = (i + 1) * TILE
                earlier = pl.ds(base, seen)
                later = pl.ds(base + i * TILE, block - i * TILE)
                a = a_ref[rows, :]
                q = q_ref[rows, :]
                k = k_ref[rows, :]
                v = v_ref[rows, :]
                matched = ic_ref[rows, :] == near_ref[r]
                back_q = jnp.where(matched, dot_nt(a, state), 0.0)
                back_k = None
                back_v = None
                mask = mask_ref[rows, pl.ds(0, seen)]
                flip = flip_ref[rows, pl.ds(i * TILE, block - i * TILE)]
                for h in range(4):
                    grads = dot_nt(a, one_head(v_ref[earlier, :], h)).astype(BF16) * mask
                    back_q = back_q + dot(grads, one_head(k_ref[earlier, :], h))
                    q_h = one_head(q_ref[later, :], h)
                    a_h = one_head(a_ref[later, :], h)
                    scores_t = dot_nt(k, q_h).astype(BF16) * flip
                    grads_t = dot_nt(v, a_h).astype(BF16) * flip
                    one = dot(grads_t, q_h)
                    back_k = one if back_k is None else back_k + one
                    one = dot(scores_t, a_h)
                    back_v = one if back_v is None else back_v + one
                bq_ref[rows, :] = (back_q * sigmoid_of_softplus(q.astype(F32))).astype(BF16)
                bk_ref[rows, :] = back_k
                bv_ref[rows, :] = back_v

    tile = column_spec(tokens, GROUP)
    return call(
        kernel,
        (width // GROUP,),
        [SMEM, tile, tile, tile, tile, pl.BlockSpec((row_count, GROUP // 2, 128), lambda j: (0, j, 0))]
        + [full_spec((tokens, 1)), full_spec((row_count, 1, block))],
        [tile] * 3,
        [shape((tokens, width), BF16)] + [shape((tokens, width), F32)] * 2,
        scratch=[pltpu.VMEM((tokens, block), BF16)] * 2,
        flops=48 * tokens * block * width // 2,
        bytes_accessed=18 * tokens * width,
    )(near_ids, queries, keys, values, back_attended, carried, ids_col, ids_row)


def finish_keys(back_k, back_v, keys, values, state_grad, near_ids, ids_col):
    tokens, width = keys.shape
    row_count = state_grad.shape[0]
    block = tokens // row_count

    def kernel(near_ref, bk_ref, bv_ref, k_ref, v_ref, s_ref, id_ref, ok_ref, ov_ref):
        for r in range(row_count):
            rows = pl.ds(r * block, block)
            state = unpack_state(s_ref[r])
            uses = id_ref[rows, :] == near_ref[r]
            k = k_ref[rows, :]
            back_k = bk_ref[rows, :] + jnp.where(uses, dot_nt(v_ref[rows, :], state), 0.0)
            ok_ref[rows, :] = (back_k * sigmoid_of_softplus(k.astype(F32))).astype(BF16)
            ov_ref[rows, :] = (bv_ref[rows, :] + jnp.where(uses, dot(k, state), 0.0)).astype(BF16)

    tile = column_spec(tokens, GROUP)
    return call(
        kernel,
        (width // GROUP,),
        [SMEM, tile, tile, tile, tile, pl.BlockSpec((row_count, GROUP // 2, 128), lambda j: (0, j, 0))]
        + [full_spec((tokens, 1))],
        [tile] * 2,
        [shape((tokens, width), BF16)] * 2,
        flops=4 * tokens * GROUP * width,
        bytes_accessed=16 * tokens * width,
    )(near_ids, back_k, back_v, keys, values, state_grad, ids_col)


def input_gradient(grads, weights, inputs, back_branch):
    tokens, width = inputs.shape

    def kernel(a_ref, b_ref, c_ref, d_ref, wa_ref, wb_ref, wc_ref, wd_ref, x_ref, bb_ref, o_ref):
        back = dot_nt(a_ref[...], wa_ref[...]) + dot_nt(b_ref[...], wb_ref[...])
        back = back + dot_nt(c_ref[...], wc_ref[...]) + dot_nt(d_ref[...], wd_ref[...])
        x = x_ref[...].astype(F32)
        scale = lax.rsqrt(mean_square(x) + EPSILON)
        o_ref[...] = (bb_ref[...].astype(F32) + norm_back(x * scale, scale, back)).astype(BF16)

    tile = row_spec(TILE, width)
    return call(
        kernel,
        (tokens // TILE,),
        [tile] * 4 + [full_spec((width, width))] * 4 + [tile] * 2,
        tile,
        shape((tokens, width), BF16),
        flops=8 * tokens * width * width,
        bytes_accessed=14 * tokens * width + 8 * width * width,
    )(*grads, *weights, inputs, back_branch)


def local(
    inputs,
    doc_ids,
    w_query,
    w_key,
    w_value,
    w_outgate,
    w_output,
    w_gate,
    w_up,
    w_down,
    head_gain,
    cotangent,
):
    row_count, block_len, width = inputs.shape
    tokens = row_count * block_len
    x_first, y_first, z_first = orders(lax.axis_size("seq"))
    core = lax.axis_index("batch").astype(jnp.int32).reshape(1)
    x_flat = inputs.reshape(tokens, width)
    cot_flat = cotangent.reshape(tokens, width)
    gain = head_gain.reshape(1, width)
    ids = doc_ids.astype(F32)
    ids_col = ids.reshape(tokens, 1)
    ids_row = ids.reshape(row_count, 1, block_len)
    first_ids, last_ids = ids[:, 0], ids[:, -1]
    edge_ids = gather_ids(jnp.concatenate([first_ids, last_ids]))
    before_total, before_results, before_ids = prefix_plan(edge_ids[:, row_count:], False)
    after_total, after_results, after_ids = prefix_plan(edge_ids[:, :row_count], True)

    def half_sum(acts, grads):
        received = to_core(grad_half(acts, grads, 1 - core))
        return grad_half(acts, grads, core, received)

    normed, keys, values, state = project_keys(x_flat, ids_col, last_ids, w_key, w_value, row_count)
    carried = prefix(state, before_total, before_results, False)
    queries, gates, inside = attend(normed, keys, values, ids_col, ids_row, w_query, w_outgate)
    attended, gated, hidden, normed_mid = combine(
        queries, inside, gates, x_flat, carried, before_ids, ids_col, gain, w_output
    )
    gate, up, product = gate_up(normed_mid, w_gate, w_up)

    half_down = half_sum(product, cot_flat)
    grad_down = jnp.concatenate(
        [
            scatter_seq([half_down], x_first, (0, width // 2)),
            scatter_seq([half_down], y_first, (width // 2, width)),
        ],
        axis=1,
    )

    tiles = w_gate.shape[1] // TILE
    cuts = [0, tiles // 2, tiles]
    backs = [back_gate_up(cot_flat, w_down, gate, up, a, b) for a, b in zip(cuts[:-1], cuts[1:])]
    wide_parts = []
    for back, order in zip(backs, (z_first, None)):
        half = half_sum(normed_mid, back)
        n = half.shape[1]
        if order is not None:
            done = scatter_seq([half], order)
        else:
            middle = n // 2
            done = jnp.concatenate(
                [scatter_seq([half], x_first, (0, middle)), scatter_seq([half], y_first, (middle, n))], axis=1
            )
        wide_parts.append(done.reshape(done.shape[0], n // (2 * TILE), 2, TILE))
    wide = jnp.concatenate(wide_parts, axis=1)
    grad_gate = wide[:, :, 0].reshape(wide.shape[0], tiles * TILE)
    grad_up = wide[:, :, 1].reshape(wide.shape[0], tiles * TILE)

    back_branch, back_outgate, back_attended, gain_terms, state_out = back_mid_heads(
        backs, w_gate, w_up, cot_flat, hidden, w_output, attended, gates, gain, queries, first_ids, ids_col, row_count
    )
    state_grad = prefix(state_out, after_total, after_results, True)
    grad_output = scatter_seq([half_sum(gated, back_branch)], x_first)
    grad_outgate = scatter_seq([half_sum(normed, back_outgate)], y_first)
    back_query, part_key, part_value = attend_back(
        queries, keys, values, back_attended, carried, before_ids, ids_col, ids_row
    )
    grad_query = scatter_seq([half_sum(normed, back_query)], x_first)
    back_key, back_value = finish_keys(part_key, part_value, keys, values, state_grad, after_ids, ids_col)
    grad_key = scatter_seq([half_sum(normed, back_key)], y_first)
    grad_value = scatter_seq([half_sum(normed, back_value)], x_first)

    gain_halves = gain_terms.reshape(2, width // 2)
    gain_sent = to_core(lax.dynamic_index_in_dim(gain_halves, 1 - core[0], 0, False))
    gain_kept = lax.dynamic_index_in_dim(gain_halves, core[0], 0, False) + gain_sent
    grad_gain = scatter_seq([gain_kept], x_first)

    block_out = block_output(hidden, product, w_down).reshape(inputs.shape)
    input_grad = input_gradient(
        (back_query, back_key, back_value, back_outgate), (w_query, w_key, w_value, w_outgate), x_flat, back_branch
    ).reshape(inputs.shape)
    return (
        block_out,
        input_grad,
        grad_query,
        grad_key,
        grad_value,
        grad_outgate,
        grad_output,
        grad_gate,
        grad_up,
        grad_down,
        grad_gain,
    )


def solution(mesh):
    rows = P("batch", "seq", None)
    scattered = P(("batch", "seq"), None)
    return jax.shard_map(
        local,
        mesh=mesh,
        in_specs=(rows, P("batch", "seq")) + (P(),) * 9 + (rows,),
        out_specs=(rows, rows) + (scattered,) * 8 + (P(("batch", "seq")),),
        check_vma=False,
    )
```

time: 2100 us -> 673 us (0.32)
  waiting for transfers between devices: 1550 us -> 191 us
  Pallas kernels: 0 us -> 291 us
  matrix products: 261 us -> 0 us
  starting transfers between devices: 1.42 us -> 90.8 us
  blocking collectives: 83.6 us -> 0 us
  local copies, waits for them, and re-layouts: 118 us -> 37.3 us
    reduce_scatter x8 -> x0, waiting for transfers between devices: 1350 us -> none  [the longest x1 253 us: local(): lax.psum_scatter(grad_up, ('batch', 'seq'), scatter_dimension=0, tiled=True)]
    pallas_call x0 -> x35, Pallas kernels: none -> 291 us  [the longest x16 95.3 us: grad_half(): call(kernel, (cols // tile,), [pl.BlockSpec((tokens, wide), lambda j, s:...]
    dot_general x36 -> x0, matrix products: 261 us -> none  [the longest x8 60.7 us: project(): return jnp.dot(activations, weight, preferred_element_type=jnp.float32)]
    all_gather x2 -> x0, waiting for transfers between devices: 197 us -> none  [prefix(): gathered = jax.tree.map(lambda a: lax.all_gather(a, axis), part)]
    ppermute x0 -> x75, waiting for transfers between devices: none -> 191 us  [the longest x44 168 us: scatter_seq(): lax.ppermute(outgoing, 'seq', [(i, i ^ flip) for i in range(count)])]
    ppermute x0 -> x75, starting transfers between devices: none -> 90.8 us  [the longest x44 53 us: scatter_seq(): lax.ppermute(outgoing, 'seq', [(i, i ^ flip) for i in range(count)])]
    unnamed x2 -> x0, blocking collectives: 83.6 us -> none
    reshape x12 -> x15, local copies, waits for them, and re-layouts: 82.4 us -> 20.8 us  [the longest x10 19.6 us: piece(): return taken.reshape((2,) * left + tuple(sizes[held:]))]
  transfers between devices with their start and end apart: 10 -> 75, of which waited for: 10 -> 29; matrix products, arithmetic and copies ran while one was open for 12% -> 11% of each run, Pallas kernels for 0% -> 30%
where the time goes in v2:
time: 673 us; the launch traced here: 663 us
  Pallas kernels  291 us (43%)
  waiting for transfers between devices  191 us (28%)
  starting transfers between devices  90.8 us (13%)
  other arithmetic  51 us (8%)
  local copies, waits for them, and re-layouts  37.3 us (6%)
    ppermute x44, waiting for transfers between devices, scatter_seq(): lax.ppermute(outgoing, 'seq', [(i, i ^ flip) for i in range(count)])  168 us
    pallas_call x16, Pallas kernels, grad_half(): call(kernel, (cols // tile,), [pl.BlockSpec((tokens, wide), lambda j, s:...  95.3 us
    ppermute x44, starting transfers between devices, scatter_seq(): lax.ppermute(outgoing, 'seq', [(i, i ^ flip) for i in range(count)])  53 us
    add x38, other arithmetic, sum_pieces(): total = one if total is None else total + one  45.6 us
    pallas_call x1, Pallas kernels, back_mid_heads(): call(kernel, (steps,), [SMEM] + [chunk_spec(b, c) for b, c in zip(begins,...  33.8 us
    pallas_call x1, Pallas kernels, attend_back(): call(kernel, (width // GROUP,), [SMEM, tile, tile, tile, tile, pl.BlockSp...  29.3 us
    pallas_call x2, Pallas kernels, back_gate_up(): call(kernel, (count,), [full_spec((tokens, width)), pl.BlockSpec((TILE, w...  20 us
    pallas_call x1, Pallas kernels, gate_up(): call(kernel, (wide // TILE,), [full_spec((tokens, width)), column_spec(wi...  19.8 us
  transfers between devices with their start and end apart: 75, of which 29 were waited for; matrix products, arithmetic and copies ran while one was open for 11% of the time, Pallas kernels for 30%

profile of v2, /device:TPU:0, one launch (start us, length us, event | category | flops | bytes accessed | tf_op | source)
XLA Modules:
  0.0 663.1 jit_solution(10402462258429562425)
XLA Ops:
  1.6 2.9 collective-permute-start
  5.6 11.3 %shard_map.203 = (bf16[1024,1024]{1,0:T(8,128)(2,1)}, bf16[1024,1024]{1,0:T(8,128)(2,1)}, bf16[1024,1024]{1,0:T(8,128)(2,1)}, f32[2,512,128]{2,1,0:T(8,128)}) custom-call(f32[2]{0:T(128)} %copy-done.39, bf16[1024,1024]{1,0:T(8,128)(2,1)} %bitcast.557, f32[1024,1]{1,0:T(8,128)} %bitcast.551, bf16[1024,1024]{1,0:T(8,128)(2,1)} %wb_ref.1, bf16[1024,1024]{1,0:T(8,128)(2,1)} %wc_ref.1), custom_call_target="tpu_custom_call" | custom-call | flops 4294967296 | bytes 12582912 | tf_op jit(solution)/shard_map/pallas_call | solution.py:360
  22.9 18.5 %shard_map.204 = (bf16[1024,1024]{1,0:T(8,128)(2,1)}, bf16[1024,1024]{1,0:T(8,128)(2,1)}, f32[1024,1024]{1,0:T(8,128)}) custom-call(bf16[1024,1024]{1,0:T(8,128)(2,1)} %get-tuple-element.51.xn_ref.a_ref, bf16[1024,1024]{1,0:T(8,128)(2,1)} %get-tuple-element.52.k_ref, bf16[1024,1024]{1,0:T(8,128)(2,1)} %get-tuple-element.53.v_ref, f32[1024,1]{1,0:T(8,128)} %bitcast.552, ...), custom_call_target="tpu_custom_call" | custom-call | flops 8589934592 | bytes 18874368 | tf_op jit(solution)/shard_map/pallas_call | solution.py:415
  58.8 5.5 collective-permute-start.9
  84.5 12.0 %shard_map.209 = (bf16[1024,1024]{1,0:T(8,128)(2,1)}, bf16[1024,1024]{1,0:T(8,128)(2,1)}, f32[1024,1024]{1,0:T(8,128)}, bf16[1024,1024]{1,0:T(8,128)(2,1)}) custom-call(f32[2]{0:T(128)} %fusion.11.near_ref, bf16[1024,1024]{1,0:T(8,128)(2,1)} %get-tuple-element.54.q_ref.refs_10_, f32[1024,1024]{1,0:T(8,128)} %get-tuple-element.55.in_ref, ...), custom_call_target="tpu_custom_call" | custom-call | flops 2147483648 | bytes 23068672 | tf_op jit(solution)/shard_map/pallas_call | solution.py:458
  96.6 19.8 %shard_map.210 = (bf16[1024,2816]{1,0:T(8,128)(2,1)}, bf16[1024,2816]{1,0:T(8,128)(2,1)}, bf16[1024,2816]{1,0:T(8,128)(2,1)}) custom-call(bf16[1024,1024]{1,0:T(8,128)(2,1)} %get-tuple-element.67.n_ref.a_ref, bf16[1024,2816]{1,0:T(8,128)(2,1)} %refs_2_.1, bf16[1024,2816]{1,0:T(8,128)(2,1)} %refs_3_.1), custom_call_target="tpu_custom_call" | custom-call | flops 11811160064 | bytes 28835840 | tf_op jit(solution)/shard_map/pallas_call | solution.py:491
  116.4 9.7 %shard_map.212.refs_0_.g_ref = bf16[1024,2560]{1,0:T(8,128)(2,1)} custom-call(bf16[1024,1024]{1,0:T(8,128)(2,1)} %bitcast.500, bf16[2816,1024]{1,0:T(8,128)(2,1)} %wd_ref.4, bf16[1024,2816]{1,0:T(8,128)(2,1)} %get-tuple-element.69.g_ref, bf16[1024,2816]{1,0:T(8,128)(2,1)} %get-tuple-element.70.u_ref), custom_call_target="tpu_custom_call" | custom-call | flops 2684354560 | bytes 13107200 | tf_op jit(solution)/shard_map/pallas_call | solution.py:512
  126.1 10.3 %shard_map.213.refs_1_.g_ref = bf16[1024,3072]{1,0:T(8,128)(2,1)} custom-call(bf16[1024,1024]{1,0:T(8,128)(2,1)} %bitcast.501, bf16[2816,1024]{1,0:T(8,128)(2,1)} %wd_ref.4, bf16[1024,2816]{1,0:T(8,128)(2,1)} %get-tuple-element.69.g_ref, bf16[1024,2816]{1,0:T(8,128)(2,1)} %get-tuple-element.70.u_ref), custom_call_target="tpu_custom_call" | custom-call | flops 3221225472 | bytes 15728640 | tf_op jit(solution)/shard_map/pallas_call | solution.py:512
  136.3 33.8 %shard_map.214 = (bf16[1024,1024]{1,0:T(8,128)(2,1)}, bf16[1024,1024]{1,0:T(8,128)(2,1)}, bf16[1024,1024]{1,0:T(8,128)(2,1)}, f32[1,1024]{1,0:T(1,128)}, f32[2,512,128]{2,1,0:T(8,128)}) custom-call(f32[2]{0:T(128)} %copy-done.38, bf16[1024,2560]{1,0:T(8,128)(2,1)} %shard_map.212.refs_0_.g_ref, bf16[1024,3072]{1,0:T(8,128)(2,1)} %shard_map.213.refs_1_.g_ref, ...), custom_call_target="tpu_custom_call" | custom-call | flops 13958643712 | bytes 48234496 | tf_op jit(solution)/shard_map/pallas_call | solution.py:615
  177.4 4.0 shard_map.230
  181.5 29.3 %shard_map.215 = (bf16[1024,1024]{1,0:T(8,128)(2,1)}, f32[1024,1024]{1,0:T(8,128)}, f32[1024,1024]{1,0:T(8,128)}) custom-call(f32[2]{0:T(128)} %fusion.11.near_ref, bf16[1024,1024]{1,0:T(8,128)(2,1)} %get-tuple-element.54.q_ref.refs_10_, bf16[1024,1024]{1,0:T(8,128)(2,1)} %get-tuple-element.52.k_ref, bf16[1024,1024]{1,0:T(8,128)(2,1)} %get-tuple-element.53.v_ref, ...), custom_call_target="tpu_custom_call" | custom-call | flops 12884901888 | bytes 18874368 | tf_op jit(solution)/shard_map/pallas_call | solution.py:677
  210.8 4.0 shard_map.228
  219.2 4.1 shard_map.222
  228.7 6.6 collective-permute-done.17.refs_5_
  240.9 3.1 collective-permute-done.72
  246.0 5.2 collective-permute-done.20.refs_2_
  253.9 8.7 %shard_map.220 = (bf16[1024,1024]{1,0:T(8,128)(2,1)}, bf16[1024,1024]{1,0:T(8,128)(2,1)}) custom-call(f32[2]{0:T(128)} %fusion.13.near_ref, f32[1024,1024]{1,0:T(8,128)} %get-tuple-element.74.bk_ref, f32[1024,1024]{1,0:T(8,128)} %get-tuple-element.75.bv_ref, bf16[1024,1024]{1,0:T(8,128)(2,1)} %get-tuple-element.52.k_ref, ...), custom_call_target="tpu_custom_call" | custom-call | flops 1073741824 | bytes 16777216 | tf_op jit(solution)/shard_map/pallas_call | solution.py:706
  262.6 4.1 shard_map.226
  270.5 4.0 shard_map.224
  274.8 8.1 %shard_map.232 = f32[512,2560]{1,0:T(8,128)} custom-call(s32[1]{0:T(128)S(6)} %sub.42.half_ref, bf16[1024,1024]{1,0:T(8,128)(2,1)} %get-tuple-element.67.n_ref.a_ref, bf16[1024,2560]{1,0:T(8,128)(2,1)} %shard_map.212.refs_0_.g_ref), custom_call_target="tpu_custom_call" | custom-call | flops 2684354560 | bytes 11534336 | tf_op jit(solution)/shard_map/pallas_call | solution.py:124
  282.9 7.2 %shard_map.236 = f32[1408,1024]{1,0:T(8,128)} custom-call(s32[1]{0:T(128)S(6)} %sub.42.half_ref, bf16[1024,2816]{1,0:T(8,128)(2,1)} %get-tuple-element.68.p_ref.a_ref, bf16[1024,1024]{1,0:T(8,128)(2,1)} %bitcast.503), custom_call_target="tpu_custom_call" | custom-call | flops 2952790016 | bytes 10747904 | tf_op jit(solution)/shard_map/pallas_call | solution.py:124
  290.7 9.0 %shard_map.234 = f32[512,3072]{1,0:T(8,128)} custom-call(s32[1]{0:T(128)S(6)} %sub.42.half_ref, bf16[1024,1024]{1,0:T(8,128)(2,1)} %get-tuple-element.67.n_ref.a_ref, bf16[1024,3072]{1,0:T(8,128)(2,1)} %shard_map.213.refs_1_.g_ref), custom_call_target="tpu_custom_call" | custom-call | flops 3221225472 | bytes 13631488 | tf_op jit(solution)/shard_map/pallas_call | solution.py:124
  300.3 4.4 shard_map.231
  307.4 4.4 shard_map.229
  313.7 4.6 shard_map.223
  319.6 11.6 %collective-permute-done.43 = f32[2,2,2,32,1024]{4,3,2,1,0:T(8,128)S(1)} collective-permute-done((f32[2,2,2,32,1024]{4,3,2,1,0:T(8,128)S(1)}, f32[2,2,2,32,1024]{4,3,2,1,0:T(8,128)S(1)}, u32[]{:S(2)}, u32[]{:S(2)}) %collective-permute-start.43) | collective-permute-done | bytes 1048608 | tf_op jit(solution)/shard_map/ppermute | solution.py:67
  332.5 4.4 shard_map.227
  339.0 4.4 shard_map.225
  344.7 12.6 %collective-permute-done.23 = f32[2,2,2,32,1024]{4,3,2,1,0:T(8,128)S(1)} collective-permute-done((f32[2,2,2,32,1024]{4,3,2,1,0:T(8,128)S(1)}, f32[2,2,2,32,1024]{4,3,2,1,0:T(8,128)S(1)}, u32[]{:S(2)}, u32[]{:S(2)}) %collective-permute-start.23) | collective-permute-done | bytes 1048608 | tf_op jit(solution)/shard_map/ppermute | solution.py:67
  360.8 17.3 %collective-permute-done.33 = f32[2,2,2,32,1024]{4,3,2,1,0:T(8,128)} collective-permute-done((f32[2,2,2,32,1024]{4,3,2,1,0:T(8,128)S(1)}, f32[2,2,2,32,1024]{4,3,2,1,0:T(8,128)}, u32[]{:S(2)}, u32[]{:S(2)}) %collective-permute-start.33) | collective-permute-done | bytes 1048608 | tf_op jit(solution)/shard_map/ppermute | solution.py:67
  379.2 11.1 %shard_map.211 = bf16[1024,1024]{1,0:T(8,128)(2,1)} custom-call(f32[1024,1024]{1,0:T(8,128)} %get-tuple-element.66.h_ref.refs_5_, bf16[1024,2816]{1,0:T(8,128)(2,1)} %get-tuple-element.68.p_ref.a_ref, bf16[2816,1024]{1,0:T(8,128)(2,1)} %wd_ref.4), custom_call_target="tpu_custom_call" | custom-call | flops 5905580032 | bytes 17825792 | tf_op jit(solution)/shard_map/pallas_call | solution.py:530
  397.8 5.6 collective-permute-done.39
  417.9 9.8 %shard_map.233 = f32[512,2560]{1,0:T(8,128)} custom-call(s32[1]{0:T(128)} %bitcast.15.half_ref, bf16[1024,1024]{1,0:T(8,128)(2,1)} %get-tuple-element.67.n_ref.a_ref, bf16[1024,2560]{1,0:T(8,128)(2,1)} %shard_map.212.refs_0_.g_ref, f32[512,2560]{1,0:T(8,128)} %collective-permute-done.47.rest_0_), custom_call_target="tpu_custom_call" | custom-call | flops 2684354560 | bytes 16777216 | tf_op jit(solution)/shard_map/pallas_call | solution.py:124
  427.7 3.4 dynamic-slice_bitcast_fusion
  433.6 8.3 %shard_map.237 = f32[1408,1024]{1,0:T(8,128)} custom-call(s32[1]{0:T(128)} %bitcast.15.half_ref, bf16[1024,2816]{1,0:T(8,128)(2,1)} %get-tuple-element.68.p_ref.a_ref, bf16[1024,1024]{1,0:T(8,128)(2,1)} %bitcast.504, f32[1408,1024]{1,0:T(8,128)} %collective-permute-done.61.rest_0_), custom_call_target="tpu_custom_call" | custom-call | flops 2952790016 | bytes 16515072 | tf_op jit(solution)/shard_map/pallas_call | solution.py:124
  448.5 10.5 %shard_map.235 = f32[512,3072]{1,0:T(8,128)} custom-call(s32[1]{0:T(128)} %bitcast.15.half_ref, bf16[1024,1024]{1,0:T(8,128)(2,1)} %get-tuple-element.67.n_ref.a_ref, bf16[1024,3072]{1,0:T(8,128)(2,1)} %shard_map.213.refs_1_.g_ref, f32[512,3072]{1,0:T(8,128)} %collective-permute-done.52.rest_0_), custom_call_target="tpu_custom_call" | custom-call | flops 3221225472 | bytes 19922944 | tf_op jit(solution)/shard_map/pallas_call | solution.py:124
  468.3 16.0 %shard_map.221 = bf16[1024,1024]{1,0:T(8,128)(2,1)} custom-call(bf16[1024,1024]{1,0:T(8,128)(2,1)} %get-tuple-element.73.a_ref.g_ref, bf16[1024,1024]{1,0:T(8,128)(2,1)} %get-tuple-element.85.b_ref.g_ref, bf16[1024,1024]{1,0:T(8,128)(2,1)} %get-tuple-element.86.c_ref.g_ref, bf16[1024,1024]{1,0:T(8,128)(2,1)} %get-tuple-element.87.d_ref.g_ref, ...), custom_call_target="tpu_custom_call" | custom-call | flops 8589934592 | bytes 23068672 | tf_op jit(solution)/shard_map/pallas_call | solution.py:729
  491.1 6.5 collective-permute-done.66
  502.2 21.7 %collective-permute-done.26 = f32[32,1024]{1,0:T(8,128)S(1)} collective-permute-done((f32[32,1024]{1,0:T(8,128)S(1)}, f32[32,1024]{1,0:T(8,128)S(1)}, u32[]{:S(2)}, u32[]{:S(2)}) %collective-permute-start.26) | collective-permute-done | bytes 131104 | tf_op jit(solution)/shard_map/ppermute | solution.py:67
  531.1 3.0 collective-permute-start.30
  535.8 6.0 collective-permute-done.63
  555.1 3.9 collective-permute-done.64
  560.1 3.6 collective-permute-start.65
  565.0 47.7 %collective-permute-done.31 = f32[32,1024]{1,0:T(8,128)S(1)} collective-permute-done((f32[32,1024]{1,0:T(8,128)S(1)}, f32[32,1024]{1,0:T(8,128)S(1)}, u32[]{:S(2)}, u32[]{:S(2)}) %collective-permute-start.31) | collective-permute-done | bytes 131104 | tf_op jit(solution)/shard_map/ppermute | solution.py:67
  616.1 5.9 collective-permute-start.59
  625.4 9.8 %collective-permute-done.59 = f32[2,32,1536]{2,1,0:T(8,128)S(1)} collective-permute-done((f32[2,32,1536]{2,1,0:T(8,128)S(1)}, f32[2,32,1536]{2,1,0:T(8,128)S(1)}, u32[]{:S(2)}, u32[]{:S(2)}) %collective-permute-start.59) | collective-permute-done | bytes 393248 | tf_op jit(solution)/shard_map/ppermute | solution.py:67
  640.7 6.6 collective-permute-done.60
  651.2 6.2 collective-permute-done.51
  (346 shorter events, 190.8 us)
Async XLA Ops:
  1.6 39.7 %collective-permute-start = (f32[1,4]{1,0:T(1,128)S(1)}, f32[1,4]{1,0:T(1,128)S(1)}, u32[]{:S(2)}, u32[]{:S(2)}) collective-permute-start(f32[1,4]{1,0:T(1,128)S(1)} %maximum_bitcast_fusion), channel_id=1, source_target_pairs={{0,1},{1,0},{2,3},{3,2},{4,5},{5,4},{6,7},{7,6},{8,9},{9,8},{10,11... | collective-permute-start | bytes 56 | tf_op jit(solution)/shard_map/ppermute | solution.py:147
  18.8 37.5 %collective-permute-start.4 = (f32[2,128,128]{2,1,0:T(8,128)}, f32[2,128,128]{2,1,0:T(8,128)S(1)}, u32[]{:S(2)}, u32[]{:S(2)}) collective-permute-start(f32[2,128,128]{2,1,0:T(8,128)} %get-tuple-element.59), channel_id=1, source_target_pairs={{0,1},{1,0},{2,3},{3,2},{4,5},{5,4},{6,7},{7,6},{8,9},{9,8},{10,11... | collective-permute-start | bytes 393224 | tf_op jit(solution)/shard_map/ppermute | solution.py:255
  18.8 37.5 %collective-permute-start.5 = (f32[2,128,128]{2,1,0:T(8,128)}, f32[2,128,128]{2,1,0:T(8,128)S(1)}, u32[]{:S(2)}, u32[]{:S(2)}) collective-permute-start(f32[2,128,128]{2,1,0:T(8,128)} %get-tuple-element.60), channel_id=1, source_target_pairs={{0,2},{1,3},{2,0},{3,1},{4,6},{5,7},{6,4},{7,5},{8,10},{9,11},{10,... | collective-permute-start | bytes 393224 | tf_op jit(solution)/shard_map/ppermute | solution.py:255
  20.8 35.5 %collective-permute-start.6 = (f32[2,128,128]{2,1,0:T(8,128)}, f32[2,128,128]{2,1,0:T(8,128)S(1)}, u32[]{:S(2)}, u32[]{:S(2)}) collective-permute-start(f32[2,128,128]{2,1,0:T(8,128)} %get-tuple-element.61), channel_id=1, source_target_pairs={{0,3},{1,2},{2,1},{3,0},{4,7},{5,6},{6,5},{7,4},{8,11},{9,10},{10,... | collective-permute-start | bytes 393224 | tf_op jit(solution)/shard_map/ppermute | solution.py:255
  172.0 51.3 %collective-permute-start.70 = (f32[512]{0:T(512)S(1)}, f32[512]{0:T(512)S(1)}, u32[]{:S(2)}, u32[]{:S(2)}) collective-permute-start(f32[512]{0:T(512)S(1)} %bitcast.582), channel_id=1, source_target_pairs={{0,16},{16,0},{1,17},{17,1},{2,18},{18,2},{3,19},{19,3},{4,20},{20... | collective-permute-start | bytes 6152 | tf_op jit(solution)/shard_map/ppermute | solution.py:74
  174.0 40.9 %collective-permute-start.13 = (f32[2,128,128]{2,1,0:T(8,128)}, f32[2,128,128]{2,1,0:T(8,128)S(1)}, u32[]{:S(2)}, u32[]{:S(2)}) collective-permute-start(f32[2,128,128]{2,1,0:T(8,128)} %get-tuple-element.78), channel_id=1, source_target_pairs={{0,1},{1,0},{2,3},{3,2},{4,5},{5,4},{6,7},{7,6},{8,9},{9,8},{10,11... | collective-permute-start | bytes 393224 | tf_op jit(solution)/shard_map/ppermute | solution.py:255
  175.4 39.9 %collective-permute-start.14 = (f32[2,128,128]{2,1,0:T(8,128)}, f32[2,128,128]{2,1,0:T(8,128)S(1)}, u32[]{:S(2)}, u32[]{:S(2)}) collective-permute-start(f32[2,128,128]{2,1,0:T(8,128)} %get-tuple-element.79), channel_id=1, source_target_pairs={{0,2},{1,3},{2,0},{3,1},{4,6},{5,7},{6,4},{7,5},{8,10},{9,11},{10,... | collective-permute-start | bytes 393224 | tf_op jit(solution)/shard_map/ppermute | solution.py:255
  176.0 39.4 %collective-permute-start.15 = (f32[2,128,128]{2,1,0:T(8,128)}, f32[2,128,128]{2,1,0:T(8,128)S(1)}, u32[]{:S(2)}, u32[]{:S(2)}) collective-permute-start(f32[2,128,128]{2,1,0:T(8,128)} %get-tuple-element.80), channel_id=1, source_target_pairs={{0,3},{1,2},{2,1},{3,0},{4,7},{5,6},{6,5},{7,4},{8,11},{9,10},{10,... | collective-permute-start | bytes 393224 | tf_op jit(solution)/shard_map/ppermute | solution.py:255
  181.5 108.6 %collective-permute-start.42 = (f32[512,1024]{1,0:T(8,128)}, f32[512,1024]{1,0:T(8,128)S(1)}, u32[]{:S(2)}, u32[]{:S(2)}) collective-permute-start(f32[512,1024]{1,0:T(8,128)} %shard_map.230), channel_id=1, source_target_pairs={{0,16},{16,0},{1,17},{17,1},{2,18},{18,2},{3,19},{19,3},{4,20},{20... | collective-permute-start | bytes 6291464 | tf_op jit(solution)/shard_map/ppermute | solution.py:74
  214.9 75.7 %collective-permute-start.37 = (f32[512,1024]{1,0:T(8,128)}, f32[512,1024]{1,0:T(8,128)}, u32[]{:S(2)}, u32[]{:S(2)}) collective-permute-start(f32[512,1024]{1,0:T(8,128)} %shard_map.228), channel_id=1, source_target_pairs={{0,16},{16,0},{1,17},{17,1},{2,18},{18,2},{3,19},{19,3},{4,20},{20... | collective-permute-start | bytes 6291464 | tf_op jit(solution)/shard_map/ppermute | solution.py:74
  235.3 64.4 %collective-permute-start.22 = (f32[512,1024]{1,0:T(8,128)}, f32[512,1024]{1,0:T(8,128)}, u32[]{:S(2)}, u32[]{:S(2)}) collective-permute-start(f32[512,1024]{1,0:T(8,128)} %shard_map.222), channel_id=1, source_target_pairs={{0,16},{16,0},{1,17},{17,1},{2,18},{18,2},{3,19},{19,3},{4,20},{20... | collective-permute-start | bytes 6291464 | tf_op jit(solution)/shard_map/ppermute | solution.py:74
  266.7 39.4 %collective-permute-start.32 = (f32[512,1024]{1,0:T(8,128)}, f32[512,1024]{1,0:T(8,128)}, u32[]{:S(2)}, u32[]{:S(2)}) collective-permute-start(f32[512,1024]{1,0:T(8,128)} %shard_map.226), channel_id=1, source_target_pairs={{0,16},{16,0},{1,17},{17,1},{2,18},{18,2},{3,19},{19,3},{4,20},{20... | collective-permute-start | bytes 6291464 | tf_op jit(solution)/shard_map/ppermute | solution.py:74
  274.8 38.3 %collective-permute-start.27 = (f32[512,1024]{1,0:T(8,128)}, f32[512,1024]{1,0:T(8,128)S(1)}, u32[]{:S(2)}, u32[]{:S(2)}) collective-permute-start(f32[512,1024]{1,0:T(8,128)} %shard_map.224), channel_id=1, source_target_pairs={{0,16},{16,0},{1,17},{17,1},{2,18},{18,2},{3,19},{19,3},{4,20},{20... | collective-permute-start | bytes 6291464 | tf_op jit(solution)/shard_map/ppermute | solution.py:74
  290.1 126.4 %collective-permute-start.47 = (f32[512,2560]{1,0:T(8,128)}, f32[512,2560]{1,0:T(8,128)}, u32[]{:S(2)}, u32[]{:S(2)}) collective-permute-start(f32[512,2560]{1,0:T(8,128)} %shard_map.232), channel_id=1, source_target_pairs={{0,16},{16,0},{1,17},{17,1},{2,18},{18,2},{3,19},{19,3},{4,20},{20... | collective-permute-start | bytes 15728648 | tf_op jit(solution)/shard_map/ppermute | solution.py:74
  290.6 140.5 %collective-permute-start.61 = (f32[1408,1024]{1,0:T(8,128)}, f32[1408,1024]{1,0:T(8,128)}, u32[]{:S(2)}, u32[]{:S(2)}) collective-permute-start(f32[1408,1024]{1,0:T(8,128)} %shard_map.236), channel_id=1, source_target_pairs={{0,16},{16,0},{1,17},{17,1},{2,18},{18,2},{3,19},{19,3},{4,20},{20... | collective-permute-start | bytes 17301512 | tf_op jit(solution)/shard_map/ppermute | solution.py:74
  299.7 147.3 %collective-permute-start.52 = (f32[512,3072]{1,0:T(8,128)}, f32[512,3072]{1,0:T(8,128)}, u32[]{:S(2)}, u32[]{:S(2)}) collective-permute-start(f32[512,3072]{1,0:T(8,128)} %shard_map.234), channel_id=1, source_target_pairs={{0,16},{16,0},{1,17},{17,1},{2,18},{18,2},{3,19},{19,3},{4,20},{20... | collective-permute-start | bytes 18874376 | tf_op jit(solution)/shard_map/ppermute | solution.py:74
  306.1 25.2 %collective-permute-start.43 = (f32[2,2,2,32,1024]{4,3,2,1,0:T(8,128)S(1)}, f32[2,2,2,32,1024]{4,3,2,1,0:T(8,128)S(1)}, u32[]{:S(2)}, u32[]{:S(2)}) collective-permute-start(f32[2,2,2,32,1024]{4,3,2,1,0:T(8,128)S(1)} %dynamic-slice_bitcast_fusion.5), channel_id=1, source_target_pairs={{0,1},{1,0},{2,3},{3,2},{4,5},{5,4},{6,7},{7,6},{8,9},{9,8},{10,11... | collective-permute-start | bytes 3145736 | tf_op jit(solution)/shard_map/ppermute | solution.py:67
  313.2 25.0 %collective-permute-start.38 = (f32[2,2,2,32,1024]{4,3,2,1,0:T(8,128)S(1)}, f32[2,2,2,32,1024]{4,3,2,1,0:T(8,128)S(1)}, u32[]{:S(2)}, u32[]{:S(2)}) collective-permute-start(f32[2,2,2,32,1024]{4,3,2,1,0:T(8,128)S(1)} %dynamic-slice_bitcast_fusion.6), channel_id=1, source_target_pairs={{0,2},{1,3},{2,0},{3,1},{4,6},{5,7},{6,4},{7,5},{8,10},{9,11},{10,... | collective-permute-start | bytes 3145736 | tf_op jit(solution)/shard_map/ppermute | solution.py:67
  331.2 26.1 %collective-permute-start.23 = (f32[2,2,2,32,1024]{4,3,2,1,0:T(8,128)S(1)}, f32[2,2,2,32,1024]{4,3,2,1,0:T(8,128)S(1)}, u32[]{:S(2)}, u32[]{:S(2)}) collective-permute-start(f32[2,2,2,32,1024]{4,3,2,1,0:T(8,128)S(1)} %dynamic-slice_bitcast_fusion.9), channel_id=1, source_target_pairs={{0,1},{1,0},{2,3},{3,2},{4,5},{5,4},{6,7},{7,6},{8,9},{9,8},{10,11... | collective-permute-start | bytes 3145736 | tf_op jit(solution)/shard_map/ppermute | solution.py:67
  338.2 39.8 %collective-permute-start.33 = (f32[2,2,2,32,1024]{4,3,2,1,0:T(8,128)S(1)}, f32[2,2,2,32,1024]{4,3,2,1,0:T(8,128)}, u32[]{:S(2)}, u32[]{:S(2)}) collective-permute-start(f32[2,2,2,32,1024]{4,3,2,1,0:T(8,128)S(1)} %dynamic-slice_bitcast_fusion.7), channel_id=1, source_target_pairs={{0,1},{1,0},{2,3},{3,2},{4,5},{5,4},{6,7},{7,6},{8,9},{9,8},{10,11... | collective-permute-start | bytes 3145736 | tf_op jit(solution)/shard_map/ppermute | solution.py:67
  358.3 33.1 %collective-permute-start.28 = (f32[2,2,2,32,1024]{4,3,2,1,0:T(8,128)S(1)}, f32[2,2,2,32,1024]{4,3,2,1,0:T(8,128)S(1)}, u32[]{:S(2)}, u32[]{:S(2)}) collective-permute-start(f32[2,2,2,32,1024]{4,3,2,1,0:T(8,128)S(1)} %dynamic-slice_bitcast_fusion.8), channel_id=1, source_target_pairs={{0,2},{1,3},{2,0},{3,1},{4,6},{5,7},{6,4},{7,5},{8,10},{9,11},{10,... | collective-permute-start | bytes 3145736 | tf_op jit(solution)/shard_map/ppermute | solution.py:67
  378.1 15.2 %collective-permute-start.44 = (f32[2,2,32,1024]{3,2,1,0:T(8,128)S(1)}, f32[2,2,32,1024]{3,2,1,0:T(8,128)S(1)}, u32[]{:S(2)}, u32[]{:S(2)}) collective-permute-start(f32[2,2,32,1024]{3,2,1,0:T(8,128)S(1)} %bitcast_add_fusion.7), channel_id=1, source_target_pairs={{0,2},{1,3},{2,0},{3,1},{4,6},{5,7},{6,4},{7,5},{8,10},{9,11},{10,... | collective-permute-start | bytes 1572872 | tf_op jit(solution)/shard_map/ppermute | solution.py:67
  411.4 49.7 %collective-permute-start.34 = (f32[2,2,32,1024]{3,2,1,0:T(8,128)S(1)}, f32[2,2,32,1024]{3,2,1,0:T(8,128)S(1)}, u32[]{:S(2)}, u32[]{:S(2)}) collective-permute-start(f32[2,2,32,1024]{3,2,1,0:T(8,128)S(1)} %bitcast_add_fusion.9), channel_id=1, source_target_pairs={{0,2},{1,3},{2,0},{3,1},{4,6},{5,7},{6,4},{7,5},{8,10},{9,11},{10,... | collective-permute-start | bytes 1572872 | tf_op jit(solution)/shard_map/ppermute | solution.py:67
  414.2 47.4 %collective-permute-start.29 = (f32[2,2,32,1024]{3,2,1,0:T(8,128)S(1)}, f32[2,2,32,1024]{3,2,1,0:T(8,128)S(1)}, u32[]{:S(2)}, u32[]{:S(2)}) collective-permute-start(f32[2,2,32,1024]{3,2,1,0:T(8,128)S(1)} %bitcast_add_fusion.10), channel_id=1, source_target_pairs={{0,1},{1,0},{2,3},{3,2},{4,5},{5,4},{6,7},{7,6},{8,9},{9,8},{10,11... | collective-permute-start | bytes 1572872 | tf_op jit(solution)/shard_map/ppermute | solution.py:67
  416.5 44.1 %collective-permute-start.25 = (f32[2,32,1024]{2,1,0:T(8,128)S(1)}, f32[2,32,1024]{2,1,0:T(8,128)S(1)}, u32[]{:S(2)}, u32[]{:S(2)}) collective-permute-start(f32[2,32,1024]{2,1,0:T(8,128)S(1)} %bitcast_add_fusion.34), channel_id=1, source_target_pairs={{0,4},{1,5},{2,6},{3,7},{4,0},{5,1},{6,2},{7,3},{8,12},{9,13},{10,... | collective-permute-start | bytes 786440 | tf_op jit(solution)/shard_map/ppermute | solution.py:67
  431.1 35.2 %collective-permute-start.46 = (f32[32,1024]{1,0:T(8,128)S(1)}, f32[32,1024]{1,0:T(8,128)}, u32[]{:S(2)}, u32[]{:S(2)}) collective-permute-start(f32[32,1024]{1,0:T(8,128)S(1)} %bitcast_add_fusion.60), channel_id=1, source_target_pairs={{0,8},{1,9},{2,10},{3,11},{4,12},{5,13},{6,14},{7,15},{8,0},{9,1},... | collective-permute-start | bytes 393224 | tf_op jit(solution)/shard_map/ppermute | solution.py:67
  447.0 40.8 %collective-permute-start.62 = (f32[2,2,2,88,512]{4,3,2,1,0:T(8,128)}, f32[2,2,2,88,512]{4,3,2,1,0:T(8,128)}, u32[]{:S(2)}, u32[]{:S(2)}) collective-permute-start(f32[2,2,2,88,512]{4,3,2,1,0:T(8,128)} %dynamic-slice_bitcast_fusion.4), channel_id=1, source_target_pairs={{0,1},{1,0},{2,3},{3,2},{4,5},{5,4},{6,7},{7,6},{8,9},{9,8},{10,11... | collective-permute-start | bytes 4325384 | tf_op jit(solution)/shard_map/ppermute | solution.py:67
  461.1 84.0 %collective-permute-start.48 = (f32[2,2,2,32,2560]{4,3,2,1,0:T(8,128)}, f32[2,2,2,32,2560]{4,3,2,1,0:T(8,128)}, u32[]{:S(2)}, u32[]{:S(2)}) collective-permute-start(f32[2,2,2,32,2560]{4,3,2,1,0:T(8,128)} %dynamic-slice_bitcast_fusion), channel_id=1, source_target_pairs={{0,4},{1,5},{2,6},{3,7},{4,0},{5,1},{6,2},{7,3},{8,12},{9,13},{10,... | collective-permute-start | bytes 7864328 | tf_op jit(solution)/shard_map/ppermute | solution.py:67
  462.8 34.8 %collective-permute-start.66 = (f32[2,2,2,88,512]{4,3,2,1,0:T(8,128)}, f32[2,2,2,88,512]{4,3,2,1,0:T(8,128)}, u32[]{:S(2)}, u32[]{:S(2)}) collective-permute-start(f32[2,2,2,88,512]{4,3,2,1,0:T(8,128)} %dynamic-slice_bitcast_fusion.3), channel_id=1, source_target_pairs={{0,2},{1,3},{2,0},{3,1},{4,6},{5,7},{6,4},{7,5},{8,10},{9,11},{10,... | collective-permute-start | bytes 4325384 | tf_op jit(solution)/shard_map/ppermute | solution.py:67
  466.3 64.9 %collective-permute-start.53 = (f32[2,2,2,32,1536]{4,3,2,1,0:T(8,128)}, f32[2,2,2,32,1536]{4,3,2,1,0:T(8,128)}, u32[]{:S(2)}, u32[]{:S(2)}) collective-permute-start(f32[2,2,2,32,1536]{4,3,2,1,0:T(8,128)} %dynamic-slice_bitcast_fusion.2), channel_id=1, source_target_pairs={{0,1},{1,0},{2,3},{3,2},{4,5},{5,4},{6,7},{7,6},{8,9},{9,8},{10,11... | collective-permute-start | bytes 4718600 | tf_op jit(solution)/shard_map/ppermute | solution.py:67
  468.3 65.9 %collective-permute-start.57 = (f32[2,2,2,32,1536]{4,3,2,1,0:T(8,128)S(1)}, f32[2,2,2,32,1536]{4,3,2,1,0:T(8,128)}, u32[]{:S(2)}, u32[]{:S(2)}) collective-permute-start(f32[2,2,2,32,1536]{4,3,2,1,0:T(8,128)S(1)} %dynamic-slice_bitcast_fusion.1), channel_id=1, source_target_pairs={{0,2},{1,3},{2,0},{3,1},{4,6},{5,7},{6,4},{7,5},{8,10},{9,11},{10,... | collective-permute-start | bytes 4718600 | tf_op jit(solution)/shard_map/ppermute | solution.py:67
  487.9 38.2 %collective-permute-start.35 = (f32[2,32,1024]{2,1,0:T(8,128)S(1)}, f32[2,32,1024]{2,1,0:T(8,128)S(1)}, u32[]{:S(2)}, u32[]{:S(2)}) collective-permute-start(f32[2,32,1024]{2,1,0:T(8,128)S(1)} %bitcast_add_fusion.30), channel_id=1, source_target_pairs={{0,4},{1,5},{2,6},{3,7},{4,0},{5,1},{6,2},{7,3},{8,12},{9,13},{10,... | collective-permute-start | bytes 786440 | tf_op jit(solution)/shard_map/ppermute | solution.py:67
  497.6 26.3 %collective-permute-start.26 = (f32[32,1024]{1,0:T(8,128)S(1)}, f32[32,1024]{1,0:T(8,128)S(1)}, u32[]{:S(2)}, u32[]{:S(2)}) collective-permute-start(f32[32,1024]{1,0:T(8,128)S(1)} %bitcast_add_fusion.84), channel_id=1, source_target_pairs={{0,8},{1,9},{2,10},{3,11},{4,12},{5,13},{6,14},{7,15},{8,0},{9,1},... | collective-permute-start | bytes 393224 | tf_op jit(solution)/shard_map/ppermute | solution.py:67
  523.9 17.9 %collective-permute-start.63 = (f32[2,2,88,512]{3,2,1,0:T(8,128)S(1)}, f32[2,2,88,512]{3,2,1,0:T(8,128)S(1)}, u32[]{:S(2)}, u32[]{:S(2)}) collective-permute-start(f32[2,2,88,512]{3,2,1,0:T(8,128)S(1)} %get-tuple-element.129), channel_id=1, source_target_pairs={{0,2},{1,3},{2,0},{3,1},{4,6},{5,7},{6,4},{7,5},{8,10},{9,11},{10,... | collective-permute-start | bytes 2162696 | tf_op jit(solution)/shard_map/ppermute | solution.py:67
  526.1 16.2 %collective-permute-start.67 = (f32[2,2,88,512]{3,2,1,0:T(8,128)S(1)}, f32[2,2,88,512]{3,2,1,0:T(8,128)S(1)}, u32[]{:S(2)}, u32[]{:S(2)}) collective-permute-start(f32[2,2,88,512]{3,2,1,0:T(8,128)S(1)} %get-tuple-element.130), channel_id=1, source_target_pairs={{0,1},{1,0},{2,3},{3,2},{4,5},{5,4},{6,7},{7,6},{8,9},{9,8},{10,11... | collective-permute-start | bytes 2162696 | tf_op jit(solution)/shard_map/ppermute | solution.py:67
  531.1 18.2 %collective-permute-start.30 = (f32[2,32,1024]{2,1,0:T(8,128)S(1)}, f32[2,32,1024]{2,1,0:T(8,128)S(1)}, u32[]{:S(2)}, u32[]{:S(2)}) collective-permute-start(f32[2,32,1024]{2,1,0:T(8,128)S(1)} %bitcast_add_fusion.32), channel_id=1, source_target_pairs={{0,4},{1,5},{2,6},{3,7},{4,0},{5,1},{6,2},{7,3},{8,12},{9,13},{10,... | collective-permute-start | bytes 786440 | tf_op jit(solution)/shard_map/ppermute | solution.py:67
  534.2 17.4 %collective-permute-start.36 = (f32[32,1024]{1,0:T(8,128)S(1)}, f32[32,1024]{1,0:T(8,128)S(1)}, u32[]{:S(2)}, u32[]{:S(2)}) collective-permute-start(f32[32,1024]{1,0:T(8,128)S(1)} %bitcast_add_fusion.72), channel_id=1, source_target_pairs={{0,8},{1,9},{2,10},{3,11},{4,12},{5,13},{6,14},{7,15},{8,0},{9,1},... | collective-permute-start | bytes 393224 | tf_op jit(solution)/shard_map/ppermute | solution.py:67
  541.8 18.3 %collective-permute-start.54 = (f32[2,2,32,1536]{3,2,1,0:T(8,128)S(1)}, f32[2,2,32,1536]{3,2,1,0:T(8,128)S(1)}, u32[]{:S(2)}, u32[]{:S(2)}) collective-permute-start(f32[2,2,32,1536]{3,2,1,0:T(8,128)S(1)} %get-tuple-element.123), channel_id=1, source_target_pairs={{0,2},{1,3},{2,0},{3,1},{4,6},{5,7},{6,4},{7,5},{8,10},{9,11},{10,... | collective-permute-start | bytes 2359304 | tf_op jit(solution)/shard_map/ppermute | solution.py:67
  542.3 21.4 %collective-permute-start.58 = (f32[2,2,32,1536]{3,2,1,0:T(8,128)S(1)}, f32[2,2,32,1536]{3,2,1,0:T(8,128)S(1)}, u32[]{:S(2)}, u32[]{:S(2)}) collective-permute-start(f32[2,2,32,1536]{3,2,1,0:T(8,128)S(1)} %get-tuple-element.124), channel_id=1, source_target_pairs={{0,1},{1,0},{2,3},{3,2},{4,5},{5,4},{6,7},{7,6},{8,9},{9,8},{10,11... | collective-permute-start | bytes 2359304 | tf_op jit(solution)/shard_map/ppermute | solution.py:67
  545.1 13.9 %collective-permute-start.64 = (f32[2,88,512]{2,1,0:T(8,128)S(1)}, f32[2,88,512]{2,1,0:T(8,128)S(1)}, u32[]{:S(2)}, u32[]{:S(2)}) collective-permute-start(f32[2,88,512]{2,1,0:T(8,128)S(1)} %get-tuple-element.127), channel_id=1, source_target_pairs={{0,4},{1,5},{2,6},{3,7},{4,0},{5,1},{6,2},{7,3},{8,12},{9,13},{10,... | collective-permute-start | bytes 1081352 | tf_op jit(solution)/shard_map/ppermute | solution.py:67
  549.4 73.8 %collective-permute-start.49 = (f32[2,2,32,2560]{3,2,1,0:T(8,128)S(1)}, f32[2,2,32,2560]{3,2,1,0:T(8,128)S(1)}, u32[]{:S(2)}, u32[]{:S(2)}) collective-permute-start(f32[2,2,32,2560]{3,2,1,0:T(8,128)S(1)} %bitcast_add_fusion), channel_id=1, source_target_pairs={{0,8},{1,9},{2,10},{3,11},{4,12},{5,13},{6,14},{7,15},{8,0},{9,1},... | collective-permute-start | bytes 3932168 | tf_op jit(solution)/shard_map/ppermute | solution.py:67
  551.6 61.1 %collective-permute-start.31 = (f32[32,1024]{1,0:T(8,128)S(1)}, f32[32,1024]{1,0:T(8,128)S(1)}, u32[]{:S(2)}, u32[]{:S(2)}) collective-permute-start(f32[32,1024]{1,0:T(8,128)S(1)} %bitcast_add_fusion.78), channel_id=1, source_target_pairs={{0,8},{1,9},{2,10},{3,11},{4,12},{5,13},{6,14},{7,15},{8,0},{9,1},... | collective-permute-start | bytes 393224 | tf_op jit(solution)/shard_map/ppermute | solution.py:67
  559.0 55.3 %collective-permute-start.68 = (f32[2,88,512]{2,1,0:T(8,128)S(1)}, f32[2,88,512]{2,1,0:T(8,128)S(1)}, u32[]{:S(2)}, u32[]{:S(2)}) collective-permute-start(f32[2,88,512]{2,1,0:T(8,128)S(1)} %get-tuple-element.128), channel_id=1, source_target_pairs={{0,4},{1,5},{2,6},{3,7},{4,0},{5,1},{6,2},{7,3},{8,12},{9,13},{10,... | collective-permute-start | bytes 1081352 | tf_op jit(solution)/shard_map/ppermute | solution.py:67
  560.1 54.5 %collective-permute-start.65 = (f32[88,512]{1,0:T(8,128)S(1)}, f32[88,512]{1,0:T(8,128)S(1)}, u32[]{:S(2)}, u32[]{:S(2)}) collective-permute-start(f32[88,512]{1,0:T(8,128)S(1)} %bitcast_add_fusion.54), channel_id=1, source_target_pairs={{0,8},{1,9},{2,10},{3,11},{4,12},{5,13},{6,14},{7,15},{8,0},{9,1},... | collective-permute-start | bytes 540680 | tf_op jit(solution)/shard_map/ppermute | solution.py:67
  565.0 57.0 %collective-permute-start.55 = (f32[2,32,1536]{2,1,0:T(8,128)S(1)}, f32[2,32,1536]{2,1,0:T(8,128)S(1)}, u32[]{:S(2)}, u32[]{:S(2)}) collective-permute-start(f32[2,32,1536]{2,1,0:T(8,128)S(1)} %get-tuple-element.121), channel_id=1, source_target_pairs={{0,4},{1,5},{2,6},{3,7},{4,0},{5,1},{6,2},{7,3},{8,12},{9,13},{10,... | collective-permute-start | bytes 1179656 | tf_op jit(solution)/shard_map/ppermute | solution.py:67
  616.0 22.9 %collective-permute-start.69 = (f32[88,512]{1,0:T(8,128)S(1)}, f32[88,512]{1,0:T(8,128)S(1)}, u32[]{:S(2)}, u32[]{:S(2)}) collective-permute-start(f32[88,512]{1,0:T(8,128)S(1)} %get-tuple-element.126), channel_id=1, source_target_pairs={{0,8},{1,9},{2,10},{3,11},{4,12},{5,13},{6,14},{7,15},{8,0},{9,1},... | collective-permute-start | bytes 540680 | tf_op jit(solution)/shard_map/ppermute | solution.py:67
  616.1 19.2 %collective-permute-start.59 = (f32[2,32,1536]{2,1,0:T(8,128)S(1)}, f32[2,32,1536]{2,1,0:T(8,128)S(1)}, u32[]{:S(2)}, u32[]{:S(2)}) collective-permute-start(f32[2,32,1536]{2,1,0:T(8,128)S(1)} %get-tuple-element.122), channel_id=1, source_target_pairs={{0,4},{1,5},{2,6},{3,7},{4,0},{5,1},{6,2},{7,3},{8,12},{9,13},{10,... | collective-permute-start | bytes 1179656 | tf_op jit(solution)/shard_map/ppermute | solution.py:67
  624.5 23.8 %collective-permute-start.50 = (f32[2,32,2560]{2,1,0:T(8,128)S(1)}, f32[2,32,2560]{2,1,0:T(8,128)S(1)}, u32[]{:S(2)}, u32[]{:S(2)}) collective-permute-start(f32[2,32,2560]{2,1,0:T(8,128)S(1)} %bitcast_add_fusion.5), channel_id=1, source_target_pairs={{0,1},{1,0},{2,3},{3,2},{4,5},{5,4},{6,7},{7,6},{8,9},{9,8},{10,11... | collective-permute-start | bytes 1966088 | tf_op jit(solution)/shard_map/ppermute | solution.py:67
  (70 other events, 702.1 us)

commit v3 on v2

v3 whole, which is shorter than its diff:
```python
import functools

import jax
import jax.numpy as jnp
from jax import lax
from jax.experimental import pallas as pl
from jax.experimental.pallas import tpu as pltpu
from jax.sharding import PartitionSpec as P

HEADS = 16
HEAD_DIM = 64
GROUP = 4 * HEAD_DIM
TILE = 256
EPSILON = 1e-06
F32 = jnp.float32
BF16 = jnp.bfloat16
VMEM_BYTES = 56 << 20
FLOPS_US = 1e11
STEPS = 2


def chip_grid(count):
    bits = count.bit_length() - 1
    z_bits = min(bits, 2)
    y_bits = (bits - z_bits + 1) // 2
    return z_bits, y_bits, bits - z_bits - y_bits


def orders(count):
    z_bits, y_bits, x_bits = chip_grid(count)
    z_axes = list(range(z_bits))[::-1]
    y_axes = list(range(z_bits, z_bits + y_bits))[::-1]
    x_axes = list(range(z_bits + y_bits, z_bits + y_bits + x_bits))[::-1]
    return x_axes + y_axes, y_axes + x_axes, z_axes


class Scatter:
    def __init__(self, turns, halves, order):
        self.turns = turns
        self.count = lax.axis_size("seq")
        self.bits = self.count.bit_length() - 1
        self.position = lax.axis_index("seq").astype(jnp.int32).reshape(1)
        self.rows = halves[0][0].shape[0] // self.count
        axes = tuple(range(self.bits))
        self.parts = [
            ([h.reshape((self.count, self.rows, h.shape[1])) for h in half], axes) for half in halves
        ]
        self.order = list(order)
        self.done = ()

    def total(self, flipped, widths=None):
        fixed = self.done if flipped is None else self.done + (flipped,)
        left = tuple(a for a in range(self.bits) if a not in fixed)
        bits, done = self.bits, self.done

        def block(axes, j, position):
            at = 0
            for a in axes:
                if a in left:
                    bit = (j >> (len(left) - 1 - left.index(a))) & 1
                else:
                    bit = (position[0] >> (bits - 1 - a)) & 1
                    if a == flipped:
                        bit = 1 - bit
                at = at * 2 + bit
            return at

        count = 1 << len(left)
        deep = max(1, count // STEPS)
        arrays, specs, places = [], [], []
        for held, axes in self.parts:
            begin = 0
            for array in held:
                wide = array.shape[2]
                for d in range(deep):
                    arrays.append(array)
                    specs.append(
                        pl.BlockSpec(
                            (1, self.rows, wide),
                            lambda j, position, axes=axes, d=d: (block(axes, j * deep + d, position), 0, 0),
                        )
                    )
                    places.append((d, begin, begin + wide))
                begin += wide
        final = widths is not None
        widths = widths or [begin]

        def kernel(position_ref, *refs):
            ins, outs = refs[: len(arrays)], refs[len(arrays) :]
            edge = 0
            for out, wide in zip(outs, widths):
                covers = sorted({p[1:] for p in places if p[1] < edge + wide and p[2] > edge})
                smallest = [p for p in covers if not any(q != p and p[0] <= q[0] and q[1] <= p[1] for q in covers)]
                for d in range(deep):
                    for low, high in smallest:
                        low, high = max(low, edge), min(high, edge + wide)
                        one = None
                        for ref, (at, begin, stop) in zip(ins, places):
                            if at == d and begin <= low and high <= stop:
                                term = ref[0, :, pl.ds(low - begin, high - low)]
                                one = term if one is None else one + term
                        if final:
                            out[:, pl.ds(low - edge, high - low)] = one
                        else:
                            out[d, :, pl.ds(low - edge, high - low)] = one
                edge += wide

        if final:
            out_specs = [pl.BlockSpec((self.rows, w), lambda j, position: (0, 0)) for w in widths]
            out_shape = [shape((self.rows, w), F32) for w in widths]
        else:
            out_specs = [pl.BlockSpec((deep, self.rows, w), lambda j, position: (j, 0, 0)) for w in widths]
            out_shape = [shape((count, self.rows, w), F32) for w in widths]
        return self.turns.call(kernel, (count // deep,), specs, out_specs, out_shape, prefetch=1, us=2)(
            self.position, *arrays
        )

    def finish_planes(self):
        while self.order:
            self.step()
        (terms,) = self.total(None)
        return scatter_between_planes(terms.reshape(-1, terms.shape[2]))

    def step(self):
        axis = self.order.pop(0)
        (outgoing,) = self.total(axis)
        flip = 1 << (self.bits - 1 - axis)
        incoming = lax.ppermute(outgoing, "seq", [(i, i ^ flip) for i in range(self.count)])
        self.done = self.done + (axis,)
        left = tuple(a for a in range(self.bits) if a not in self.done)
        self.parts.append(([incoming], left))

    def finish(self, *widths):
        while self.order:
            self.step()
        return self.total(None, list(widths))


def to_core(arrays):
    return [lax.ppermute(array, "batch", [(0, 1), (1, 0)]) for array in arrays]


class Turns:
    def __init__(self):
        self.last = ()

    def call(self, kernel, grid, in_specs, out_specs, out_shape, scratch=(), prefetch=0, us=10):
        given = len(in_specs) + prefetch
        waits = len(self.last)

        def body(*refs):
            kernel(*refs[:given], *refs[given + waits :])

        spec = pltpu.PrefetchScalarGridSpec(
            num_scalar_prefetch=prefetch,
            grid=grid,
            in_specs=list(in_specs) + [pl.BlockSpec(memory_space=pl.ANY)] * waits,
            out_specs=out_specs,
            scratch_shapes=scratch,
        )

        def run(*args):
            out = pl.pallas_call(
                body,
                grid_spec=spec,
                out_shape=out_shape,
                compiler_params=pltpu.CompilerParams(vmem_limit_bytes=VMEM_BYTES),
                cost_estimate=pl.CostEstimate(flops=int(us * FLOPS_US), bytes_accessed=0, transcendentals=0),
            )(*args, *self.last)
            self.last = (out[0] if isinstance(out, (list, tuple)) else out,)
            return out

        return run


def shape(dims, dtype):
    return jax.ShapeDtypeStruct(dims, dtype)


def dot(a, b):
    return lax.dot_general(a, b, (((1,), (0,)), ((), ())), preferred_element_type=F32)


def dot_nt(a, b):
    return lax.dot_general(a, b, (((1,), (1,)), ((), ())), preferred_element_type=F32)


def dot_tn(a, b):
    return lax.dot_general(a, b, (((0,), (0,)), ((), ())), preferred_element_type=F32)


def grad_halves(turns, pairs, core, tile, apart=False, us=10):
    tokens, width = pairs[0][0].shape
    wide = width // 2
    per = pairs[0][1].shape[1] // tile
    acts = []
    for one, _ in pairs:
        if not any(one is a for a in acts):
            acts.append(one)
    number, kinds = len(pairs), len(acts)
    which = [[one is a for a in acts].index(True) for one, _ in pairs]
    one_buffer = pl.Buffered(1)
    sent_half = pl.BlockSpec((tokens, wide), lambda j, s: (0, 1 - s[0]), pipeline_mode=one_buffer)
    kept_half = pl.BlockSpec((tokens, wide), lambda j, s: (0, s[0]), pipeline_mode=one_buffer)

    def kernel(core_ref, *refs):
        step = pl.program_id(0)
        outs = refs[2 * kinds + number :]
        for i in range(number):

            @pl.when((step >= i * per) & (step < (i + 1) * per))
            def _(i=i):
                grads = refs[2 * kinds + i][...]
                outs[i if apart else 0][...] = dot_tn(refs[2 * which[i]][...], grads)
                outs[number + i if apart else 1][...] = dot_tn(refs[2 * which[i] + 1][...], grads)

    def part(i):
        return pl.BlockSpec((tokens, tile), lambda j, s: (0, jnp.clip(j - i * per, 0, per - 1)))

    def out_part(i):
        if not apart:
            return pl.BlockSpec((wide, tile), lambda j, s: (0, j))
        return pl.BlockSpec((wide, tile), lambda j, s: (0, jnp.clip(j - i * per, 0, per - 1)))

    arrays = number if apart else 1
    cols = tile * per if apart else tile * per * number
    outs = turns.call(
        kernel,
        (per * number,),
        [sent_half, kept_half] * kinds + [part(i) for i in range(number)],
        [out_part(i) for i in range(arrays)] * 2,
        [shape((wide, cols), F32)] * (2 * arrays),
        prefetch=1,
        us=us,
    )(core, *[a for one in acts for a in (one, one)], *[g for _, g in pairs])
    return list(outs[:arrays]), list(outs[arrays:])


def scatter_between_planes(array):
    count = lax.axis_size("seq")
    planes = 1 << chip_grid(count)[0]
    plane = count // planes
    groups = [[k + plane * z for z in range(planes)] for k in range(plane)]
    return lax.psum_scatter(array, "seq", scatter_dimension=0, axis_index_groups=groups, tiled=True)


def small_call(turns, kernel, out_shape, args):
    def whole(array):
        return pl.BlockSpec(array.shape, lambda _: (0,) * len(array.shape))

    specs = [pl.BlockSpec(memory_space=pltpu.SMEM)] + [whole(a) for a in args[1:]]
    return turns.call(kernel, (1,), specs, [whole(o) for o in out_shape], out_shape, us=2)(*args)


class Prefix:
    def __init__(self, turns, state, edge_ids, reverse):
        self.turns = turns
        self.reverse = reverse
        self.count = lax.axis_size("seq")
        z_bits, y_bits, x_bits = chip_grid(self.count)
        self.planes = 1 << z_bits
        self.plane = plane = 1 << (y_bits + x_bits)
        position = lax.axis_index("seq")
        place = jnp.stack([position // plane, position % plane]).astype(jnp.int32)
        self.place = jnp.concatenate([place, edge_ids])
        row_count, depth, lanes = state.shape
        self.size = size = depth // plane
        self.row_count = row_count
        self.share = shape((row_count, size + 8, lanes), F32)

        def split(at_ref, s_ref, *outs):
            for k in range(plane):
                begin = pl.multiple_of((at_ref[1] ^ k) * size, size)
                outs[k][:, pl.ds(0, size), :] = s_ref[:, pl.ds(begin, size), :]
                for r in range(row_count):
                    outs[k][r, pl.ds(size, 8), :] = jnp.full((8, lanes), at_ref[2 + r].astype(F32))

        shares = small_call(turns, split, [self.share] * plane, (self.place, state))
        self.swapped = self.swap(shares)

    def swap(self, shares):
        plane = self.plane
        return [shares[0]] + [
            lax.ppermute(
                shares[k],
                "seq",
                [(i, (i // plane) * plane + ((i % plane) ^ k)) for i in range(self.count)],
            )
            for k in range(1, plane)
        ]

    def pass_on(self):
        plane, size = self.plane, self.size
        end = 0 if self.reverse else plane - 1

        def total(at_ref, *refs):
            out = refs[plane]
            for r in range(self.row_count):
                last = refs[0][r, pl.ds(size, 8), :]
                for k in range(1, plane):
                    last = jnp.where((at_ref[1] ^ k) == end, refs[k][r, pl.ds(size, 8), :], last)
                summed = None
                for k in range(plane):
                    same = refs[k][r, pl.ds(size, 1), :] == last[:1]
                    one = jnp.where(same, refs[k][r, pl.ds(0, size), :], 0.0)
                    summed = one if summed is None else summed + one
                out[r, pl.ds(0, size), :] = summed
                out[r, pl.ds(size, 8), :] = last

        (total_share,) = small_call(self.turns, total, [self.share], (self.place, *self.swapped))
        self.passed = []
        for step in range(1, self.planes):
            shift = -step * plane if self.reverse else step * plane
            moves = [(i, i + shift) for i in range(self.count) if 0 <= i + shift < self.count]
            self.passed.append(lax.ppermute(total_share, "seq", moves))

    def swap_back(self):
        plane, size, planes = self.plane, self.size, self.planes

        def results(at_ref, *refs):
            shares, passed, outs = refs[:plane], refs[plane : plane + planes - 1], refs[plane + planes - 1 :]
            z_at, at = at_ref[0], at_ref[1]
            for r in range(self.row_count):
                ids = [one[r, pl.ds(size, 8), :] for one in shares]
                far_ids = [one[r, pl.ds(size, 8), :] for one in passed]
                there = [
                    (z_at + step < planes) if self.reverse else (z_at >= step) for step in range(1, planes)
                ]
                for k in range(plane):
                    target = at ^ k
                    near = jnp.where(there[0], far_ids[0], -1.0) if planes > 1 else jnp.full_like(ids[0], -1.0)
                    beside = target + 1 if self.reverse else target - 1
                    for j in range(plane):
                        near = jnp.where((at ^ j) == beside, ids[j], near)
                    summed = jnp.zeros((size, 128), F32)
                    for j in range(plane):
                        before = (at ^ j) > target if self.reverse else (at ^ j) < target
                        same = before & (ids[j][:1] == near[:1])
                        summed = summed + jnp.where(same, shares[j][r, pl.ds(0, size), :], 0.0)
                    for one, far, is_there in zip(passed, far_ids, there):
                        same = is_there & (far[:1] == near[:1])
                        summed = summed + jnp.where(same, one[r, pl.ds(0, size), :], 0.0)
                    outs[k][r, pl.ds(0, size), :] = summed
                    outs[k][r, pl.ds(size, 8), :] = near

        back = small_call(
            self.turns, results, [self.share] * plane, (self.place, *self.swapped, *self.passed)
        )
        self.back = self.swap(back)

    def join(self):
        plane, size = self.plane, self.size

        def join(at_ref, *refs):
            out, near = refs[plane:]
            for k in range(plane):
                begin = pl.multiple_of((at_ref[1] ^ k) * size, size)
                out[:, pl.ds(begin, size), :] = refs[k][:, pl.ds(0, size), :]
            near[...] = refs[0][:, pl.ds(size, 8), :]

        dims = (self.row_count, size * plane, 128)
        return small_call(
            self.turns, join, [shape(dims, F32), shape((self.row_count, 8, 128), F32)], (self.place, *self.back)
        )


class Scan:
    def __init__(self, turns, payload, reverse):
        self.turns = turns
        self.reverse = reverse
        self.count = lax.axis_size("seq")
        self.bits = self.count.bit_length() - 1
        self.position = lax.axis_index("seq")
        self.payload = payload
        self.result = None
        self.at = 0

    def send(self):
        flip = 1 << self.at
        self.got = lax.ppermute(self.payload, "seq", [(i, i ^ flip) for i in range(self.count)])

    def take(self):
        row_count, height, lanes = self.payload.shape
        depth = height - 16
        bit = ((self.position >> self.at) & 1).astype(jnp.int32).reshape(1)
        first = self.at == 0
        self.at += 1
        last = self.at == self.bits

        def add(bit_ref, own_ref, got_ref, *refs):
            earlier = bit_ref[0] == (0 if self.reverse else 1)
            outs = refs if first else refs[1:]
            ids = pl.ds(depth, 8)
            states = pl.ds(0, depth)
            sums = pl.ds(depth + 8, 8)
            for r in range(row_count):
                own_id, got_id = own_ref[r, ids, :], got_ref[r, ids, :]
                got = got_ref[r, states, :]
                near = jnp.full_like(own_id, -1.0) if first else refs[0][r, ids, :]
                near = jnp.where(earlier & (near < 0.0), got_id, near)
                outs[0][r, ids, :] = near
                for out in outs:
                    out[r, sums, :] = own_ref[r, sums, :] + got_ref[r, sums, :]
                use = earlier & (near[:1] == got_id[:1])
                kept = jnp.where(use, got, 0.0)
                outs[0][r, states, :] = kept if first else refs[0][r, states, :] + kept
                if not last:
                    same = own_id[:1] == got_id[:1]
                    outs[1][r, states, :] = jnp.where(same | earlier, own_ref[r, states, :], 0.0) + jnp.where(
                        same | jnp.logical_not(earlier), got, 0.0
                    )
                    outs[1][r, ids, :] = jnp.where(earlier, own_id, got_id)

        like = shape(self.payload.shape, F32)
        held = () if first else (self.result,)
        outs = small_call(
            self.turns, add, [like] * (1 if last else 2), (bit, self.payload, self.got, *held)
        )
        self.result = outs[0]
        if not last:
            self.payload = outs[1]


def softplus(v):
    return jnp.maximum(v, 0.0) + jnp.log1p(jnp.exp(-jnp.abs(v)))


def sigmoid(v):
    return 1.0 / (1.0 + jnp.exp(-v))


def sigmoid_of_softplus(s):
    return jnp.where(s < 0.01, s * (1.0 - s * (0.5 - s * (1.0 / 6.0))), 1.0 - jnp.exp(-s))


def mean_square(v):
    return jnp.mean(v * v, axis=-1, keepdims=True)


def head_ones():
    a = lax.broadcasted_iota(jnp.int32, (GROUP, GROUP), 0) >> 6
    b = lax.broadcasted_iota(jnp.int32, (GROUP, GROUP), 1) >> 6
    return jnp.where(a == b, 1.0 / HEAD_DIM, 0.0).astype(BF16)


def head_mean(v, ones):
    high = v.astype(BF16)
    low = (v - high.astype(F32)).astype(BF16)
    return dot(high, ones) + dot(low, ones)


def one_head(block, h):
    lanes = lax.broadcasted_iota(jnp.int32, (1, GROUP), 1) >> 6
    return jnp.where(lanes == h, block, jnp.zeros_like(block))


def pack_state(full):
    left = lax.broadcasted_iota(jnp.int32, (HEAD_DIM, 128), 1) < HEAD_DIM
    pairs = []
    for p in range(2):
        block = full[128 * p : 128 * p + 128, 128 * p : 128 * p + 128]
        pairs.append(jnp.where(left, block[:HEAD_DIM], block[HEAD_DIM:]))
    return jnp.concatenate(pairs, axis=0)


def unpack_state(packed):
    left = lax.broadcasted_iota(jnp.int32, (HEAD_DIM, 128), 1) < HEAD_DIM
    none = jnp.zeros((128, 128), F32)
    rows = []
    for p in range(2):
        block = packed[HEAD_DIM * p : HEAD_DIM * p + HEAD_DIM]
        square = jnp.concatenate([jnp.where(left, block, 0.0), jnp.where(left, 0.0, block)], axis=0)
        rows.append(jnp.concatenate([square, none] if p == 0 else [none, square], axis=1))
    return jnp.concatenate(rows, axis=0).astype(BF16)


def full_spec(dims, buffers=1):
    return pl.BlockSpec(dims, lambda *_: (0,) * len(dims), pipeline_mode=pl.Buffered(buffers))


def whole_out(dims):
    return pl.BlockSpec(dims, lambda *_: (0,) * len(dims))


def column_spec(tokens, tile, begin=0):
    return pl.BlockSpec((tokens, tile), lambda j, *_: (0, j + begin))


def row_spec(tile, width):
    return pl.BlockSpec((tile, width), lambda i, *_: (i, 0))


SMEM = pl.BlockSpec(memory_space=pltpu.SMEM)


def project_keys(turns, inputs, ids_col, last_ids, w_key, w_value, row_count):
    tokens, width = inputs.shape
    block = tokens // row_count

    def kernel(last_ref, x_ref, id_ref, wk_ref, wv_ref, xn_ref, k_ref, v_ref, s_ref):
        @pl.when(pl.program_id(0) == 0)
        def _():
            for i in range(tokens // TILE):
                x = x_ref[pl.ds(i * TILE, TILE), :].astype(F32)
                xn_ref[pl.ds(i * TILE, TILE), :] = (x * lax.rsqrt(mean_square(x) + EPSILON)).astype(BF16)

        xn = xn_ref[...]
        keys = softplus(dot(xn, wk_ref[...])).astype(BF16)
        values = dot(xn, wv_ref[...]).astype(BF16)
        k_ref[...] = keys
        v_ref[...] = values
        for r in range(row_count):
            at = slice(r * block, (r + 1) * block)
            kept = jnp.where(id_ref[at] == last_ref[r], keys[at], jnp.zeros((), BF16))
            s_ref[r] = pack_state(dot_tn(kept, values[at]))

    return turns.call(
        kernel,
        (width // GROUP,),
        [SMEM, full_spec((tokens, width)), full_spec((tokens, 1)), column_spec(width, GROUP), column_spec(width, GROUP)],
        [
            whole_out((tokens, width)),
            column_spec(tokens, GROUP),
            column_spec(tokens, GROUP),
            pl.BlockSpec((row_count, GROUP // 2, 128), lambda j: (0, j, 0)),
        ],
        [shape((tokens, width), BF16)] * 3 + [shape((row_count, width // 2, 128), F32)],
        us=9.5,
    )(last_ids, inputs, ids_col, w_key, w_value)


def block_mask(id_col, id_row, first, transposed):
    dims = (id_col.shape[0], id_row.shape[1])
    a = lax.broadcasted_iota(jnp.int32, dims, 0) + first
    b = lax.broadcasted_iota(jnp.int32, dims, 1)
    causal = b >= a if transposed else a >= b
    return jnp.where(causal & (id_col == id_row), 1.0, 0.0).astype(BF16)


def attend(turns, normed, keys, values, ids_col, ids_row, w_query, w_outgate, begin, end):
    tokens, width = normed.shape
    row_count, _, block = ids_row.shape

    def kernel(xn_ref, k_ref, v_ref, ic_ref, ir_ref, wq_ref, wg_ref, q_ref, g_ref, o_ref, mask_ref):
        @pl.when(pl.program_id(0) == 0)
        def _():
            for r in range(row_count):
                for i in range(block // TILE):
                    at = pl.ds(r * block + i * TILE, TILE)
                    mask_ref[at, :] = block_mask(ic_ref[at, :], ir_ref[r], i * TILE, False)

        xn = xn_ref[...]
        q_ref[...] = softplus(dot(xn, wq_ref[...])).astype(BF16)
        g_ref[...] = sigmoid(dot(xn, wg_ref[...])).astype(BF16)
        for r in range(row_count):
            base = r * block
            for i in range(block // TILE):
                rows = pl.ds(base + i * TILE, TILE)
                seen = (i + 1) * TILE
                q = q_ref[rows, :]
                mask = mask_ref[rows, pl.ds(0, seen)]
                total = None
                for h in range(4):
                    k = one_head(k_ref[pl.ds(base, seen), :], h)
                    v = one_head(v_ref[pl.ds(base, seen), :], h)
                    scores = dot_nt(q, k).astype(BF16) * mask
                    one = dot(scores, v)
                    total = one if total is None else total + one
                o_ref[rows, :] = total

    return turns.call(
        kernel,
        (end - begin,),
        [
            full_spec((tokens, width)),
            column_spec(tokens, GROUP, begin),
            column_spec(tokens, GROUP, begin),
            full_spec((tokens, 1)),
            full_spec((row_count, 1, block)),
            column_spec(width, GROUP, begin),
            column_spec(width, GROUP, begin),
        ],
        [column_spec(tokens, GROUP)] * 3,
        [shape((tokens, (end - begin) * GROUP), BF16)] * 2 + [shape((tokens, (end - begin) * GROUP), F32)],
        scratch=[pltpu.VMEM((tokens, block), BF16)],
        us=8.3,
    )(normed, keys, values, ids_col, ids_row, w_query, w_outgate)


def combine(turns, parts, inputs, carried, near_ids, ids_col, head_gain, w_output):
    tokens, width = inputs.shape
    row_count = carried.shape[0]
    block = tokens // row_count
    per_row = block // TILE
    number = len(parts)
    per_part = width // GROUP // number

    def kernel(*refs):
        (x_ref, c_ref, near_ref, id_ref, gain_ref, wo_ref) = refs[3 * number : 3 * number + 6]
        (at_ref, go_ref, h_ref, nm_ref) = refs[3 * number + 6 :]
        matched = id_ref[...] == near_ref[0, pl.ds(0, 1), pl.ds(0, 1)]
        ones = head_ones()
        for j in range(width // GROUP):
            q_ref, g_ref, in_ref = refs[3 * (j // per_part) : 3 * (j // per_part) + 3]
            own = pl.ds((j % per_part) * GROUP, GROUP)
            cols = pl.ds(j * GROUP, GROUP)
            state = unpack_state(c_ref[0, pl.ds(j * GROUP // 2, GROUP // 2), :])
            across = dot(q_ref[:, own], state)
            attended = in_ref[:, own] + jnp.where(matched, across, 0.0)
            at_ref[:, cols] = attended.astype(BF16)
            unit = attended * lax.rsqrt(head_mean(attended * attended, ones) + EPSILON)
            go_ref[:, cols] = (unit * gain_ref[:, cols] * g_ref[:, own].astype(F32)).astype(BF16)
        hidden = x_ref[...].astype(F32) + dot(go_ref[...], wo_ref[...])
        h_ref[...] = hidden
        nm_ref[...] = (hidden * lax.rsqrt(mean_square(hidden) + EPSILON)).astype(BF16)

    tile = row_spec(TILE, width)
    return turns.call(
        kernel,
        (tokens // TILE,),
        [row_spec(TILE, width // number)] * (3 * number)
        + [
            tile,
            pl.BlockSpec((1, width // 2, 128), lambda i: (i // per_row, 0, 0)),
            pl.BlockSpec((1, 8, 128), lambda i: (i // per_row, 0, 0)),
            row_spec(TILE, 1),
            full_spec((1, width)),
            full_spec((width, width)),
        ],
        [tile] * 4,
        [shape((tokens, width), BF16)] * 2 + [shape((tokens, width), F32), shape((tokens, width), BF16)],
        us=7.2,
    )(*[a for part in parts for a in part], inputs, carried, near_ids, ids_col, head_gain, w_output)


def back_product(turns, cotangent, w_down):
    tokens, width = cotangent.shape
    wide = w_down.shape[0]

    def kernel(c_ref, w_ref, o_ref):
        o_ref[...] = dot_nt(c_ref[...], w_ref[...]).astype(BF16)

    return turns.call(
        kernel,
        (wide // TILE,),
        [full_spec((tokens, width)), row_spec(TILE, width)],
        column_spec(tokens, TILE),
        shape((tokens, wide), BF16),
        us=8.5,
    )(cotangent, w_down)


def gate_up(turns, normed, w_gate, w_up, back):
    tokens, width = normed.shape
    wide = w_gate.shape[1]

    def kernel(n_ref, wg_ref, wu_ref, b_ref, p_ref, g_ref, u_ref):
        n = n_ref[...]
        gate = dot(n, wg_ref[...])
        up = dot(n, wu_ref[...])
        b = b_ref[...].astype(F32)
        p_ref[...] = (gate * up).astype(BF16)
        g_ref[...] = (b * up).astype(BF16)
        u_ref[...] = (b * gate).astype(BF16)

    tile = column_spec(tokens, TILE)
    return turns.call(
        kernel,
        (wide // TILE,),
        [full_spec((tokens, width)), column_spec(width, TILE), column_spec(width, TILE), tile],
        [tile] * 3,
        [shape((tokens, wide), BF16)] * 3,
        us=18,
    )(normed, w_gate, w_up, back)


def block_output(turns, hidden, product, w_down):
    tokens, width = hidden.shape
    wide = product.shape[1]

    def kernel(h_ref, p_ref, w_ref, o_ref):
        o_ref[...] = (h_ref[...] + dot(p_ref[...], w_ref[...])).astype(BF16)

    return turns.call(
        kernel,
        (tokens // TILE,),
        [row_spec(TILE, width), row_spec(TILE, wide), full_spec((wide, width))],
        row_spec(TILE, width),
        shape((tokens, width), BF16),
        us=9,
    )(hidden, product, w_down)


def norm_back(unit, scale, grad):
    return scale * (grad - unit * jnp.mean(grad * unit, axis=-1, keepdims=True))


def back_mid_heads(
    turns,
    back_gate,
    back_up,
    w_gate,
    w_up,
    cotangent,
    hidden,
    w_output,
    attended,
    parts,
    head_gain,
    first_ids,
    ids_col,
    row_count,
):
    tokens, width = cotangent.shape
    block = tokens // row_count
    per_row = block // TILE
    steps = back_gate.shape[1] // TILE
    number = len(parts)
    per_part = width // GROUP // number

    def kernel(first_ref, *refs):
        (bg_ref, bu_ref, wg_ref, wu_ref, c_ref, h_ref, wo_ref, at_ref, gain_ref, id_ref) = refs[:10]
        q_refs, g_refs = refs[10 : 10 + number], refs[10 + number : 10 + 2 * number]
        (bb_ref, bo_ref, ba_ref, s_ref, acc_ref) = refs[10 + 2 * number :]
        step = pl.program_id(0)

        @pl.when(step == 0)
        def _():
            acc_ref[...] = jnp.zeros_like(acc_ref)

        acc_ref[...] += dot_nt(bg_ref[...], wg_ref[...]) + dot_nt(bu_ref[...], wu_ref[...])

        @pl.when(step == steps - 1)
        def _():
            ones = head_ones()
            gains = [jnp.zeros((1, GROUP), F32)] * (width // GROUP)
            for r in range(row_count):
                sums = [None] * (width // GROUP)
                for i in range(per_row):
                    rows = pl.ds(r * block + i * TILE, TILE)
                    h = h_ref[rows, :]
                    scale = lax.rsqrt(mean_square(h) + EPSILON)
                    back = c_ref[rows, :].astype(F32) + norm_back(h * scale, scale, acc_ref[rows, :])
                    bb_ref[rows, :] = back.astype(BF16)
                    acc_ref[rows, :] = dot_nt(bb_ref[rows, :], wo_ref[...])
                    in_first = id_ref[rows, :] == first_ref[r]
                    for j in range(width // GROUP):
                        cols = pl.ds(j * GROUP, GROUP)
                        own = pl.ds((j % per_part) * GROUP, GROUP)
                        attended = at_ref[rows, cols].astype(F32)
                        scale_h = lax.rsqrt(head_mean(attended * attended, ones) + EPSILON)
                        unit = attended * scale_h
                        gate = g_refs[j // per_part][rows, own].astype(F32)
                        gain = gain_ref[:, cols]
                        gated = acc_ref[rows, cols] * gate
                        along = unit * gated
                        gains[j] = gains[j] + jnp.sum(along, axis=0, keepdims=True)
                        bo_ref[rows, cols] = (along * gain * (1.0 - gate)).astype(BF16)
                        back_unit = gated * gain
                        mean = head_mean(back_unit * unit, ones)
                        ba = (scale_h * (back_unit - unit * mean)).astype(BF16)
                        ba_ref[rows, cols] = ba
                        q = jnp.where(in_first, q_refs[j // per_part][rows, own], jnp.zeros((), BF16))
                        one = dot_tn(q, ba)
                        sums[j] = one if sums[j] is None else sums[j] + one
                for j in range(width // GROUP):
                    s_ref[r, pl.ds(j * GROUP // 2, GROUP // 2), :] = pack_state(sums[j])
                s_ref[r, pl.ds(width // 2, 8), :] = jnp.full((8, 128), first_ref[r])
            s_ref[:, pl.ds(width // 2 + 8, 8), :] = jnp.zeros((row_count, 8, 128), F32)
            for j in range(width // GROUP):
                for p in range(2):
                    s_ref[0, pl.ds(width // 2 + 8 + 2 * j + p, 1), :] = gains[j][:, 128 * p : 128 * p + 128]

    whole = full_spec((tokens, width))
    tile = column_spec(tokens, TILE)
    weights = column_spec(width, TILE)
    return turns.call(
        kernel,
        (steps,),
        [SMEM, tile, tile, weights, weights, whole, whole, full_spec((width, width)), whole, full_spec((1, width))]
        + [full_spec((tokens, 1))]
        + [full_spec((tokens, width // number))] * (2 * number),
        [whole_out((tokens, width))] * 3 + [whole_out((row_count, width // 2 + 16, 128))],
        [shape((tokens, width), BF16)] * 3 + [shape((row_count, width // 2 + 16, 128), F32)],
        scratch=[pltpu.VMEM((tokens, width), F32)],
        us=28,
    )(
        first_ids,
        back_gate,
        back_up,
        w_gate,
        w_up,
        cotangent,
        hidden,
        w_output,
        attended,
        head_gain,
        ids_col,
        *[part[0] for part in parts],
        *[part[1] for part in parts],
    )


def attend_back(turns, queries, keys, values, back_attended, carried, near_ids, ids_col, ids_row, begin):
    tokens, width = queries.shape
    row_count, _, block = ids_row.shape

    def kernel(near_ref, q_ref, k_ref, v_ref, a_ref, c_ref, ic_ref, ir_ref, bq_ref, bk_ref, bv_ref, mask_ref, flip_ref):
        @pl.when(pl.program_id(0) == 0)
        def _():
            for r in range(row_count):
                for i in range(block // TILE):
                    at = pl.ds(r * block + i * TILE, TILE)
                    mask_ref[at, :] = block_mask(ic_ref[at, :], ir_ref[r], i * TILE, False)
                    flip_ref[at, :] = block_mask(ic_ref[at, :], ir_ref[r], i * TILE, True)

        for r in range(row_count):
            base = r * block
            state = unpack_state(c_ref[r])
            for i in range(block // TILE):
                rows = pl.ds(base + i * TILE, TILE)
                seen = (i + 1) * TILE
                earlier = pl.ds(base, seen)
                later = pl.ds(base + i * TILE, block - i * TILE)
                a = a_ref[rows, :]
                q = q_ref[rows, :]
                k = k_ref[rows, :]
                v = v_ref[rows, :]
                matched = ic_ref[rows, :] == near_ref[r, pl.ds(0, 1), pl.ds(0, 1)]
                back_q = jnp.where(matched, dot_nt(a, state), 0.0)
                back_k = None
                back_v = None
                mask = mask_ref[rows, pl.ds(0, seen)]
                flip = flip_ref[rows, pl.ds(i * TILE, block - i * TILE)]
                for h in range(4):
                    grads = dot_nt(a, one_head(v_ref[earlier, :], h)).astype(BF16) * mask
                    back_q = back_q + dot(grads, one_head(k_ref[earlier, :], h))
                    q_h = one_head(q_ref[later, :], h)
                    a_h = one_head(a_ref[later, :], h)
                    scores_t = dot_nt(k, q_h).astype(BF16) * flip
                    grads_t = dot_nt(v, a_h).astype(BF16) * flip
                    one = dot(grads_t, q_h)
                    back_k = one if back_k is None else back_k + one
                    one = dot(scores_t, a_h)
                    back_v = one if back_v is None else back_v + one
                bq_ref[rows, :] = (back_q * sigmoid_of_softplus(q.astype(F32))).astype(BF16)
                bk_ref[rows, :] = back_k
                bv_ref[rows, :] = back_v

    tile = column_spec(tokens, GROUP)
    there = column_spec(tokens, GROUP, begin)
    return turns.call(
        kernel,
        (width // GROUP,),
        [full_spec((row_count, 8, 128)), tile, there, there, there]
        + [pl.BlockSpec((row_count, GROUP // 2, 128), lambda j: (0, j + begin, 0))]
        + [full_spec((tokens, 1)), full_spec((row_count, 1, block))],
        [tile] * 3,
        [shape((tokens, width), BF16)] + [shape((tokens, width), F32)] * 2,
        scratch=[pltpu.VMEM((tokens, block), BF16)] * 2,
        us=14,
    )(near_ids, queries, keys, values, back_attended, carried, ids_col, ids_row)


def finish_keys(turns, parts, keys, values, state_grad, ids_col):
    tokens, width = keys.shape
    row_count = state_grad.shape[0]
    block = tokens // row_count

    number = len(parts)
    per_part = width // GROUP // number

    def kernel(near_ref, k_ref, v_ref, s_ref, id_ref, *refs):
        ok_ref, ov_ref = refs[2 * number :]
        for i in range(number):

            @pl.when(pl.program_id(0) // per_part == i)
            def _(i=i):
                work(near_ref, k_ref, v_ref, s_ref, id_ref, refs[2 * i], refs[2 * i + 1], ok_ref, ov_ref)

    def work(near_ref, k_ref, v_ref, s_ref, id_ref, bk_ref, bv_ref, ok_ref, ov_ref):
        for r in range(row_count):
            rows = pl.ds(r * block, block)
            state = unpack_state(s_ref[r])
            uses = id_ref[rows, :] == near_ref[r, pl.ds(0, 1), pl.ds(0, 1)]
            k = k_ref[rows, :]
            back_k = bk_ref[rows, :] + jnp.where(uses, dot_nt(v_ref[rows, :], state), 0.0)
            ok_ref[rows, :] = (back_k * sigmoid_of_softplus(k.astype(F32))).astype(BF16)
            ov_ref[rows, :] = (bv_ref[rows, :] + jnp.where(uses, dot(k, state), 0.0)).astype(BF16)

    tile = column_spec(tokens, GROUP)

    def part(i):
        return pl.BlockSpec((tokens, GROUP), lambda j: (0, jnp.clip(j - i * per_part, 0, per_part - 1)))

    return turns.call(
        kernel,
        (width // GROUP,),
        [pl.BlockSpec((row_count, 8, 128), lambda j: (0, width // 16, 0)), tile, tile]
        + [pl.BlockSpec((row_count, GROUP // 2, 128), lambda j: (0, j, 0)), full_spec((tokens, 1))]
        + [part(i) for i in range(number) for _ in range(2)],
        [tile] * 2,
        [shape((tokens, width), BF16)] * 2,
        us=5,
    )(state_grad, keys, values, state_grad, ids_col, *[a for part in parts for a in part])


def input_gradient(turns, back_query_parts, grads, weights, inputs, back_branch):
    tokens, width = inputs.shape
    number = len(back_query_parts)
    narrow = width // number

    def kernel(*refs):
        q_refs, g_refs = refs[:number], refs[number : number + len(grads)]
        w_refs = refs[number + len(grads) : -3]
        x_ref, bb_ref, o_ref = refs[-3:]
        back = None
        for i, q_ref in enumerate(q_refs):
            one = dot_nt(q_ref[...], w_refs[0][:, pl.ds(i * narrow, narrow)])
            back = one if back is None else back + one
        for g_ref, w_ref in zip(g_refs, w_refs[1:]):
            back = back + dot_nt(g_ref[...], w_ref[...])
        x = x_ref[...].astype(F32)
        scale = lax.rsqrt(mean_square(x) + EPSILON)
        o_ref[...] = (bb_ref[...].astype(F32) + norm_back(x * scale, scale, back)).astype(BF16)

    tile = row_spec(TILE, width)
    return turns.call(
        kernel,
        (tokens // TILE,),
        [row_spec(TILE, narrow)] * number
        + [tile] * len(grads)
        + [full_spec((width, width))] * len(weights)
        + [tile] * 2,
        tile,
        shape((tokens, width), BF16),
        us=13,
    )(*back_query_parts, *grads, *weights, inputs, back_branch)


def local(
    inputs,
    doc_ids,
    w_query,
    w_key,
    w_value,
    w_outgate,
    w_output,
    w_gate,
    w_up,
    w_down,
    head_gain,
    cotangent,
):
    row_count, block_len, width = inputs.shape
    tokens = row_count * block_len
    x_first, y_first, z_order = orders(lax.axis_size("seq"))
    core = lax.axis_index("batch").astype(jnp.int32).reshape(1)
    x_flat = inputs.reshape(tokens, width)
    cot_flat = cotangent.reshape(tokens, width)
    gain = head_gain.reshape(1, width)
    ids = doc_ids.astype(F32)
    ids_col = ids.reshape(tokens, 1)
    ids_row = ids.reshape(row_count, 1, block_len)
    first_ids, last_ids = ids[:, 0], ids[:, -1]
    groups = width // GROUP

    turns = Turns()

    normed, keys, values, state = project_keys(turns, x_flat, ids_col, last_ids, w_key, w_value, row_count)
    before = Prefix(turns, state, doc_ids[:, -1], False)
    part_a = attend(turns, normed, keys, values, ids_col, ids_row, w_query, w_outgate, 0, groups // 2)
    before.pass_on()
    part_b = attend(turns, normed, keys, values, ids_col, ids_row, w_query, w_outgate, groups // 2, groups)
    before.swap_back()
    back = back_product(turns, cot_flat, w_down)
    carried, before_ids = before.join()
    parts = (part_a, part_b)
    attended, gated, hidden, normed_mid = combine(
        turns, parts, x_flat, carried, before_ids, ids_col, gain, w_output
    )
    product, back_gate, back_up = gate_up(turns, normed_mid, w_gate, w_up, back)

    down_sent, down_kept = grad_halves(turns, [(product, cot_flat)], core, 512, us=12)
    down_got = to_core(down_sent)
    gate_sent, gate_kept = grad_halves(turns, [(normed_mid, back_gate)], core, 1408, us=12)
    gate_got = to_core(gate_sent)
    up_sent, up_kept = grad_halves(turns, [(normed_mid, back_up)], core, 1408, us=12)
    up_got = to_core(up_sent)
    down = Scatter(turns, [down_kept, down_got], x_first)
    down.step()
    gate = Scatter(turns, [gate_kept, gate_got], y_first)
    gate.step()
    up = Scatter(turns, [up_kept, up_got], z_order + x_first)
    up.step()
    back_branch, back_outgate, back_attended, state_out = back_mid_heads(
        turns,
        back_gate,
        back_up,
        w_gate,
        w_up,
        cot_flat,
        hidden,
        w_output,
        attended,
        parts,
        gain,
        first_ids,
        ids_col,
        row_count,
    )
    scan = Scan(turns, state_out, True)
    scan.send()
    out_sent, out_kept = grad_halves(
        turns, [(gated, back_branch), (normed, back_outgate)], core, 512, us=10
    )
    out_got = to_core(out_sent)

    def within(i):
        return attend_back(
            turns, parts[i][0], keys, values, back_attended, carried, before_ids, ids_col, ids_row, i * groups // 2
        )

    back_a = within(0)
    scan.take()
    scan.send()
    outer = Scatter(turns, [out_kept, out_got], x_first + z_order)
    outer.step()
    back_b = within(1)
    scan.take()
    scan.send()
    down.step()
    q_sent, q_kept = grad_halves(turns, [(normed, back_a[0]), (normed, back_b[0])], core, 512, us=6)
    q_got = to_core(q_sent)
    scan.take()
    scan.send()
    up.step()
    gate.step()
    block_out = block_output(turns, hidden, product, w_down).reshape(inputs.shape)
    scan.take()
    back_key, back_value = finish_keys(
        turns, (back_a[1:], back_b[1:]), keys, values, scan.result, ids_col
    )
    query = Scatter(turns, [q_kept, q_got], y_first + z_order)
    query.step()
    kv_sent, kv_kept = grad_halves(turns, [(normed, back_key), (normed, back_value)], core, 512, True, us=10)
    kv_got = to_core(kv_sent)
    grad_down = down.finish_planes()
    outer.step()
    key = Scatter(turns, [kv_kept[:1], kv_got[:1]], x_first + z_order)
    key.step()
    value = Scatter(turns, [kv_kept[1:], kv_got[1:]], y_first + z_order)
    value.step()
    input_grad = input_gradient(
        turns,
        (back_a[0], back_b[0]),
        (back_key, back_value, back_outgate),
        (w_query, w_key, w_value, w_outgate),
        x_flat,
        back_branch,
    ).reshape(inputs.shape)
    up.step()
    grad_gate = gate.finish_planes()
    outer.step()
    query.step()
    key.step()
    value.step()
    up.step()
    outer.step()
    query.step()
    key.step()
    value.step()
    (grad_up,) = up.finish(w_gate.shape[1])
    grad_output, grad_outgate = outer.finish(width, width)
    query.step()
    key.step()
    value.step()
    (grad_query,) = query.finish(width)
    (grad_key,) = key.finish(width)
    (grad_value,) = value.finish(width)
    gain_sum = scan.result[0, -8:]
    gain_sum = (gain_sum + to_core([gain_sum])[0]).reshape(width)
    share = width // (2 * lax.axis_size("seq"))
    place = lax.axis_index("batch") * lax.axis_size("seq") + lax.axis_index("seq")
    grad_gain = lax.dynamic_slice_in_dim(gain_sum, place * share, share)
    return (
        block_out,
        input_grad,
        grad_query,
        grad_key,
        grad_value,
        grad_outgate,
        grad_output,
        grad_gate,
        grad_up,
        grad_down,
        grad_gain,
    )


def solution(mesh):
    rows = P("batch", "seq", None)
    scattered = P(("batch", "seq"), None)
    return jax.shard_map(
        local,
        mesh=mesh,
        in_specs=(rows, P("batch", "seq")) + (P(),) * 9 + (rows,),
        out_specs=(rows, rows) + (scattered,) * 8 + (P(("batch", "seq")),),
        check_vma=False,
    )
```

time: 673 us -> 495 us (0.74)
  waiting for transfers between devices: 191 us -> 80.1 us
  Pallas kernels: 291 us -> 343 us
  other arithmetic: 51 us -> 1.96 us
  starting transfers between devices: 90.8 us -> 42.5 us
  local copies, waits for them, and re-layouts: 37.3 us -> 5.05 us
  between operations: 1.7 us -> 14.5 us
    ppermute x63 -> x39, waiting for transfers between devices: 184 us -> 80 us  [the longest x4 44.6 us: send(): lax.ppermute(self.payload, 'seq', [(i, i ^ flip) for i in range(self.coun...]
    pallas_call x35 -> x57, Pallas kernels: 291 us -> 343 us  [run(): pl.pallas_call(body, grid_spec=spec, out_shape=out_shape, compiler_params...]
    add x39 -> x0, other arithmetic: 45.6 us -> none  [the longest x38 45.6 us: sum_pieces(): total = one if total is None else total + one]
    ppermute x63 -> x39, starting transfers between devices: 76.9 us -> 34.5 us  [the longest x24 20 us: step(): lax.ppermute(outgoing, 'seq', [(i, i ^ flip) for i in range(self.count)])]
    reshape x14 -> x0, local copies, waits for them, and re-layouts: 20.2 us -> none  [the longest x10 19.6 us: piece(): return taken.reshape((2,) * left + tuple(sizes[held:]))]
    unnamed x91 -> x6, local copies, waits for them, and re-layouts: 9.85 us -> 1.05 us
    ppermute x12 -> x6, starting transfers between devices: 14 us -> 7.94 us  [swap(): lax.ppermute(shares[k], 'seq', [(i, i // plane * plane + (i % plane ^ k))...]
  transfers between devices with their start and end apart: 75 -> 47, of which waited for: 29 -> 11; matrix products, arithmetic and copies ran while one was open for 11% -> 1% of each run, Pallas kernels for 30% -> 57%
where the time goes in v3:
time: 495 us; the launch traced here: 487 us
  Pallas kernels  343 us (69%)
  waiting for transfers between devices  80.1 us (16%)
  starting transfers between devices  42.5 us (9%)
  between operations  14.5 us (3%)
  local copies, waits for them, and re-layouts  5.05 us (1%)
    pallas_call x57, Pallas kernels, run(): pl.pallas_call(body, grid_spec=spec, out_shape=out_shape, compiler_params...  343 us
    ppermute x4, waiting for transfers between devices, send(): lax.ppermute(self.payload, 'seq', [(i, i ^ flip) for i in range(self.coun...  44.6 us
    ppermute x24, waiting for transfers between devices, step(): lax.ppermute(outgoing, 'seq', [(i, i ^ flip) for i in range(self.count)])  35.4 us
    ppermute x24, starting transfers between devices, step(): lax.ppermute(outgoing, 'seq', [(i, i ^ flip) for i in range(self.count)])  20 us
    ppermute x3, starting transfers between devices, pass_on(): self.passed.append(lax.ppermute(total_share, 'seq', moves))  11.2 us
  transfers between devices with their start and end apart: 47, of which 11 were waited for; matrix products, arithmetic and copies ran while one was open for 1% of the time, Pallas kernels for 57%

profile of v3, /device:TPU:0, one launch (start us, length us, event | category | flops | bytes accessed | tf_op | source)
XLA Modules:
  0.0 487.1 jit_solution(16308264687585008533)
XLA Ops:
  11.1 11.3 %shard_map.203 = (bf16[1024,1024]{1,0:T(8,128)(2,1)}, bf16[1024,1024]{1,0:T(8,128)(2,1)}, bf16[1024,1024]{1,0:T(8,128)(2,1)}, f32[2,512,128]{2,1,0:T(8,128)}) custom-call(f32[2]{0:T(128)} %get-tuple-element.134.refs_0_, bf16[1024,1024]{1,0:T(8,128)(2,1)} %bitcast.54, f32[1024,1]{1,0:T(8,128)} %bitcast.42, bf16[1024,1024]{1,0:T(8,128)(2,1)} %refs_6_.5, ...), custom_call_target="tpu_custom_call" | custom-call | flops 950000025600 | tf_op jit(solution)/shard_map/pallas_call | solution.py:163
  24.3 2.9 collective-permute-start
  29.4 11.2 %shard_map.205 = (bf16[1024,512]{1,0:T(8,128)(2,1)}, bf16[1024,512]{1,0:T(8,128)(2,1)}, f32[1024,512]{1,0:T(8,128)}) custom-call(bf16[1024,1024]{1,0:T(8,128)(2,1)} %get-tuple-element.72.refs_2_.refs_0_.refs_3_.refs_4_.refs_1_, bf16[1024,1024]{1,0:T(8,128)(2,1)} %get-tuple-element.73.refs_1_.refs_2_, bf16[1024,1024]{1,0:T(8,128)(2,1)} %get-tuple-element.74.refs_2_.refs_3_, ...), custom_call_target="tpu_custom_call" | custom-call | flops 830000005120 | tf_op jit(solution)/shard_map/pallas_call | solution.py:163
  42.4 4.6 collective-permute-start.3
  47.0 4.5 collective-permute-start.4
  53.7 11.3 %shard_map.207 = (bf16[1024,512]{1,0:T(8,128)(2,1)}, bf16[1024,512]{1,0:T(8,128)(2,1)}, f32[1024,512]{1,0:T(8,128)}) custom-call(bf16[1024,1024]{1,0:T(8,128)(2,1)} %get-tuple-element.72.refs_2_.refs_0_.refs_3_.refs_4_.refs_1_, bf16[1024,1024]{1,0:T(8,128)(2,1)} %get-tuple-element.73.refs_1_.refs_2_, bf16[1024,1024]{1,0:T(8,128)(2,1)} %get-tuple-element.74.refs_2_.refs_3_, ...), custom_call_target="tpu_custom_call" | custom-call | flops 830000005120 | tf_op jit(solution)/shard_map/pallas_call | solution.py:163
  70.7 13.4 %shard_map.209.refs_5_.refs_3_ = bf16[1024,2816]{1,0:T(8,128)(2,1)} custom-call(bf16[1024,1024]{1,0:T(8,128)(2,1)} %bitcast.51, bf16[2816,1024]{1,0:T(8,128)(2,1)} %refs_2_.3, f32[2,136,128]{2,1,0:T(8,128)} %get-tuple-element.86.refs_2_.refs_1_), custom_call_target="tpu_custom_call" | custom-call | flops 850000019456 | tf_op jit(solution)/shard_map/pallas_call | solution.py:163
  86.1 12.1 %shard_map.211 = (bf16[1024,1024]{1,0:T(8,128)(2,1)}, bf16[1024,1024]{1,0:T(8,128)(2,1)}, f32[1024,1024]{1,0:T(8,128)}, bf16[1024,1024]{1,0:T(8,128)(2,1)}) custom-call(bf16[1024,512]{1,0:T(8,128)(2,1)} %get-tuple-element.77.refs_5_.refs_0_.refs_11_.refs_1_, bf16[1024,512]{1,0:T(8,128)(2,1)} %get-tuple-element.78.refs_1_.refs_13_, ...), custom_call_target="tpu_custom_call" | custom-call | flops 719999991808 | tf_op jit(solution)/shard_map/pallas_call | solution.py:163
  98.2 21.0 %shard_map.212 = (bf16[1024,2816]{1,0:T(8,128)(2,1)}, bf16[1024,2816]{1,0:T(8,128)(2,1)}, bf16[1024,2816]{1,0:T(8,128)(2,1)}) custom-call(bf16[1024,1024]{1,0:T(8,128)(2,1)} %get-tuple-element.93.refs_0_.refs_1_.refs_2_, bf16[1024,2816]{1,0:T(8,128)(2,1)} %refs_3_.3, bf16[1024,2816]{1,0:T(8,128)(2,1)} %refs_4_.3, ...), custom_call_target="tpu_custom_call" | custom-call | flops 1799999979520 | tf_op jit(solution)/shard_map/pallas_call | solution.py:163
  119.2 12.0 %shard_map.213 = (f32[1408,1024]{1,0:T(8,128)}, f32[1408,1024]{1,0:T(8,128)}) custom-call(s32[1]{0:T(128)} %bitcast.6.refs_0_, bf16[1024,2816]{1,0:T(8,128)(2,1)} %get-tuple-element.95.refs_1_.refs_2_.refs_4_, bf16[1024,2816]{1,0:T(8,128)(2,1)} %get-tuple-element.95.refs_1_.refs_2_.refs_4_, bf16[1024,1024]{1,0:T(8,128)(2,1)} %bitcast.52, ...), custom_call_target="tpu_custom_call" | custom-call | flops 1199999942656 | tf_op jit(solution)/shard_map/pallas_call | solution.py:163
  131.2 11.9 %shard_map.214 = (f32[512,2816]{1,0:T(8,128)}, f32[512,2816]{1,0:T(8,128)}) custom-call(s32[1]{0:T(128)} %bitcast.6.refs_0_, bf16[1024,1024]{1,0:T(8,128)(2,1)} %get-tuple-element.93.refs_0_.refs_1_.refs_2_, bf16[1024,1024]{1,0:T(8,128)(2,1)} %get-tuple-element.93.refs_0_.refs_1_.refs_2_, bf16[1024,2816]{1,0:T(8,128)(2,1)} %get-tuple-element.96.refs_3_.refs_1_, ...), custom_call_target="tpu_custom_call" | custom-call | flops 1199999942656 | tf_op jit(solution)/shard_map/pallas_call | solution.py:163
  143.6 12.1 %shard_map.215 = (f32[512,2816]{1,0:T(8,128)}, f32[512,2816]{1,0:T(8,128)}) custom-call(s32[1]{0:T(128)} %bitcast.6.refs_0_, bf16[1024,1024]{1,0:T(8,128)(2,1)} %get-tuple-element.93.refs_0_.refs_1_.refs_2_, bf16[1024,1024]{1,0:T(8,128)(2,1)} %get-tuple-element.93.refs_0_.refs_1_.refs_2_, bf16[1024,2816]{1,0:T(8,128)(2,1)} %get-tuple-element.101.refs_3_.refs_2_, ...), custom_call_target="tpu_custom_call" | custom-call | flops 1199999942656 | tf_op jit(solution)/shard_map/pallas_call | solution.py:163
  155.7 4.0 shard_map.216.refs_9_
  161.2 4.0 shard_map.217.refs_9_
  166.7 4.0 shard_map.218.refs_15_
  170.8 33.8 %shard_map.219 = (bf16[1024,1024]{1,0:T(8,128)(2,1)}, bf16[1024,1024]{1,0:T(8,128)(2,1)}, bf16[1024,1024]{1,0:T(8,128)(2,1)}, f32[2,528,128]{2,1,0:T(8,128)}) custom-call(f32[2]{0:T(128)} %get-tuple-element.133.refs_0_, bf16[1024,2816]{1,0:T(8,128)(2,1)} %get-tuple-element.96.refs_3_.refs_1_, bf16[1024,2816]{1,0:T(8,128)(2,1)} %get-tuple-element.101.refs_3_.refs_2_, ...), custom_call_target="tpu_custom_call" | custom-call | flops 2799999909888 | tf_op jit(solution)/shard_map/pallas_call | solution.py:163
  205.2 10.1 %shard_map.220 = (f32[512,2048]{1,0:T(8,128)}, f32[512,2048]{1,0:T(8,128)}) custom-call(s32[1]{0:T(128)} %bitcast.6.refs_0_, bf16[1024,1024]{1,0:T(8,128)(2,1)} %get-tuple-element.106.refs_1_.refs_2_, bf16[1024,1024]{1,0:T(8,128)(2,1)} %get-tuple-element.106.refs_1_.refs_2_, bf16[1024,1024]{1,0:T(8,128)(2,1)} %get-tuple-element.72.refs_2_.refs_0_.refs_3_.refs_4_.refs_1_, ...), custom_call_target="tpu_custom_call" | custom-call | flops 999999995904 | tf_op jit(solution)/shard_map/pallas_call | solution.py:163
  215.3 16.8 %shard_map.221 = (bf16[1024,512]{1,0:T(8,128)(2,1)}, f32[1024,512]{1,0:T(8,128)}, f32[1024,512]{1,0:T(8,128)}) custom-call(f32[2,8,128]{2,1,0:T(8,128)} %get-tuple-element.91.refs_8_.refs_0_, bf16[1024,512]{1,0:T(8,128)(2,1)} %get-tuple-element.77.refs_5_.refs_0_.refs_11_.refs_1_, bf16[1024,1024]{1,0:T(8,128)(2,1)} %get-tuple-element.73.refs_1_.refs_2_, ...), custom_call_target="tpu_custom_call" | custom-call | flops 1399999954944 | tf_op jit(solution)/shard_map/pallas_call | solution.py:163
  232.0 4.4 collective-permute-done.14.refs_2_
  240.3 3.3 shard_map.223.refs_8_
  243.6 16.5 %shard_map.224 = (bf16[1024,512]{1,0:T(8,128)(2,1)}, f32[1024,512]{1,0:T(8,128)}, f32[1024,512]{1,0:T(8,128)}) custom-call(f32[2,8,128]{2,1,0:T(8,128)} %get-tuple-element.91.refs_8_.refs_0_, bf16[1024,512]{1,0:T(8,128)(2,1)} %get-tuple-element.83.refs_8_.refs_3_.refs_12_.refs_1_, bf16[1024,1024]{1,0:T(8,128)(2,1)} %get-tuple-element.73.refs_1_.refs_2_, ...), custom_call_target="tpu_custom_call" | custom-call | flops 1399999954944 | tf_op jit(solution)/shard_map/pallas_call | solution.py:163
  260.1 2.5 shard_map.225
  262.7 3.2 shard_map.226.refs_5_
  265.9 6.3 %shard_map.227 = (f32[512,1024]{1,0:T(8,128)}, f32[512,1024]{1,0:T(8,128)}) custom-call(s32[1]{0:T(128)} %bitcast.6.refs_0_, bf16[1024,1024]{1,0:T(8,128)(2,1)} %get-tuple-element.72.refs_2_.refs_0_.refs_3_.refs_4_.refs_1_, bf16[1024,1024]{1,0:T(8,128)(2,1)} %get-tuple-element.72.refs_2_.refs_0_.refs_3_.refs_4_.refs_1_, ...), custom_call_target="tpu_custom_call" | custom-call | flops 599999971328 | tf_op jit(solution)/shard_map/pallas_call | solution.py:163
  274.1 2.4 collective-permute-done.17.refs_2_
  276.6 2.5 shard_map.228
  279.0 3.2 shard_map.229.refs_7_
  282.3 2.9 collective-permute-start.28
  285.2 3.2 shard_map.230.refs_3_
  288.4 11.1 %shard_map.231.refs_4_ = bf16[1024,1024]{1,0:T(8,128)(2,1)} custom-call(f32[1024,1024]{1,0:T(8,128)} %get-tuple-element.92.refs_6_.refs_0_, bf16[1024,2816]{1,0:T(8,128)(2,1)} %get-tuple-element.95.refs_1_.refs_2_.refs_4_, bf16[2816,1024]{1,0:T(8,128)(2,1)} %refs_2_.3, f32[4,32,2816]{2,1,0:T(8,128)} %shard_map.230.refs_3_), custom_call_target="tpu_custom_call" | custom-call | flops 899999989760 | tf_op jit(solution)/shard_map/pallas_call | solution.py:163
  299.5 37.7 %collective-permute-done.19.refs_2_ = f32[2,528,128]{2,1,0:T(8,128)} collective-permute-done((f32[2,528,128]{2,1,0:T(8,128)}, f32[2,528,128]{2,1,0:T(8,128)}, u32[]{:S(2)}, u32[]{:S(2)}) %collective-permute-start.19) | collective-permute-done | bytes 540704 | tf_op jit(solution)/shard_map/ppermute | solution.py:380
  340.7 9.0 %shard_map.233 = (bf16[1024,1024]{1,0:T(8,128)(2,1)}, bf16[1024,1024]{1,0:T(8,128)(2,1)}) custom-call(f32[2,528,128]{2,1,0:T(8,128)} %shard_map.232.refs_0_.refs_3_.refs_9_, bf16[1024,1024]{1,0:T(8,128)(2,1)} %get-tuple-element.73.refs_1_.refs_2_, bf16[1024,1024]{1,0:T(8,128)(2,1)} %get-tuple-element.74.refs_2_.refs_3_, ...), custom_call_target="tpu_custom_call" | custom-call | flops 499999997952 | tf_op jit(solution)/shard_map/pallas_call | solution.py:163
  352.5 2.6 shard_map.234.refs_5_
  355.6 9.6 %shard_map.235 = (f32[512,1024]{1,0:T(8,128)}, f32[512,1024]{1,0:T(8,128)}, f32[512,1024]{1,0:T(8,128)}, f32[512,1024]{1,0:T(8,128)}) custom-call(s32[1]{0:T(128)} %bitcast.6.refs_0_, bf16[1024,1024]{1,0:T(8,128)(2,1)} %get-tuple-element.72.refs_2_.refs_0_.refs_3_.refs_4_.refs_1_, ...), custom_call_target="tpu_custom_call" | custom-call | flops 999999995904 | tf_op jit(solution)/shard_map/pallas_call | solution.py:163
  365.3 3.7 shard_map.236.refs_7_
  369.5 2.8 shard_map.237.refs_9_
  373.9 2.5 shard_map.238.refs_9_
  377.0 2.5 shard_map.239.refs_11_
  379.5 16.2 %shard_map.240.refs_5_ = bf16[1024,1024]{1,0:T(8,128)(2,1)} custom-call(bf16[1024,512]{1,0:T(8,128)(2,1)} %get-tuple-element.110.refs_3_.refs_0_, bf16[1024,512]{1,0:T(8,128)(2,1)} %get-tuple-element.114.refs_4_.refs_1_, bf16[1024,1024]{1,0:T(8,128)(2,1)} %get-tuple-element.124.refs_9_.refs_3_.refs_2_, ...), custom_call_target="tpu_custom_call" | custom-call | flops 1300000014336 | tf_op jit(solution)/shard_map/pallas_call | solution.py:163
  396.6 2.6 shard_map.241.refs_9_
  400.3 3.7 shard_map.242.refs_5_
  412.9 13.5 %collective-permute-done.32.refs_5_.refs_6_.refs_3_ = f32[8,32,1024]{2,1,0:T(8,128)} collective-permute-done((f32[8,32,1024]{2,1,0:T(8,128)}, f32[8,32,1024]{2,1,0:T(8,128)}, u32[]{:S(2)}, u32[]{:S(2)}) %collective-permute-start.32) | collective-permute-done | bytes 1048608 | tf_op jit(solution)/shard_map/ppermute | solution.py:128
  440.3 4.1 collective-permute-done.37.refs_4_
  446.4 2.4 shard_map.252.refs_7_
  448.7 3.6 collective-permute-done.35.refs_6_
  456.5 3.4 collective-permute-done.41.refs_5_
  462.1 6.1 %collective-permute-done.40.refs_5_ = f32[2,32,1024]{2,1,0:T(8,128)} collective-permute-done((f32[2,32,1024]{2,1,0:T(8,128)}, f32[2,32,1024]{2,1,0:T(8,128)}, u32[]{:S(2)}, u32[]{:S(2)}) %collective-permute-start.40) | collective-permute-done | bytes 262176 | tf_op jit(solution)/shard_map/ppermute | solution.py:128
  474.4 3.7 collective-permute-done.43.refs_6_
  (119 shorter events, 80.7 us)
Async XLA Ops:
  7.2 472.9 %reduce-scatter.5.cloned.1.call-start = ((), (), s32[]{:S(2)}) async-start(), calls=%async_computation.3 | async-start | bytes 1802240 | tf_op jit(solution)/shard_map/reduce_scatter | solution.py:244
  8.8 13.6 %copy-start = (f32[2,512]{1,0:T(2,128)}, f32[2,512]{1,0:T(2,128)S(1)}, u32[]{:S(2)}) copy-start(f32[2,512]{1,0:T(2,128)S(1)} %get-tuple-element.136) | copy-start | bytes 12292
  24.3 16.3 %collective-permute-start = (f32[2,136,128]{2,1,0:T(8,128)}, f32[2,136,128]{2,1,0:T(8,128)}, u32[]{:S(2)}, u32[]{:S(2)}) collective-permute-start(f32[2,136,128]{2,1,0:T(8,128)} %get-tuple-element.80), channel_id=1, source_target_pairs={{0,1},{1,0},{2,3},{3,2},{4,5},{5,4},{6,7},{7,6},{8,9},{9,8},{10,11... | collective-permute-start | bytes 417800 | tf_op jit(solution)/shard_map/ppermute | solution.py:284
  27.3 13.3 %collective-permute-start.1 = (f32[2,136,128]{2,1,0:T(8,128)}, f32[2,136,128]{2,1,0:T(8,128)}, u32[]{:S(2)}, u32[]{:S(2)}) collective-permute-start(f32[2,136,128]{2,1,0:T(8,128)} %get-tuple-element.81), channel_id=1, source_target_pairs={{0,2},{1,3},{2,0},{3,1},{4,6},{5,7},{6,4},{7,5},{8,10},{9,11},{10,... | collective-permute-start | bytes 417800 | tf_op jit(solution)/shard_map/ppermute | solution.py:284
  28.8 11.8 %collective-permute-start.2 = (f32[2,136,128]{2,1,0:T(8,128)}, f32[2,136,128]{2,1,0:T(8,128)}, u32[]{:S(2)}, u32[]{:S(2)}) collective-permute-start(f32[2,136,128]{2,1,0:T(8,128)} %get-tuple-element.82), channel_id=1, source_target_pairs={{0,3},{1,2},{2,1},{3,0},{4,7},{5,6},{6,5},{7,4},{8,11},{9,10},{10,... | collective-permute-start | bytes 417800 | tf_op jit(solution)/shard_map/ppermute | solution.py:284
  42.4 22.5 %collective-permute-start.3 = (f32[2,136,128]{2,1,0:T(8,128)}, f32[2,136,128]{2,1,0:T(8,128)}, u32[]{:S(2)}, u32[]{:S(2)}) collective-permute-start(f32[2,136,128]{2,1,0:T(8,128)} %shard_map.206.refs_7_), channel_id=1, source_target_pairs={{0,4},{1,5},{2,6},{3,7},{4,8},{5,9},{6,10},{7,11},{8,12},{9,13},{1... | collective-permute-start | bytes 417800 | tf_op jit(solution)/shard_map/ppermute | solution.py:315
  47.0 17.9 %collective-permute-start.4 = (f32[2,136,128]{2,1,0:T(8,128)}, f32[2,136,128]{2,1,0:T(8,128)}, u32[]{:S(2)}, u32[]{:S(2)}) collective-permute-start(f32[2,136,128]{2,1,0:T(8,128)} %shard_map.206.refs_7_), channel_id=1, source_target_pairs={{0,8},{1,9},{2,10},{3,11},{4,12},{5,13},{6,14},{7,15},{16,24},{17,... | collective-permute-start | bytes 417800 | tf_op jit(solution)/shard_map/ppermute | solution.py:315
  51.6 13.4 %collective-permute-start.5 = (f32[2,136,128]{2,1,0:T(8,128)}, f32[2,136,128]{2,1,0:T(8,128)}, u32[]{:S(2)}, u32[]{:S(2)}) collective-permute-start(f32[2,136,128]{2,1,0:T(8,128)} %shard_map.206.refs_7_), channel_id=1, source_target_pairs={{0,12},{1,13},{2,14},{3,15},{16,28},{17,29},{18,30},{19,31}} | collective-permute-start | bytes 417800 | tf_op jit(solution)/shard_map/ppermute | solution.py:315
  67.2 16.9 %collective-permute-start.6 = (f32[2,136,128]{2,1,0:T(8,128)}, f32[2,136,128]{2,1,0:T(8,128)}, u32[]{:S(2)}, u32[]{:S(2)}) collective-permute-start(f32[2,136,128]{2,1,0:T(8,128)} %get-tuple-element.87), channel_id=1, source_target_pairs={{0,1},{1,0},{2,3},{3,2},{4,5},{5,4},{6,7},{7,6},{8,9},{9,8},{10,11... | collective-permute-start | bytes 417800 | tf_op jit(solution)/shard_map/ppermute | solution.py:284
  68.7 15.4 %collective-permute-start.7 = (f32[2,136,128]{2,1,0:T(8,128)}, f32[2,136,128]{2,1,0:T(8,128)}, u32[]{:S(2)}, u32[]{:S(2)}) collective-permute-start(f32[2,136,128]{2,1,0:T(8,128)} %get-tuple-element.88), channel_id=1, source_target_pairs={{0,2},{1,3},{2,0},{3,1},{4,6},{5,7},{6,4},{7,5},{8,10},{9,11},{10,... | collective-permute-start | bytes 417800 | tf_op jit(solution)/shard_map/ppermute | solution.py:284
  70.2 13.9 %collective-permute-start.8 = (f32[2,136,128]{2,1,0:T(8,128)}, f32[2,136,128]{2,1,0:T(8,128)}, u32[]{:S(2)}, u32[]{:S(2)}) collective-permute-start(f32[2,136,128]{2,1,0:T(8,128)} %get-tuple-element.89), channel_id=1, source_target_pairs={{0,3},{1,2},{2,1},{3,0},{4,7},{5,6},{6,5},{7,4},{8,11},{9,10},{10,... | collective-permute-start | bytes 417800 | tf_op jit(solution)/shard_map/ppermute | solution.py:284
  131.1 24.6 %collective-permute-start.10 = (f32[1408,1024]{1,0:T(8,128)}, f32[1408,1024]{1,0:T(8,128)}, u32[]{:S(2)}, u32[]{:S(2)}) collective-permute-start(f32[1408,1024]{1,0:T(8,128)} %get-tuple-element.97.refs_4_), channel_id=1, source_target_pairs={{0,16},{16,0},{1,17},{17,1},{2,18},{18,2},{3,19},{19,3},{4,20},{20... | collective-permute-start | bytes 17301512 | tf_op jit(solution)/shard_map/ppermute | solution.py:140
  143.1 18.2 %collective-permute-start.9 = (f32[512,2816]{1,0:T(8,128)}, f32[512,2816]{1,0:T(8,128)}, u32[]{:S(2)}, u32[]{:S(2)}) collective-permute-start(f32[512,2816]{1,0:T(8,128)} %get-tuple-element.99.refs_4_), channel_id=1, source_target_pairs={{0,16},{16,0},{1,17},{17,1},{2,18},{18,2},{3,19},{19,3},{4,20},{20... | collective-permute-start | bytes 17301512 | tf_op jit(solution)/shard_map/ppermute | solution.py:140
  155.7 11.0 %collective-permute-start.12 = (f32[512,2816]{1,0:T(8,128)}, f32[512,2816]{1,0:T(8,128)}, u32[]{:S(2)}, u32[]{:S(2)}) collective-permute-start(f32[512,2816]{1,0:T(8,128)} %get-tuple-element.102.refs_9_), channel_id=1, source_target_pairs={{0,16},{16,0},{1,17},{17,1},{2,18},{18,2},{3,19},{19,3},{4,20},{20... | collective-permute-start | bytes 17301512 | tf_op jit(solution)/shard_map/ppermute | solution.py:140
  159.7 102.9 %collective-permute-start.18 = (f32[8,88,1024]{2,1,0:T(8,128)}, f32[8,88,1024]{2,1,0:T(8,128)}, u32[]{:S(2)}, u32[]{:S(2)}) collective-permute-start(f32[8,88,1024]{2,1,0:T(8,128)} %shard_map.216.refs_9_), channel_id=1, source_target_pairs={{0,1},{1,0},{2,3},{3,2},{4,5},{5,4},{6,7},{7,6},{8,9},{9,8},{10,11... | collective-permute-start | bytes 8650760 | tf_op jit(solution)/shard_map/ppermute | solution.py:128
  165.2 117.0 %collective-permute-start.11 = (f32[8,32,2816]{2,1,0:T(8,128)}, f32[8,32,2816]{2,1,0:T(8,128)}, u32[]{:S(2)}, u32[]{:S(2)}) collective-permute-start(f32[8,32,2816]{2,1,0:T(8,128)} %shard_map.217.refs_9_), channel_id=1, source_target_pairs={{0,2},{1,3},{2,0},{3,1},{4,6},{5,7},{6,4},{7,5},{8,10},{9,11},{10,... | collective-permute-start | bytes 8650760 | tf_op jit(solution)/shard_map/ppermute | solution.py:128
  170.8 108.3 %collective-permute-start.13 = (f32[8,32,2816]{2,1,0:T(8,128)}, f32[8,32,2816]{2,1,0:T(8,128)}, u32[]{:S(2)}, u32[]{:S(2)}) collective-permute-start(f32[8,32,2816]{2,1,0:T(8,128)} %shard_map.218.refs_15_), channel_id=1, source_target_pairs={{0,4},{1,5},{2,6},{3,7},{4,0},{5,1},{6,2},{7,3},{8,12},{9,13},{10,... | collective-permute-start | bytes 8650760 | tf_op jit(solution)/shard_map/ppermute | solution.py:128
  204.6 31.9 %collective-permute-start.14 = (f32[2,528,128]{2,1,0:T(8,128)}, f32[2,528,128]{2,1,0:T(8,128)}, u32[]{:S(2)}, u32[]{:S(2)}) collective-permute-start(f32[2,528,128]{2,1,0:T(8,128)} %get-tuple-element.104.refs_1_), channel_id=1, source_target_pairs={{0,1},{1,0},{2,3},{3,2},{4,5},{5,4},{6,7},{7,6},{8,9},{9,8},{10,11... | collective-permute-start | bytes 1622024 | tf_op jit(solution)/shard_map/ppermute | solution.py:380
  215.3 25.1 %collective-permute-start.16 = (f32[512,2048]{1,0:T(8,128)}, f32[512,2048]{1,0:T(8,128)}, u32[]{:S(2)}, u32[]{:S(2)}) collective-permute-start(f32[512,2048]{1,0:T(8,128)} %get-tuple-element.109.refs_8_), channel_id=1, source_target_pairs={{0,16},{16,0},{1,17},{17,1},{2,18},{18,2},{3,19},{19,3},{4,20},{20... | collective-permute-start | bytes 12582920 | tf_op jit(solution)/shard_map/ppermute | solution.py:140
  238.8 21.4 %collective-permute-start.15 = (f32[2,528,128]{2,1,0:T(8,128)}, f32[2,528,128]{2,1,0:T(8,128)}, u32[]{:S(2)}, u32[]{:S(2)}) collective-permute-start(f32[2,528,128]{2,1,0:T(8,128)} %get-tuple-element.111.refs_1_), channel_id=1, source_target_pairs={{0,2},{1,3},{2,0},{3,1},{4,6},{5,7},{6,4},{7,5},{8,10},{9,11},{10,... | collective-permute-start | bytes 1622024 | tf_op jit(solution)/shard_map/ppermute | solution.py:380
  262.7 13.9 %collective-permute-start.17 = (f32[2,528,128]{2,1,0:T(8,128)}, f32[2,528,128]{2,1,0:T(8,128)}, u32[]{:S(2)}, u32[]{:S(2)}) collective-permute-start(f32[2,528,128]{2,1,0:T(8,128)} %get-tuple-element.115.refs_1_), channel_id=1, source_target_pairs={{0,4},{1,5},{2,6},{3,7},{4,0},{5,1},{6,2},{7,3},{8,12},{9,13},{10,... | collective-permute-start | bytes 1622024 | tf_op jit(solution)/shard_map/ppermute | solution.py:380
  272.1 93.1 %collective-permute-start.24 = (f32[4,88,1024]{2,1,0:T(8,128)}, f32[4,88,1024]{2,1,0:T(8,128)}, u32[]{:S(2)}, u32[]{:S(2)}) collective-permute-start(f32[4,88,1024]{2,1,0:T(8,128)} %shard_map.226.refs_5_), channel_id=1, source_target_pairs={{0,2},{1,3},{2,0},{3,1},{4,6},{5,7},{6,4},{7,5},{8,10},{9,11},{10,... | collective-permute-start | bytes 4325384 | tf_op jit(solution)/shard_map/ppermute | solution.py:128
  272.6 96.4 %collective-permute-start.23 = (f32[8,32,2048]{2,1,0:T(8,128)}, f32[8,32,2048]{2,1,0:T(8,128)}, u32[]{:S(2)}, u32[]{:S(2)}) collective-permute-start(f32[8,32,2048]{2,1,0:T(8,128)} %shard_map.223.refs_8_), channel_id=1, source_target_pairs={{0,1},{1,0},{2,3},{3,2},{4,5},{5,4},{6,7},{7,6},{8,9},{9,8},{10,11... | collective-permute-start | bytes 6291464 | tf_op jit(solution)/shard_map/ppermute | solution.py:128
  276.6 75.9 %collective-permute-start.20 = (f32[512,1024]{1,0:T(8,128)}, f32[512,1024]{1,0:T(8,128)}, u32[]{:S(2)}, u32[]{:S(2)}) collective-permute-start(f32[512,1024]{1,0:T(8,128)} %get-tuple-element.117.refs_4_), channel_id=1, source_target_pairs={{0,16},{16,0},{1,17},{17,1},{2,18},{18,2},{3,19},{19,3},{4,20},{20... | collective-permute-start | bytes 6291464 | tf_op jit(solution)/shard_map/ppermute | solution.py:140
  279.0 58.1 %collective-permute-start.19 = (f32[2,528,128]{2,1,0:T(8,128)}, f32[2,528,128]{2,1,0:T(8,128)}, u32[]{:S(2)}, u32[]{:S(2)}) collective-permute-start(f32[2,528,128]{2,1,0:T(8,128)} %get-tuple-element.119.refs_1_), channel_id=1, source_target_pairs={{0,8},{1,9},{2,10},{3,11},{4,12},{5,13},{6,14},{7,15},{8,0},{9,1},... | collective-permute-start | bytes 1622024 | tf_op jit(solution)/shard_map/ppermute | solution.py:380
  282.3 113.4 %collective-permute-start.28 = (f32[4,32,2816]{2,1,0:T(8,128)}, f32[4,32,2816]{2,1,0:T(8,128)}, u32[]{:S(2)}, u32[]{:S(2)}) collective-permute-start(f32[4,32,2816]{2,1,0:T(8,128)} %shard_map.229.refs_7_), channel_id=1, source_target_pairs={{0,8},{1,9},{2,10},{3,11},{4,12},{5,13},{6,14},{7,15},{8,0},{9,1},... | collective-permute-start | bytes 4325384 | tf_op jit(solution)/shard_map/ppermute | solution.py:128
  340.7 9.0 %collective-permute-start.44 = (f32[8,128]{1,0:T(8,128)}, f32[8,128]{1,0:T(8,128)}, u32[]{:S(2)}, u32[]{:S(2)}) collective-permute-start(f32[8,128]{1,0:T(8,128)} %slice_bitcast_fusion), channel_id=1, source_target_pairs={{0,16},{16,0},{1,17},{17,1},{2,18},{18,2},{3,19},{19,3},{4,20},{20... | collective-permute-start | bytes 12296 | tf_op jit(solution)/shard_map/ppermute | solution.py:140
  349.7 49.5 %collective-permute-start.27 = (f32[4,32,2816]{2,1,0:T(8,128)}, f32[4,32,2816]{2,1,0:T(8,128)}, u32[]{:S(2)}, u32[]{:S(2)}) collective-permute-start(f32[4,32,2816]{2,1,0:T(8,128)} %shard_map.230.refs_3_), channel_id=1, source_target_pairs={{0,1},{1,0},{2,3},{3,2},{4,5},{5,4},{6,7},{7,6},{8,9},{9,8},{10,11... | collective-permute-start | bytes 4325384 | tf_op jit(solution)/shard_map/ppermute | solution.py:128
  355.1 51.2 %collective-permute-start.25 = (f32[8,32,1024]{2,1,0:T(8,128)}, f32[8,32,1024]{2,1,0:T(8,128)}, u32[]{:S(2)}, u32[]{:S(2)}) collective-permute-start(f32[8,32,1024]{2,1,0:T(8,128)} %shard_map.234.refs_5_), channel_id=1, source_target_pairs={{0,2},{1,3},{2,0},{3,1},{4,6},{5,7},{6,4},{7,5},{8,10},{9,11},{10,... | collective-permute-start | bytes 3145736 | tf_op jit(solution)/shard_map/ppermute | solution.py:128
  365.2 7.1 %collective-permute-start.22 = (f32[512,1024]{1,0:T(8,128)}, f32[512,1024]{1,0:T(8,128)}, u32[]{:S(2)}, u32[]{:S(2)}) collective-permute-start(f32[512,1024]{1,0:T(8,128)} %get-tuple-element.130.refs_9_), channel_id=1, source_target_pairs={{0,16},{16,0},{1,17},{17,1},{2,18},{18,2},{3,19},{19,3},{4,20},{20... | collective-permute-start | bytes 6291464 | tf_op jit(solution)/shard_map/ppermute | solution.py:140
  369.0 111.1 %reduce-scatter.3.cloned.1.call-start = ((), (), s32[]{:S(2)}) async-start(), calls=%async_computation.2 | async-start | bytes 1802240 | tf_op jit(solution)/shard_map/reduce_scatter | solution.py:244
  369.0 7.3 %collective-permute-start.21 = (f32[512,1024]{1,0:T(8,128)}, f32[512,1024]{1,0:T(8,128)}, u32[]{:S(2)}, u32[]{:S(2)}) collective-permute-start(f32[512,1024]{1,0:T(8,128)} %get-tuple-element.128), channel_id=1, source_target_pairs={{0,16},{16,0},{1,17},{17,1},{2,18},{18,2},{3,19},{19,3},{4,20},{20... | collective-permute-start | bytes 6291464 | tf_op jit(solution)/shard_map/ppermute | solution.py:140
  372.3 31.7 %collective-permute-start.26 = (f32[4,32,2048]{2,1,0:T(8,128)}, f32[4,32,2048]{2,1,0:T(8,128)}, u32[]{:S(2)}, u32[]{:S(2)}) collective-permute-start(f32[4,32,2048]{2,1,0:T(8,128)} %shard_map.237.refs_9_), channel_id=1, source_target_pairs={{0,2},{1,3},{2,0},{3,1},{4,6},{5,7},{6,4},{7,5},{8,10},{9,11},{10,... | collective-permute-start | bytes 3145736 | tf_op jit(solution)/shard_map/ppermute | solution.py:128
  376.4 33.1 %collective-permute-start.33 = (f32[8,32,1024]{2,1,0:T(8,128)}, f32[8,32,1024]{2,1,0:T(8,128)}, u32[]{:S(2)}, u32[]{:S(2)}) collective-permute-start(f32[8,32,1024]{2,1,0:T(8,128)} %shard_map.238.refs_9_), channel_id=1, source_target_pairs={{0,1},{1,0},{2,3},{3,2},{4,5},{5,4},{6,7},{7,6},{8,9},{9,8},{10,11... | collective-permute-start | bytes 3145736 | tf_op jit(solution)/shard_map/ppermute | solution.py:128
  395.7 30.7 %collective-permute-start.32 = (f32[8,32,1024]{2,1,0:T(8,128)}, f32[8,32,1024]{2,1,0:T(8,128)}, u32[]{:S(2)}, u32[]{:S(2)}) collective-permute-start(f32[8,32,1024]{2,1,0:T(8,128)} %shard_map.239.refs_11_), channel_id=1, source_target_pairs={{0,2},{1,3},{2,0},{3,1},{4,6},{5,7},{6,4},{7,5},{8,10},{9,11},{10,... | collective-permute-start | bytes 3145736 | tf_op jit(solution)/shard_map/ppermute | solution.py:128
  399.2 29.9 %collective-permute-start.31 = (f32[2,32,2816]{2,1,0:T(8,128)}, f32[2,32,2816]{2,1,0:T(8,128)}, u32[]{:S(2)}, u32[]{:S(2)}) collective-permute-start(f32[2,32,2816]{2,1,0:T(8,128)} %shard_map.241.refs_9_), channel_id=1, source_target_pairs={{0,1},{1,0},{2,3},{3,2},{4,5},{5,4},{6,7},{7,6},{8,9},{9,8},{10,11... | collective-permute-start | bytes 2162696 | tf_op jit(solution)/shard_map/ppermute | solution.py:128
  406.2 26.0 %collective-permute-start.30 = (f32[2,32,2048]{2,1,0:T(8,128)}, f32[2,32,2048]{2,1,0:T(8,128)}, u32[]{:S(2)}, u32[]{:S(2)}) collective-permute-start(f32[2,32,2048]{2,1,0:T(8,128)} %shard_map.243.refs_7_), channel_id=1, source_target_pairs={{0,4},{1,5},{2,6},{3,7},{4,0},{5,1},{6,2},{7,3},{8,12},{9,13},{10,... | collective-permute-start | bytes 1572872 | tf_op jit(solution)/shard_map/ppermute | solution.py:128
  408.5 25.8 %collective-permute-start.29 = (f32[4,32,1024]{2,1,0:T(8,128)}, f32[4,32,1024]{2,1,0:T(8,128)}, u32[]{:S(2)}, u32[]{:S(2)}) collective-permute-start(f32[4,32,1024]{2,1,0:T(8,128)} %shard_map.244.refs_7_), channel_id=1, source_target_pairs={{0,1},{1,0},{2,3},{3,2},{4,5},{5,4},{6,7},{7,6},{8,9},{9,8},{10,11... | collective-permute-start | bytes 1572872 | tf_op jit(solution)/shard_map/ppermute | solution.py:128
  411.8 25.8 %collective-permute-start.38 = (f32[4,32,1024]{2,1,0:T(8,128)}, f32[4,32,1024]{2,1,0:T(8,128)}, u32[]{:S(2)}, u32[]{:S(2)}) collective-permute-start(f32[4,32,1024]{2,1,0:T(8,128)} %shard_map.245.refs_7_), channel_id=1, source_target_pairs={{0,2},{1,3},{2,0},{3,1},{4,6},{5,7},{6,4},{7,5},{8,10},{9,11},{10,... | collective-permute-start | bytes 1572872 | tf_op jit(solution)/shard_map/ppermute | solution.py:128
  428.6 15.8 %collective-permute-start.37 = (f32[4,32,1024]{2,1,0:T(8,128)}, f32[4,32,1024]{2,1,0:T(8,128)}, u32[]{:S(2)}, u32[]{:S(2)}) collective-permute-start(f32[4,32,1024]{2,1,0:T(8,128)} %shard_map.246.refs_6_), channel_id=1, source_target_pairs={{0,1},{1,0},{2,3},{3,2},{4,5},{5,4},{6,7},{7,6},{8,9},{9,8},{10,11... | collective-permute-start | bytes 1572872 | tf_op jit(solution)/shard_map/ppermute | solution.py:128
  431.3 15.1 %collective-permute-start.36 = (f32[1,32,2816]{2,1,0:T(8,128)}, f32[1,32,2816]{2,1,0:T(8,128)}, u32[]{:S(2)}, u32[]{:S(2)}) collective-permute-start(f32[1,32,2816]{2,1,0:T(8,128)} %shard_map.247.refs_6_), channel_id=1, source_target_pairs={{0,2},{1,3},{2,0},{3,1},{4,6},{5,7},{6,4},{7,5},{8,10},{9,11},{10,... | collective-permute-start | bytes 1081352 | tf_op jit(solution)/shard_map/ppermute | solution.py:128
  434.3 18.1 %collective-permute-start.35 = (f32[1,32,2048]{2,1,0:T(8,128)}, f32[1,32,2048]{2,1,0:T(8,128)}, u32[]{:S(2)}, u32[]{:S(2)}) collective-permute-start(f32[1,32,2048]{2,1,0:T(8,128)} %shard_map.248.refs_5_), channel_id=1, source_target_pairs={{0,8},{1,9},{2,10},{3,11},{4,12},{5,13},{6,14},{7,15},{8,0},{9,1},... | collective-permute-start | bytes 786440 | tf_op jit(solution)/shard_map/ppermute | solution.py:128
  436.3 18.1 %collective-permute-start.34 = (f32[2,32,1024]{2,1,0:T(8,128)}, f32[2,32,1024]{2,1,0:T(8,128)}, u32[]{:S(2)}, u32[]{:S(2)}) collective-permute-start(f32[2,32,1024]{2,1,0:T(8,128)} %shard_map.249.refs_5_), channel_id=1, source_target_pairs={{0,4},{1,5},{2,6},{3,7},{4,0},{5,1},{6,2},{7,3},{8,12},{9,13},{10,... | collective-permute-start | bytes 786440 | tf_op jit(solution)/shard_map/ppermute | solution.py:128
  439.6 20.3 %collective-permute-start.41 = (f32[2,32,1024]{2,1,0:T(8,128)}, f32[2,32,1024]{2,1,0:T(8,128)}, u32[]{:S(2)}, u32[]{:S(2)}) collective-permute-start(f32[2,32,1024]{2,1,0:T(8,128)} %shard_map.250.refs_5_), channel_id=1, source_target_pairs={{0,4},{1,5},{2,6},{3,7},{4,0},{5,1},{6,2},{7,3},{8,12},{9,13},{10,... | collective-permute-start | bytes 786440 | tf_op jit(solution)/shard_map/ppermute | solution.py:128
  446.4 21.9 %collective-permute-start.40 = (f32[2,32,1024]{2,1,0:T(8,128)}, f32[2,32,1024]{2,1,0:T(8,128)}, u32[]{:S(2)}, u32[]{:S(2)}) collective-permute-start(f32[2,32,1024]{2,1,0:T(8,128)} %shard_map.251.refs_7_), channel_id=1, source_target_pairs={{0,4},{1,5},{2,6},{3,7},{4,0},{5,1},{6,2},{7,3},{8,12},{9,13},{10,... | collective-permute-start | bytes 786440 | tf_op jit(solution)/shard_map/ppermute | solution.py:128
  456.3 13.8 %collective-permute-start.39 = (f32[1,32,1024]{2,1,0:T(8,128)}, f32[1,32,1024]{2,1,0:T(8,128)}, u32[]{:S(2)}, u32[]{:S(2)}) collective-permute-start(f32[1,32,1024]{2,1,0:T(8,128)} %shard_map.254.refs_6_), channel_id=1, source_target_pairs={{0,8},{1,9},{2,10},{3,11},{4,12},{5,13},{6,14},{7,15},{8,0},{9,1},... | collective-permute-start | bytes 393224 | tf_op jit(solution)/shard_map/ppermute | solution.py:128
  461.7 10.8 %collective-permute-start.42 = (f32[1,32,1024]{2,1,0:T(8,128)}, f32[1,32,1024]{2,1,0:T(8,128)}, u32[]{:S(2)}, u32[]{:S(2)}) collective-permute-start(f32[1,32,1024]{2,1,0:T(8,128)} %shard_map.255.refs_6_), channel_id=1, source_target_pairs={{0,8},{1,9},{2,10},{3,11},{4,12},{5,13},{6,14},{7,15},{8,0},{9,1},... | collective-permute-start | bytes 393224 | tf_op jit(solution)/shard_map/ppermute | solution.py:128
  470.1 8.1 %collective-permute-start.43 = (f32[1,32,1024]{2,1,0:T(8,128)}, f32[1,32,1024]{2,1,0:T(8,128)}, u32[]{:S(2)}, u32[]{:S(2)}) collective-permute-start(f32[1,32,1024]{2,1,0:T(8,128)} %shard_map.256.refs_7_), channel_id=1, source_target_pairs={{0,8},{1,9},{2,10},{3,11},{4,12},{5,13},{6,14},{7,15},{8,0},{9,1},... | collective-permute-start | bytes 393224 | tf_op jit(solution)/shard_map/ppermute | solution.py:128
  (1 other events, 6.3 us)
Sparse Core Ops, SparseCore 0:
  369.1 30.6 reduce-scatter.4
  409.6 38.7 reduce-scatter.2

commit v4 on v3

--- a/solution.py
+++ b/solution.py
@@ -43,10 +43,20 @@
         self.rows = halves[0][0].shape[0] // self.count
         axes = tuple(range(self.bits))
         self.parts = [
-            ([h.reshape((self.count, self.rows, h.shape[1])) for h in half], axes) for half in halves
+            ([h.reshape((self.count, self.rows, h.shape[1])) for h in half], axes, 0) for half in halves
         ]
+        self.width = sum(h.shape[1] for h in halves[0])
         self.order = list(order)
         self.done = ()
+
+    def beside(self, others, order):
+        for one in (self, *others):
+            while one.order:
+                one.step()
+        for other in others:
+            self.parts += [(held, axes, begin + self.width) for held, axes, begin in other.parts]
+            self.width += other.width
+        self.order = list(order)
 
     def total(self, flipped, widths=None):
         fixed = self.done if flipped is None else self.done + (flipped,)
@@ -68,8 +78,7 @@
         count = 1 << len(left)
         deep = max(1, count // STEPS)
         arrays, specs, places = [], [], []
-        for held, axes in self.parts:
-            begin = 0
+        for held, axes, begin in self.parts:
             for array in held:
                 wide = array.shape[2]
                 for d in range(deep):
@@ -83,7 +92,7 @@
                     places.append((d, begin, begin + wide))
                 begin += wide
         final = widths is not None
-        widths = widths or [begin]
+        widths = widths or [self.width]
 
         def kernel(position_ref, *refs):
             ins, outs = refs[: len(arrays)], refs[len(arrays) :]
@@ -128,7 +137,7 @@
         incoming = lax.ppermute(outgoing, "seq", [(i, i ^ flip) for i in range(self.count)])
         self.done = self.done + (axis,)
         left = tuple(a for a in range(self.bits) if a not in self.done)
-        self.parts.append(([incoming], left))
+        self.parts.append(([incoming], left, 0))
 
     def finish(self, *widths):
         while self.order:
@@ -636,15 +645,16 @@
 def back_product(turns, cotangent, w_down):
     tokens, width = cotangent.shape
     wide = w_down.shape[0]
+    tile = wide // 2
 
     def kernel(c_ref, w_ref, o_ref):
         o_ref[...] = dot_nt(c_ref[...], w_ref[...]).astype(BF16)
 
     return turns.call(
         kernel,
-        (wide // TILE,),
-        [full_spec((tokens, width)), row_spec(TILE, width)],
-        column_spec(tokens, TILE),
+        (wide // tile,),
+        [full_spec((tokens, width)), row_spec(tile, width)],
+        column_spec(tokens, tile),
         shape((tokens, wide), BF16),
         us=8.5,
     )(cotangent, w_down)

time: 495 us -> 492 us (level)
  no operation moved by 1% of the time
where the time goes in v4:
time: 492 us; the launch traced here: 485 us
  Pallas kernels  341 us (69%)
  waiting for transfers between devices  80.3 us (16%)
  starting transfers between devices  42.7 us (9%)
  between operations  14.5 us (3%)
  local copies, waits for them, and re-layouts  5.05 us (1%)
    pallas_call x57, Pallas kernels, run(): pl.pallas_call(body, grid_spec=spec, out_shape=out_shape, compiler_params...  341 us
    ppermute x4, waiting for transfers between devices, send(): lax.ppermute(self.payload, 'seq', [(i, i ^ flip) for i in range(self.coun...  44.8 us
    ppermute x24, waiting for transfers between devices, step(): lax.ppermute(outgoing, 'seq', [(i, i ^ flip) for i in range(self.count)])  35.4 us
    ppermute x24, starting transfers between devices, step(): lax.ppermute(outgoing, 'seq', [(i, i ^ flip) for i in range(self.count)])  19.9 us
    ppermute x3, starting transfers between devices, pass_on(): self.passed.append(lax.ppermute(total_share, 'seq', moves))  11.5 us
  transfers between devices with their start and end apart: 47, of which 11 were waited for; matrix products, arithmetic and copies ran while one was open for 1% of the time, Pallas kernels for 57%

profile of v4, /device:TPU:0, one launch (start us, length us, event | category | flops | bytes accessed | tf_op | source)
XLA Modules:
  0.0 485.2 jit_solution(17606025758704932439)
XLA Ops:
  11.1 11.3 %shard_map.203 = (bf16[1024,1024]{1,0:T(8,128)(2,1)}, bf16[1024,1024]{1,0:T(8,128)(2,1)}, bf16[1024,1024]{1,0:T(8,128)(2,1)}, f32[2,512,128]{2,1,0:T(8,128)}) custom-call(f32[2]{0:T(128)} %get-tuple-element.134.refs_0_, bf16[1024,1024]{1,0:T(8,128)(2,1)} %bitcast.54, f32[1024,1]{1,0:T(8,128)} %bitcast.42, bf16[1024,1024]{1,0:T(8,128)(2,1)} %refs_6_.5, ...), custom_call_target="tpu_custom_call" | custom-call | flops 950000025600 | tf_op jit(solution)/shard_map/pallas_call | solution.py:172
  24.3 2.9 collective-permute-start
  29.4 11.2 %shard_map.205 = (bf16[1024,512]{1,0:T(8,128)(2,1)}, bf16[1024,512]{1,0:T(8,128)(2,1)}, f32[1024,512]{1,0:T(8,128)}) custom-call(bf16[1024,1024]{1,0:T(8,128)(2,1)} %get-tuple-element.72.refs_2_.refs_0_.refs_3_.refs_4_.refs_1_, bf16[1024,1024]{1,0:T(8,128)(2,1)} %get-tuple-element.73.refs_1_.refs_2_, bf16[1024,1024]{1,0:T(8,128)(2,1)} %get-tuple-element.74.refs_2_.refs_3_, ...), custom_call_target="tpu_custom_call" | custom-call | flops 830000005120 | tf_op jit(solution)/shard_map/pallas_call | solution.py:172
  42.4 4.6 collective-permute-start.3
  47.0 4.5 collective-permute-start.4
  51.6 2.4 collective-permute-start.5
  54.0 11.3 %shard_map.207 = (bf16[1024,512]{1,0:T(8,128)(2,1)}, bf16[1024,512]{1,0:T(8,128)(2,1)}, f32[1024,512]{1,0:T(8,128)}) custom-call(bf16[1024,1024]{1,0:T(8,128)(2,1)} %get-tuple-element.72.refs_2_.refs_0_.refs_3_.refs_4_.refs_1_, bf16[1024,1024]{1,0:T(8,128)(2,1)} %get-tuple-element.73.refs_1_.refs_2_, bf16[1024,1024]{1,0:T(8,128)(2,1)} %get-tuple-element.74.refs_2_.refs_3_, ...), custom_call_target="tpu_custom_call" | custom-call | flops 830000005120 | tf_op jit(solution)/shard_map/pallas_call | solution.py:172
  71.0 11.0 %shard_map.209.refs_5_.refs_3_ = bf16[1024,2816]{1,0:T(8,128)(2,1)} custom-call(bf16[1024,1024]{1,0:T(8,128)(2,1)} %bitcast.51, bf16[2816,1024]{1,0:T(8,128)(2,1)} %refs_2_.3, f32[2,136,128]{2,1,0:T(8,128)} %get-tuple-element.86.refs_2_.refs_1_), custom_call_target="tpu_custom_call" | custom-call | flops 850000019456 | tf_op jit(solution)/shard_map/pallas_call | solution.py:172
  84.1 12.1 %shard_map.211 = (bf16[1024,1024]{1,0:T(8,128)(2,1)}, bf16[1024,1024]{1,0:T(8,128)(2,1)}, f32[1024,1024]{1,0:T(8,128)}, bf16[1024,1024]{1,0:T(8,128)(2,1)}) custom-call(bf16[1024,512]{1,0:T(8,128)(2,1)} %get-tuple-element.77.refs_5_.refs_0_.refs_11_.refs_1_, bf16[1024,512]{1,0:T(8,128)(2,1)} %get-tuple-element.78.refs_1_.refs_13_, ...), custom_call_target="tpu_custom_call" | custom-call | flops 719999991808 | tf_op jit(solution)/shard_map/pallas_call | solution.py:172
  96.2 21.0 %shard_map.212 = (bf16[1024,2816]{1,0:T(8,128)(2,1)}, bf16[1024,2816]{1,0:T(8,128)(2,1)}, bf16[1024,2816]{1,0:T(8,128)(2,1)}) custom-call(bf16[1024,1024]{1,0:T(8,128)(2,1)} %get-tuple-element.93.refs_0_.refs_1_.refs_2_, bf16[1024,2816]{1,0:T(8,128)(2,1)} %refs_3_.3, bf16[1024,2816]{1,0:T(8,128)(2,1)} %refs_4_.3, ...), custom_call_target="tpu_custom_call" | custom-call | flops 1799999979520 | tf_op jit(solution)/shard_map/pallas_call | solution.py:172
  117.2 12.0 %shard_map.213 = (f32[1408,1024]{1,0:T(8,128)}, f32[1408,1024]{1,0:T(8,128)}) custom-call(s32[1]{0:T(128)} %bitcast.6.refs_0_, bf16[1024,2816]{1,0:T(8,128)(2,1)} %get-tuple-element.95.refs_1_.refs_2_.refs_4_, bf16[1024,2816]{1,0:T(8,128)(2,1)} %get-tuple-element.95.refs_1_.refs_2_.refs_4_, bf16[1024,1024]{1,0:T(8,128)(2,1)} %bitcast.52, ...), custom_call_target="tpu_custom_call" | custom-call | flops 1199999942656 | tf_op jit(solution)/shard_map/pallas_call | solution.py:172
  129.1 12.1 %shard_map.214 = (f32[512,2816]{1,0:T(8,128)}, f32[512,2816]{1,0:T(8,128)}) custom-call(s32[1]{0:T(128)} %bitcast.6.refs_0_, bf16[1024,1024]{1,0:T(8,128)(2,1)} %get-tuple-element.93.refs_0_.refs_1_.refs_2_, bf16[1024,1024]{1,0:T(8,128)(2,1)} %get-tuple-element.93.refs_0_.refs_1_.refs_2_, bf16[1024,2816]{1,0:T(8,128)(2,1)} %get-tuple-element.96.refs_3_.refs_1_, ...), custom_call_target="tpu_custom_call" | custom-call | flops 1199999942656 | tf_op jit(solution)/shard_map/pallas_call | solution.py:172
  141.7 11.9 %shard_map.215 = (f32[512,2816]{1,0:T(8,128)}, f32[512,2816]{1,0:T(8,128)}) custom-call(s32[1]{0:T(128)} %bitcast.6.refs_0_, bf16[1024,1024]{1,0:T(8,128)(2,1)} %get-tuple-element.93.refs_0_.refs_1_.refs_2_, bf16[1024,1024]{1,0:T(8,128)(2,1)} %get-tuple-element.93.refs_0_.refs_1_.refs_2_, bf16[1024,2816]{1,0:T(8,128)(2,1)} %get-tuple-element.101.refs_3_.refs_2_, ...), custom_call_target="tpu_custom_call" | custom-call | flops 1199999942656 | tf_op jit(solution)/shard_map/pallas_call | solution.py:172
  153.7 4.0 shard_map.216.refs_9_
  159.1 4.0 shard_map.217.refs_9_
  164.6 4.0 shard_map.218.refs_15_
  168.7 33.8 %shard_map.219 = (bf16[1024,1024]{1,0:T(8,128)(2,1)}, bf16[1024,1024]{1,0:T(8,128)(2,1)}, bf16[1024,1024]{1,0:T(8,128)(2,1)}, f32[2,528,128]{2,1,0:T(8,128)}) custom-call(f32[2]{0:T(128)} %get-tuple-element.133.refs_0_, bf16[1024,2816]{1,0:T(8,128)(2,1)} %get-tuple-element.96.refs_3_.refs_1_, bf16[1024,2816]{1,0:T(8,128)(2,1)} %get-tuple-element.101.refs_3_.refs_2_, ...), custom_call_target="tpu_custom_call" | custom-call | flops 2799999909888 | tf_op jit(solution)/shard_map/pallas_call | solution.py:172
  203.1 10.1 %shard_map.220 = (f32[512,2048]{1,0:T(8,128)}, f32[512,2048]{1,0:T(8,128)}) custom-call(s32[1]{0:T(128)} %bitcast.6.refs_0_, bf16[1024,1024]{1,0:T(8,128)(2,1)} %get-tuple-element.106.refs_1_.refs_2_, bf16[1024,1024]{1,0:T(8,128)(2,1)} %get-tuple-element.106.refs_1_.refs_2_, bf16[1024,1024]{1,0:T(8,128)(2,1)} %get-tuple-element.72.refs_2_.refs_0_.refs_3_.refs_4_.refs_1_, ...), custom_call_target="tpu_custom_call" | custom-call | flops 999999995904 | tf_op jit(solution)/shard_map/pallas_call | solution.py:172
  213.2 16.6 %shard_map.221 = (bf16[1024,512]{1,0:T(8,128)(2,1)}, f32[1024,512]{1,0:T(8,128)}, f32[1024,512]{1,0:T(8,128)}) custom-call(f32[2,8,128]{2,1,0:T(8,128)} %get-tuple-element.91.refs_8_.refs_0_, bf16[1024,512]{1,0:T(8,128)(2,1)} %get-tuple-element.77.refs_5_.refs_0_.refs_11_.refs_1_, bf16[1024,1024]{1,0:T(8,128)(2,1)} %get-tuple-element.73.refs_1_.refs_2_, ...), custom_call_target="tpu_custom_call" | custom-call | flops 1399999954944 | tf_op jit(solution)/shard_map/pallas_call | solution.py:172
  229.8 4.7 collective-permute-done.14.refs_2_
  238.2 3.3 shard_map.223.refs_8_
  241.6 16.8 %shard_map.224 = (bf16[1024,512]{1,0:T(8,128)(2,1)}, f32[1024,512]{1,0:T(8,128)}, f32[1024,512]{1,0:T(8,128)}) custom-call(f32[2,8,128]{2,1,0:T(8,128)} %get-tuple-element.91.refs_8_.refs_0_, bf16[1024,512]{1,0:T(8,128)(2,1)} %get-tuple-element.83.refs_8_.refs_3_.refs_12_.refs_1_, bf16[1024,1024]{1,0:T(8,128)(2,1)} %get-tuple-element.73.refs_1_.refs_2_, ...), custom_call_target="tpu_custom_call" | custom-call | flops 1399999954944 | tf_op jit(solution)/shard_map/pallas_call | solution.py:172
  258.3 2.5 shard_map.225
  260.8 3.2 shard_map.226.refs_5_
  264.0 6.3 %shard_map.227 = (f32[512,1024]{1,0:T(8,128)}, f32[512,1024]{1,0:T(8,128)}) custom-call(s32[1]{0:T(128)} %bitcast.6.refs_0_, bf16[1024,1024]{1,0:T(8,128)(2,1)} %get-tuple-element.72.refs_2_.refs_0_.refs_3_.refs_4_.refs_1_, bf16[1024,1024]{1,0:T(8,128)(2,1)} %get-tuple-element.72.refs_2_.refs_0_.refs_3_.refs_4_.refs_1_, ...), custom_call_target="tpu_custom_call" | custom-call | flops 599999971328 | tf_op jit(solution)/shard_map/pallas_call | solution.py:172
  272.3 2.5 collective-permute-done.17.refs_2_
  274.7 2.5 shard_map.228
  277.2 3.2 shard_map.229.refs_7_
  280.4 2.9 collective-permute-start.28
  283.4 3.2 shard_map.230.refs_3_
  286.6 11.1 %shard_map.231.refs_4_ = bf16[1024,1024]{1,0:T(8,128)(2,1)} custom-call(f32[1024,1024]{1,0:T(8,128)} %get-tuple-element.92.refs_6_.refs_0_, bf16[1024,2816]{1,0:T(8,128)(2,1)} %get-tuple-element.95.refs_1_.refs_2_.refs_4_, bf16[2816,1024]{1,0:T(8,128)(2,1)} %refs_2_.3, f32[4,32,2816]{2,1,0:T(8,128)} %shard_map.230.refs_3_), custom_call_target="tpu_custom_call" | custom-call | flops 899999989760 | tf_op jit(solution)/shard_map/pallas_call | solution.py:172
  297.7 37.7 %collective-permute-done.19.refs_2_ = f32[2,528,128]{2,1,0:T(8,128)} collective-permute-done((f32[2,528,128]{2,1,0:T(8,128)}, f32[2,528,128]{2,1,0:T(8,128)}, u32[]{:S(2)}, u32[]{:S(2)}) %collective-permute-start.19) | collective-permute-done | bytes 540704 | tf_op jit(solution)/shard_map/ppermute | solution.py:389
  338.9 8.9 %shard_map.233 = (bf16[1024,1024]{1,0:T(8,128)(2,1)}, bf16[1024,1024]{1,0:T(8,128)(2,1)}) custom-call(f32[2,528,128]{2,1,0:T(8,128)} %shard_map.232.refs_0_.refs_3_.refs_9_, bf16[1024,1024]{1,0:T(8,128)(2,1)} %get-tuple-element.73.refs_1_.refs_2_, bf16[1024,1024]{1,0:T(8,128)(2,1)} %get-tuple-element.74.refs_2_.refs_3_, ...), custom_call_target="tpu_custom_call" | custom-call | flops 499999997952 | tf_op jit(solution)/shard_map/pallas_call | solution.py:172
  350.6 2.6 shard_map.234.refs_5_
  353.7 9.6 %shard_map.235 = (f32[512,1024]{1,0:T(8,128)}, f32[512,1024]{1,0:T(8,128)}, f32[512,1024]{1,0:T(8,128)}, f32[512,1024]{1,0:T(8,128)}) custom-call(s32[1]{0:T(128)} %bitcast.6.refs_0_, bf16[1024,1024]{1,0:T(8,128)(2,1)} %get-tuple-element.72.refs_2_.refs_0_.refs_3_.refs_4_.refs_1_, ...), custom_call_target="tpu_custom_call" | custom-call | flops 999999995904 | tf_op jit(solution)/shard_map/pallas_call | solution.py:172
  363.3 3.7 shard_map.236.refs_7_
  367.6 2.8 shard_map.237.refs_9_
  372.0 2.5 shard_map.238.refs_9_
  375.1 2.5 shard_map.239.refs_11_
  377.6 16.2 %shard_map.240.refs_5_ = bf16[1024,1024]{1,0:T(8,128)(2,1)} custom-call(bf16[1024,512]{1,0:T(8,128)(2,1)} %get-tuple-element.110.refs_3_.refs_0_, bf16[1024,512]{1,0:T(8,128)(2,1)} %get-tuple-element.114.refs_4_.refs_1_, bf16[1024,1024]{1,0:T(8,128)(2,1)} %get-tuple-element.124.refs_9_.refs_3_.refs_2_, ...), custom_call_target="tpu_custom_call" | custom-call | flops 1300000014336 | tf_op jit(solution)/shard_map/pallas_call | solution.py:172
  394.7 2.6 shard_map.241.refs_9_
  398.4 3.7 shard_map.242.refs_5_
  411.0 13.5 %collective-permute-done.32.refs_5_.refs_6_.refs_3_ = f32[8,32,1024]{2,1,0:T(8,128)} collective-permute-done((f32[8,32,1024]{2,1,0:T(8,128)}, f32[8,32,1024]{2,1,0:T(8,128)}, u32[]{:S(2)}, u32[]{:S(2)}) %collective-permute-start.32) | collective-permute-done | bytes 1048608 | tf_op jit(solution)/shard_map/ppermute | solution.py:137
  438.4 4.1 collective-permute-done.37.refs_4_
  446.9 3.6 collective-permute-done.35.refs_6_
  454.6 3.4 collective-permute-done.41.refs_5_
  460.2 6.1 %collective-permute-done.40.refs_5_ = f32[2,32,1024]{2,1,0:T(8,128)} collective-permute-done((f32[2,32,1024]{2,1,0:T(8,128)}, f32[2,32,1024]{2,1,0:T(8,128)}, u32[]{:S(2)}, u32[]{:S(2)}) %collective-permute-start.40) | collective-permute-done | bytes 262176 | tf_op jit(solution)/shard_map/ppermute | solution.py:137
  472.6 3.7 collective-permute-done.43.refs_6_
  (119 shorter events, 80.9 us)
Async XLA Ops:
  7.2 471.0 %reduce-scatter.5.cloned.1.call-start = ((), (), s32[]{:S(2)}) async-start(), calls=%async_computation.3 | async-start | bytes 1802240 | tf_op jit(solution)/shard_map/reduce_scatter | solution.py:253
  8.8 13.6 %copy-start = (f32[2,512]{1,0:T(2,128)}, f32[2,512]{1,0:T(2,128)S(1)}, u32[]{:S(2)}) copy-start(f32[2,512]{1,0:T(2,128)S(1)} %get-tuple-element.136) | copy-start | bytes 12292
  24.3 16.3 %collective-permute-start = (f32[2,136,128]{2,1,0:T(8,128)}, f32[2,136,128]{2,1,0:T(8,128)}, u32[]{:S(2)}, u32[]{:S(2)}) collective-permute-start(f32[2,136,128]{2,1,0:T(8,128)} %get-tuple-element.80), channel_id=1, source_target_pairs={{0,1},{1,0},{2,3},{3,2},{4,5},{5,4},{6,7},{7,6},{8,9},{9,8},{10,11... | collective-permute-start | bytes 417800 | tf_op jit(solution)/shard_map/ppermute | solution.py:293
  27.3 13.3 %collective-permute-start.1 = (f32[2,136,128]{2,1,0:T(8,128)}, f32[2,136,128]{2,1,0:T(8,128)}, u32[]{:S(2)}, u32[]{:S(2)}) collective-permute-start(f32[2,136,128]{2,1,0:T(8,128)} %get-tuple-element.81), channel_id=1, source_target_pairs={{0,2},{1,3},{2,0},{3,1},{4,6},{5,7},{6,4},{7,5},{8,10},{9,11},{10,... | collective-permute-start | bytes 417800 | tf_op jit(solution)/shard_map/ppermute | solution.py:293
  28.8 11.8 %collective-permute-start.2 = (f32[2,136,128]{2,1,0:T(8,128)}, f32[2,136,128]{2,1,0:T(8,128)}, u32[]{:S(2)}, u32[]{:S(2)}) collective-permute-start(f32[2,136,128]{2,1,0:T(8,128)} %get-tuple-element.82), channel_id=1, source_target_pairs={{0,3},{1,2},{2,1},{3,0},{4,7},{5,6},{6,5},{7,4},{8,11},{9,10},{10,... | collective-permute-start | bytes 417800 | tf_op jit(solution)/shard_map/ppermute | solution.py:293
  42.4 22.8 %collective-permute-start.3 = (f32[2,136,128]{2,1,0:T(8,128)}, f32[2,136,128]{2,1,0:T(8,128)}, u32[]{:S(2)}, u32[]{:S(2)}) collective-permute-start(f32[2,136,128]{2,1,0:T(8,128)} %shard_map.206.refs_7_), channel_id=1, source_target_pairs={{0,4},{1,5},{2,6},{3,7},{4,8},{5,9},{6,10},{7,11},{8,12},{9,13},{1... | collective-permute-start | bytes 417800 | tf_op jit(solution)/shard_map/ppermute | solution.py:324
  47.0 18.2 %collective-permute-start.4 = (f32[2,136,128]{2,1,0:T(8,128)}, f32[2,136,128]{2,1,0:T(8,128)}, u32[]{:S(2)}, u32[]{:S(2)}) collective-permute-start(f32[2,136,128]{2,1,0:T(8,128)} %shard_map.206.refs_7_), channel_id=1, source_target_pairs={{0,8},{1,9},{2,10},{3,11},{4,12},{5,13},{6,14},{7,15},{16,24},{17,... | collective-permute-start | bytes 417800 | tf_op jit(solution)/shard_map/ppermute | solution.py:324
  51.6 13.7 %collective-permute-start.5 = (f32[2,136,128]{2,1,0:T(8,128)}, f32[2,136,128]{2,1,0:T(8,128)}, u32[]{:S(2)}, u32[]{:S(2)}) collective-permute-start(f32[2,136,128]{2,1,0:T(8,128)} %shard_map.206.refs_7_), channel_id=1, source_target_pairs={{0,12},{1,13},{2,14},{3,15},{16,28},{17,29},{18,30},{19,31}} | collective-permute-start | bytes 417800 | tf_op jit(solution)/shard_map/ppermute | solution.py:324
  67.5 14.5 %collective-permute-start.6 = (f32[2,136,128]{2,1,0:T(8,128)}, f32[2,136,128]{2,1,0:T(8,128)}, u32[]{:S(2)}, u32[]{:S(2)}) collective-permute-start(f32[2,136,128]{2,1,0:T(8,128)} %get-tuple-element.87), channel_id=1, source_target_pairs={{0,1},{1,0},{2,3},{3,2},{4,5},{5,4},{6,7},{7,6},{8,9},{9,8},{10,11... | collective-permute-start | bytes 417800 | tf_op jit(solution)/shard_map/ppermute | solution.py:293
  69.0 13.1 %collective-permute-start.7 = (f32[2,136,128]{2,1,0:T(8,128)}, f32[2,136,128]{2,1,0:T(8,128)}, u32[]{:S(2)}, u32[]{:S(2)}) collective-permute-start(f32[2,136,128]{2,1,0:T(8,128)} %get-tuple-element.88), channel_id=1, source_target_pairs={{0,2},{1,3},{2,0},{3,1},{4,6},{5,7},{6,4},{7,5},{8,10},{9,11},{10,... | collective-permute-start | bytes 417800 | tf_op jit(solution)/shard_map/ppermute | solution.py:293
  70.5 11.5 %collective-permute-start.8 = (f32[2,136,128]{2,1,0:T(8,128)}, f32[2,136,128]{2,1,0:T(8,128)}, u32[]{:S(2)}, u32[]{:S(2)}) collective-permute-start(f32[2,136,128]{2,1,0:T(8,128)} %get-tuple-element.89), channel_id=1, source_target_pairs={{0,3},{1,2},{2,1},{3,0},{4,7},{5,6},{6,5},{7,4},{8,11},{9,10},{10,... | collective-permute-start | bytes 417800 | tf_op jit(solution)/shard_map/ppermute | solution.py:293
  129.1 24.5 %collective-permute-start.10 = (f32[1408,1024]{1,0:T(8,128)}, f32[1408,1024]{1,0:T(8,128)}, u32[]{:S(2)}, u32[]{:S(2)}) collective-permute-start(f32[1408,1024]{1,0:T(8,128)} %get-tuple-element.97.refs_4_), channel_id=1, source_target_pairs={{0,16},{16,0},{1,17},{17,1},{2,18},{18,2},{3,19},{19,3},{4,20},{20... | collective-permute-start | bytes 17301512 | tf_op jit(solution)/shard_map/ppermute | solution.py:149
  141.2 17.9 %collective-permute-start.9 = (f32[512,2816]{1,0:T(8,128)}, f32[512,2816]{1,0:T(8,128)}, u32[]{:S(2)}, u32[]{:S(2)}) collective-permute-start(f32[512,2816]{1,0:T(8,128)} %get-tuple-element.99.refs_4_), channel_id=1, source_target_pairs={{0,16},{16,0},{1,17},{17,1},{2,18},{18,2},{3,19},{19,3},{4,20},{20... | collective-permute-start | bytes 17301512 | tf_op jit(solution)/shard_map/ppermute | solution.py:149
  153.6 11.0 %collective-permute-start.12 = (f32[512,2816]{1,0:T(8,128)}, f32[512,2816]{1,0:T(8,128)}, u32[]{:S(2)}, u32[]{:S(2)}) collective-permute-start(f32[512,2816]{1,0:T(8,128)} %get-tuple-element.102.refs_9_), channel_id=1, source_target_pairs={{0,16},{16,0},{1,17},{17,1},{2,18},{18,2},{3,19},{19,3},{4,20},{20... | collective-permute-start | bytes 17301512 | tf_op jit(solution)/shard_map/ppermute | solution.py:149
  157.7 103.2 %collective-permute-start.18 = (f32[8,88,1024]{2,1,0:T(8,128)}, f32[8,88,1024]{2,1,0:T(8,128)}, u32[]{:S(2)}, u32[]{:S(2)}) collective-permute-start(f32[8,88,1024]{2,1,0:T(8,128)} %shard_map.216.refs_9_), channel_id=1, source_target_pairs={{0,1},{1,0},{2,3},{3,2},{4,5},{5,4},{6,7},{7,6},{8,9},{9,8},{10,11... | collective-permute-start | bytes 8650760 | tf_op jit(solution)/shard_map/ppermute | solution.py:137
  163.1 117.3 %collective-permute-start.11 = (f32[8,32,2816]{2,1,0:T(8,128)}, f32[8,32,2816]{2,1,0:T(8,128)}, u32[]{:S(2)}, u32[]{:S(2)}) collective-permute-start(f32[8,32,2816]{2,1,0:T(8,128)} %shard_map.217.refs_9_), channel_id=1, source_target_pairs={{0,2},{1,3},{2,0},{3,1},{4,6},{5,7},{6,4},{7,5},{8,10},{9,11},{10,... | collective-permute-start | bytes 8650760 | tf_op jit(solution)/shard_map/ppermute | solution.py:137
  168.7 108.5 %collective-permute-start.13 = (f32[8,32,2816]{2,1,0:T(8,128)}, f32[8,32,2816]{2,1,0:T(8,128)}, u32[]{:S(2)}, u32[]{:S(2)}) collective-permute-start(f32[8,32,2816]{2,1,0:T(8,128)} %shard_map.218.refs_15_), channel_id=1, source_target_pairs={{0,4},{1,5},{2,6},{3,7},{4,0},{5,1},{6,2},{7,3},{8,12},{9,13},{10,... | collective-permute-start | bytes 8650760 | tf_op jit(solution)/shard_map/ppermute | solution.py:137
  202.5 31.9 %collective-permute-start.14 = (f32[2,528,128]{2,1,0:T(8,128)}, f32[2,528,128]{2,1,0:T(8,128)}, u32[]{:S(2)}, u32[]{:S(2)}) collective-permute-start(f32[2,528,128]{2,1,0:T(8,128)} %get-tuple-element.104.refs_1_), channel_id=1, source_target_pairs={{0,1},{1,0},{2,3},{3,2},{4,5},{5,4},{6,7},{7,6},{8,9},{9,8},{10,11... | collective-permute-start | bytes 1622024 | tf_op jit(solution)/shard_map/ppermute | solution.py:389
  213.2 25.1 %collective-permute-start.16 = (f32[512,2048]{1,0:T(8,128)}, f32[512,2048]{1,0:T(8,128)}, u32[]{:S(2)}, u32[]{:S(2)}) collective-permute-start(f32[512,2048]{1,0:T(8,128)} %get-tuple-element.109.refs_8_), channel_id=1, source_target_pairs={{0,16},{16,0},{1,17},{17,1},{2,18},{18,2},{3,19},{19,3},{4,20},{20... | collective-permute-start | bytes 12582920 | tf_op jit(solution)/shard_map/ppermute | solution.py:149
  236.7 21.6 %collective-permute-start.15 = (f32[2,528,128]{2,1,0:T(8,128)}, f32[2,528,128]{2,1,0:T(8,128)}, u32[]{:S(2)}, u32[]{:S(2)}) collective-permute-start(f32[2,528,128]{2,1,0:T(8,128)} %get-tuple-element.111.refs_1_), channel_id=1, source_target_pairs={{0,2},{1,3},{2,0},{3,1},{4,6},{5,7},{6,4},{7,5},{8,10},{9,11},{10,... | collective-permute-start | bytes 1622024 | tf_op jit(solution)/shard_map/ppermute | solution.py:389
  260.8 13.9 %collective-permute-start.17 = (f32[2,528,128]{2,1,0:T(8,128)}, f32[2,528,128]{2,1,0:T(8,128)}, u32[]{:S(2)}, u32[]{:S(2)}) collective-permute-start(f32[2,528,128]{2,1,0:T(8,128)} %get-tuple-element.115.refs_1_), channel_id=1, source_target_pairs={{0,4},{1,5},{2,6},{3,7},{4,0},{5,1},{6,2},{7,3},{8,12},{9,13},{10,... | collective-permute-start | bytes 1622024 | tf_op jit(solution)/shard_map/ppermute | solution.py:389
  270.3 93.0 %collective-permute-start.24 = (f32[4,88,1024]{2,1,0:T(8,128)}, f32[4,88,1024]{2,1,0:T(8,128)}, u32[]{:S(2)}, u32[]{:S(2)}) collective-permute-start(f32[4,88,1024]{2,1,0:T(8,128)} %shard_map.226.refs_5_), channel_id=1, source_target_pairs={{0,2},{1,3},{2,0},{3,1},{4,6},{5,7},{6,4},{7,5},{8,10},{9,11},{10,... | collective-permute-start | bytes 4325384 | tf_op jit(solution)/shard_map/ppermute | solution.py:137
  270.8 96.3 %collective-permute-start.23 = (f32[8,32,2048]{2,1,0:T(8,128)}, f32[8,32,2048]{2,1,0:T(8,128)}, u32[]{:S(2)}, u32[]{:S(2)}) collective-permute-start(f32[8,32,2048]{2,1,0:T(8,128)} %shard_map.223.refs_8_), channel_id=1, source_target_pairs={{0,1},{1,0},{2,3},{3,2},{4,5},{5,4},{6,7},{7,6},{8,9},{9,8},{10,11... | collective-permute-start | bytes 6291464 | tf_op jit(solution)/shard_map/ppermute | solution.py:137
  274.7 75.9 %collective-permute-start.20 = (f32[512,1024]{1,0:T(8,128)}, f32[512,1024]{1,0:T(8,128)}, u32[]{:S(2)}, u32[]{:S(2)}) collective-permute-start(f32[512,1024]{1,0:T(8,128)} %get-tuple-element.117.refs_4_), channel_id=1, source_target_pairs={{0,16},{16,0},{1,17},{17,1},{2,18},{18,2},{3,19},{19,3},{4,20},{20... | collective-permute-start | bytes 6291464 | tf_op jit(solution)/shard_map/ppermute | solution.py:149
  277.2 58.1 %collective-permute-start.19 = (f32[2,528,128]{2,1,0:T(8,128)}, f32[2,528,128]{2,1,0:T(8,128)}, u32[]{:S(2)}, u32[]{:S(2)}) collective-permute-start(f32[2,528,128]{2,1,0:T(8,128)} %get-tuple-element.119.refs_1_), channel_id=1, source_target_pairs={{0,8},{1,9},{2,10},{3,11},{4,12},{5,13},{6,14},{7,15},{8,0},{9,1},... | collective-permute-start | bytes 1622024 | tf_op jit(solution)/shard_map/ppermute | solution.py:389
  280.4 113.3 %collective-permute-start.28 = (f32[4,32,2816]{2,1,0:T(8,128)}, f32[4,32,2816]{2,1,0:T(8,128)}, u32[]{:S(2)}, u32[]{:S(2)}) collective-permute-start(f32[4,32,2816]{2,1,0:T(8,128)} %shard_map.229.refs_7_), channel_id=1, source_target_pairs={{0,8},{1,9},{2,10},{3,11},{4,12},{5,13},{6,14},{7,15},{8,0},{9,1},... | collective-permute-start | bytes 4325384 | tf_op jit(solution)/shard_map/ppermute | solution.py:137
  338.8 9.0 %collective-permute-start.44 = (f32[8,128]{1,0:T(8,128)}, f32[8,128]{1,0:T(8,128)}, u32[]{:S(2)}, u32[]{:S(2)}) collective-permute-start(f32[8,128]{1,0:T(8,128)} %slice_bitcast_fusion), channel_id=1, source_target_pairs={{0,16},{16,0},{1,17},{17,1},{2,18},{18,2},{3,19},{19,3},{4,20},{20... | collective-permute-start | bytes 12296 | tf_op jit(solution)/shard_map/ppermute | solution.py:149
  347.8 49.5 %collective-permute-start.27 = (f32[4,32,2816]{2,1,0:T(8,128)}, f32[4,32,2816]{2,1,0:T(8,128)}, u32[]{:S(2)}, u32[]{:S(2)}) collective-permute-start(f32[4,32,2816]{2,1,0:T(8,128)} %shard_map.230.refs_3_), channel_id=1, source_target_pairs={{0,1},{1,0},{2,3},{3,2},{4,5},{5,4},{6,7},{7,6},{8,9},{9,8},{10,11... | collective-permute-start | bytes 4325384 | tf_op jit(solution)/shard_map/ppermute | solution.py:137
  353.2 51.1 %collective-permute-start.25 = (f32[8,32,1024]{2,1,0:T(8,128)}, f32[8,32,1024]{2,1,0:T(8,128)}, u32[]{:S(2)}, u32[]{:S(2)}) collective-permute-start(f32[8,32,1024]{2,1,0:T(8,128)} %shard_map.234.refs_5_), channel_id=1, source_target_pairs={{0,2},{1,3},{2,0},{3,1},{4,6},{5,7},{6,4},{7,5},{8,10},{9,11},{10,... | collective-permute-start | bytes 3145736 | tf_op jit(solution)/shard_map/ppermute | solution.py:137
  363.3 7.1 %collective-permute-start.22 = (f32[512,1024]{1,0:T(8,128)}, f32[512,1024]{1,0:T(8,128)}, u32[]{:S(2)}, u32[]{:S(2)}) collective-permute-start(f32[512,1024]{1,0:T(8,128)} %get-tuple-element.130.refs_9_), channel_id=1, source_target_pairs={{0,16},{16,0},{1,17},{17,1},{2,18},{18,2},{3,19},{19,3},{4,20},{20... | collective-permute-start | bytes 6291464 | tf_op jit(solution)/shard_map/ppermute | solution.py:149
  367.0 111.1 %reduce-scatter.3.cloned.1.call-start = ((), (), s32[]{:S(2)}) async-start(), calls=%async_computation.2 | async-start | bytes 1802240 | tf_op jit(solution)/shard_map/reduce_scatter | solution.py:253
  367.1 7.4 %collective-permute-start.21 = (f32[512,1024]{1,0:T(8,128)}, f32[512,1024]{1,0:T(8,128)}, u32[]{:S(2)}, u32[]{:S(2)}) collective-permute-start(f32[512,1024]{1,0:T(8,128)} %get-tuple-element.128), channel_id=1, source_target_pairs={{0,16},{16,0},{1,17},{17,1},{2,18},{18,2},{3,19},{19,3},{4,20},{20... | collective-permute-start | bytes 6291464 | tf_op jit(solution)/shard_map/ppermute | solution.py:149
  370.4 31.7 %collective-permute-start.26 = (f32[4,32,2048]{2,1,0:T(8,128)}, f32[4,32,2048]{2,1,0:T(8,128)}, u32[]{:S(2)}, u32[]{:S(2)}) collective-permute-start(f32[4,32,2048]{2,1,0:T(8,128)} %shard_map.237.refs_9_), channel_id=1, source_target_pairs={{0,2},{1,3},{2,0},{3,1},{4,6},{5,7},{6,4},{7,5},{8,10},{9,11},{10,... | collective-permute-start | bytes 3145736 | tf_op jit(solution)/shard_map/ppermute | solution.py:137
  374.5 33.1 %collective-permute-start.33 = (f32[8,32,1024]{2,1,0:T(8,128)}, f32[8,32,1024]{2,1,0:T(8,128)}, u32[]{:S(2)}, u32[]{:S(2)}) collective-permute-start(f32[8,32,1024]{2,1,0:T(8,128)} %shard_map.238.refs_9_), channel_id=1, source_target_pairs={{0,1},{1,0},{2,3},{3,2},{4,5},{5,4},{6,7},{7,6},{8,9},{9,8},{10,11... | collective-permute-start | bytes 3145736 | tf_op jit(solution)/shard_map/ppermute | solution.py:137
  393.8 30.7 %collective-permute-start.32 = (f32[8,32,1024]{2,1,0:T(8,128)}, f32[8,32,1024]{2,1,0:T(8,128)}, u32[]{:S(2)}, u32[]{:S(2)}) collective-permute-start(f32[8,32,1024]{2,1,0:T(8,128)} %shard_map.239.refs_11_), channel_id=1, source_target_pairs={{0,2},{1,3},{2,0},{3,1},{4,6},{5,7},{6,4},{7,5},{8,10},{9,11},{10,... | collective-permute-start | bytes 3145736 | tf_op jit(solution)/shard_map/ppermute | solution.py:137
  397.3 29.9 %collective-permute-start.31 = (f32[2,32,2816]{2,1,0:T(8,128)}, f32[2,32,2816]{2,1,0:T(8,128)}, u32[]{:S(2)}, u32[]{:S(2)}) collective-permute-start(f32[2,32,2816]{2,1,0:T(8,128)} %shard_map.241.refs_9_), channel_id=1, source_target_pairs={{0,1},{1,0},{2,3},{3,2},{4,5},{5,4},{6,7},{7,6},{8,9},{9,8},{10,11... | collective-permute-start | bytes 2162696 | tf_op jit(solution)/shard_map/ppermute | solution.py:137
  404.3 25.9 %collective-permute-start.30 = (f32[2,32,2048]{2,1,0:T(8,128)}, f32[2,32,2048]{2,1,0:T(8,128)}, u32[]{:S(2)}, u32[]{:S(2)}) collective-permute-start(f32[2,32,2048]{2,1,0:T(8,128)} %shard_map.243.refs_7_), channel_id=1, source_target_pairs={{0,4},{1,5},{2,6},{3,7},{4,0},{5,1},{6,2},{7,3},{8,12},{9,13},{10,... | collective-permute-start | bytes 1572872 | tf_op jit(solution)/shard_map/ppermute | solution.py:137
  406.6 25.7 %collective-permute-start.29 = (f32[4,32,1024]{2,1,0:T(8,128)}, f32[4,32,1024]{2,1,0:T(8,128)}, u32[]{:S(2)}, u32[]{:S(2)}) collective-permute-start(f32[4,32,1024]{2,1,0:T(8,128)} %shard_map.244.refs_7_), channel_id=1, source_target_pairs={{0,1},{1,0},{2,3},{3,2},{4,5},{5,4},{6,7},{7,6},{8,9},{9,8},{10,11... | collective-permute-start | bytes 1572872 | tf_op jit(solution)/shard_map/ppermute | solution.py:137
  409.8 25.9 %collective-permute-start.38 = (f32[4,32,1024]{2,1,0:T(8,128)}, f32[4,32,1024]{2,1,0:T(8,128)}, u32[]{:S(2)}, u32[]{:S(2)}) collective-permute-start(f32[4,32,1024]{2,1,0:T(8,128)} %shard_map.245.refs_7_), channel_id=1, source_target_pairs={{0,2},{1,3},{2,0},{3,1},{4,6},{5,7},{6,4},{7,5},{8,10},{9,11},{10,... | collective-permute-start | bytes 1572872 | tf_op jit(solution)/shard_map/ppermute | solution.py:137
  426.7 15.9 %collective-permute-start.37 = (f32[4,32,1024]{2,1,0:T(8,128)}, f32[4,32,1024]{2,1,0:T(8,128)}, u32[]{:S(2)}, u32[]{:S(2)}) collective-permute-start(f32[4,32,1024]{2,1,0:T(8,128)} %shard_map.246.refs_6_), channel_id=1, source_target_pairs={{0,1},{1,0},{2,3},{3,2},{4,5},{5,4},{6,7},{7,6},{8,9},{9,8},{10,11... | collective-permute-start | bytes 1572872 | tf_op jit(solution)/shard_map/ppermute | solution.py:137
  429.4 15.0 %collective-permute-start.36 = (f32[1,32,2816]{2,1,0:T(8,128)}, f32[1,32,2816]{2,1,0:T(8,128)}, u32[]{:S(2)}, u32[]{:S(2)}) collective-permute-start(f32[1,32,2816]{2,1,0:T(8,128)} %shard_map.247.refs_6_), channel_id=1, source_target_pairs={{0,2},{1,3},{2,0},{3,1},{4,6},{5,7},{6,4},{7,5},{8,10},{9,11},{10,... | collective-permute-start | bytes 1081352 | tf_op jit(solution)/shard_map/ppermute | solution.py:137
  432.3 18.1 %collective-permute-start.35 = (f32[1,32,2048]{2,1,0:T(8,128)}, f32[1,32,2048]{2,1,0:T(8,128)}, u32[]{:S(2)}, u32[]{:S(2)}) collective-permute-start(f32[1,32,2048]{2,1,0:T(8,128)} %shard_map.248.refs_5_), channel_id=1, source_target_pairs={{0,8},{1,9},{2,10},{3,11},{4,12},{5,13},{6,14},{7,15},{8,0},{9,1},... | collective-permute-start | bytes 786440 | tf_op jit(solution)/shard_map/ppermute | solution.py:137
  434.4 18.2 %collective-permute-start.34 = (f32[2,32,1024]{2,1,0:T(8,128)}, f32[2,32,1024]{2,1,0:T(8,128)}, u32[]{:S(2)}, u32[]{:S(2)}) collective-permute-start(f32[2,32,1024]{2,1,0:T(8,128)} %shard_map.249.refs_5_), channel_id=1, source_target_pairs={{0,4},{1,5},{2,6},{3,7},{4,0},{5,1},{6,2},{7,3},{8,12},{9,13},{10,... | collective-permute-start | bytes 786440 | tf_op jit(solution)/shard_map/ppermute | solution.py:137
  437.7 20.3 %collective-permute-start.41 = (f32[2,32,1024]{2,1,0:T(8,128)}, f32[2,32,1024]{2,1,0:T(8,128)}, u32[]{:S(2)}, u32[]{:S(2)}) collective-permute-start(f32[2,32,1024]{2,1,0:T(8,128)} %shard_map.250.refs_5_), channel_id=1, source_target_pairs={{0,4},{1,5},{2,6},{3,7},{4,0},{5,1},{6,2},{7,3},{8,12},{9,13},{10,... | collective-permute-start | bytes 786440 | tf_op jit(solution)/shard_map/ppermute | solution.py:137
  444.5 21.9 %collective-permute-start.40 = (f32[2,32,1024]{2,1,0:T(8,128)}, f32[2,32,1024]{2,1,0:T(8,128)}, u32[]{:S(2)}, u32[]{:S(2)}) collective-permute-start(f32[2,32,1024]{2,1,0:T(8,128)} %shard_map.251.refs_7_), channel_id=1, source_target_pairs={{0,4},{1,5},{2,6},{3,7},{4,0},{5,1},{6,2},{7,3},{8,12},{9,13},{10,... | collective-permute-start | bytes 786440 | tf_op jit(solution)/shard_map/ppermute | solution.py:137
  454.4 13.8 %collective-permute-start.39 = (f32[1,32,1024]{2,1,0:T(8,128)}, f32[1,32,1024]{2,1,0:T(8,128)}, u32[]{:S(2)}, u32[]{:S(2)}) collective-permute-start(f32[1,32,1024]{2,1,0:T(8,128)} %shard_map.254.refs_6_), channel_id=1, source_target_pairs={{0,8},{1,9},{2,10},{3,11},{4,12},{5,13},{6,14},{7,15},{8,0},{9,1},... | collective-permute-start | bytes 393224 | tf_op jit(solution)/shard_map/ppermute | solution.py:137
  459.8 10.9 %collective-permute-start.42 = (f32[1,32,1024]{2,1,0:T(8,128)}, f32[1,32,1024]{2,1,0:T(8,128)}, u32[]{:S(2)}, u32[]{:S(2)}) collective-permute-start(f32[1,32,1024]{2,1,0:T(8,128)} %shard_map.255.refs_6_), channel_id=1, source_target_pairs={{0,8},{1,9},{2,10},{3,11},{4,12},{5,13},{6,14},{7,15},{8,0},{9,1},... | collective-permute-start | bytes 393224 | tf_op jit(solution)/shard_map/ppermute | solution.py:137
  468.2 8.1 %collective-permute-start.43 = (f32[1,32,1024]{2,1,0:T(8,128)}, f32[1,32,1024]{2,1,0:T(8,128)}, u32[]{:S(2)}, u32[]{:S(2)}) collective-permute-start(f32[1,32,1024]{2,1,0:T(8,128)} %shard_map.256.refs_7_), channel_id=1, source_target_pairs={{0,8},{1,9},{2,10},{3,11},{4,12},{5,13},{6,14},{7,15},{8,0},{9,1},... | collective-permute-start | bytes 393224 | tf_op jit(solution)/shard_map/ppermute | solution.py:137
  (1 other events, 6.4 us)
Sparse Core Ops, SparseCore 0:
  367.2 30.6 reduce-scatter.4
  407.7 38.8 reduce-scatter.2
